TPU v7x, 32 devices: a whole 2x2x4 slice. The times are simulated.
32 devices in a mesh: dap: 4 (over x, core), dp: 8 (over z, y).
Axes of the slice: x: 2, y: 2, z: 4, core: 2. Of those that a mesh axis runs over, the one named last changes fastest.
Arguments:
- pair_rep: bfloat16 [8, 128, 128, 128], P('dp', 'dap'), may hold values from -6 to 6
- cotangent: bfloat16 [8, 128, 128, 128], P('dp', 'dap'), may hold values from -6 to 6
- tok_mask: int32 [8, 128], P('dp'), may hold values from 0 to 1, as said below
- tok_types: int32 [8, 128], P('dp'), may hold values from 0 to 3
- pair_mask: int32 [8, 128, 128], P('dp', 'dap'), may hold values 0 or 1
- triangle_gain: float32 [128], replicated, may hold values from 0.5 to 1.5
- triangle_input: bfloat16 [128, 512], replicated, may hold values from -0.5 to 0.5
- triangle_gating: bfloat16 [128, 128], replicated, may hold values from -0.5 to 0.5
- product_gain: float32 [128], replicated, may hold values from 0.5 to 1.5
- triangle_output: bfloat16 [128, 128], replicated, may hold values from -0.5 to 0.5
- attend_gain: float32 [128], replicated, may hold values from 0.5 to 1.5
- attend_bias: bfloat16 [128, 4], replicated, may hold values from -0.5 to 0.5
- attend_input: bfloat16 [128, 512], replicated, may hold values from -0.5 to 0.5
- attend_output: bfloat16 [128, 128], replicated, may hold values from -0.5 to 0.5
- type_table: float32 [4, 4, 4], replicated, may hold values from -4 to 4
Outputs:
- pair_out: bfloat16 [8, 128, 128, 128], P('dp', 'dap')
- pair_grad: bfloat16 [8, 128, 128, 128], P('dp', 'dap')
- grad_triangle_gain: float32 [128], replicated
- grad_triangle_input: float32 [128, 512], replicated
- grad_triangle_gating: float32 [128, 128], replicated
- grad_product_gain: float32 [128], replicated
- grad_triangle_output: float32 [128, 128], replicated
- grad_attend_gain: float32 [128], replicated
- grad_attend_bias: float32 [128, 4], replicated
- grad_attend_input: float32 [128, 512], replicated
- grad_attend_output: float32 [128, 128], replicated
- grad_type_table: float32 [4, 4, 4], replicated
Inputs may be any that keep to these rules, and one draw needn't show every extreme that they name: `tok_mask`: each crop's real tokens form a leading run of at least 64 tokens.
All inputs are finite; a program needn't handle non-finite values. No bound on the sum of `pair_mask` on one device may be relied on, other than what follows from the above.
Results may differ from a plain program's by a relative error of at most 0.035.
Values may be sent and summed in bfloat16 or wider, within the bound.
No kernel may reach another device: no remote copies, remote signals or barrier semaphores. Data moves between devices by JAX's collectives and lax.ppermute only.
A program may use at most 128 MiB of HBM per device.

v0:
```python
from functools import partial

import jax
import jax.numpy as jnp
from jax import lax
from jax.experimental import pallas as pl
from jax.experimental.pallas import tpu as pltpu
from jax.sharding import PartitionSpec as P

EPSILON = 1e-05
F32 = jnp.float32
BF16 = jnp.bfloat16
VMEM_LIMIT = 16 * 1024 * 1024
HEAD_ROWS = 16


def mm(left, right):
    return lax.dot_general(left, right, (((1,), (0,)), ((), ())), preferred_element_type=F32)


def mmt(left, right):
    return lax.dot_general(left, right, (((1,), (1,)), ((), ())), preferred_element_type=F32)


def sigmoid(value):
    return 1.0 / (1.0 + jnp.exp(-value))


def identity(size):
    rows = lax.broadcasted_iota(jnp.int32, (size, size), 0)
    columns = lax.broadcasted_iota(jnp.int32, (size, size), 1)
    return (rows == columns).astype(F32).astype(BF16)


def norm_parts(values, axis):
    centred = values - jnp.mean(values, axis=axis, keepdims=True)
    spread = jnp.mean(centred * centred, axis=axis, keepdims=True)
    scale = lax.rsqrt(spread + EPSILON)
    return centred * scale, scale


def norm_back(d_hat, hat, scale, axis):
    first = jnp.mean(d_hat, axis=axis, keepdims=True)
    second = jnp.mean(d_hat * hat, axis=axis, keepdims=True)
    return scale * (d_hat - first - hat * second)


def lockstep(row, indices):
    going = [row(index) for index in indices]
    results = [None] * len(going)
    running = True
    while running:
        for at, one in enumerate(going):
            try:
                next(one)
            except StopIteration as stop:
                results[at] = stop.value
                running = False
    return results


def over_rows(count, width, row, finish=None):
    def some(index, carry):
        results = lockstep(row, [index * width + at for at in range(width)])
        if finish is not None:
            finish(results)
        return carry

    lax.fori_loop(0, count // width, some, 0)


def call(kernel, outs, args, scratch=(), grid=(), in_specs=None, out_specs=None, us=5.0, name=None):
    whole = pl.BlockSpec(memory_space=pltpu.VMEM)
    return pl.pallas_call(
        kernel,
        out_shape=[jax.ShapeDtypeStruct(shape, dtype) for shape, dtype in outs],
        grid=grid,
        in_specs=in_specs or [whole] * len(args),
        out_specs=out_specs or [whole] * len(outs),
        scratch_shapes=list(scratch),
        compiler_params=pltpu.CompilerParams(vmem_limit_bytes=VMEM_LIMIT),
        cost_estimate=pl.CostEstimate(
            flops=int(us * 1.0e9), bytes_accessed=int(us * 3.0e6), transcendentals=0
        ),
        name=name,
    )(*args)


def right_kernel(pair, live, gain, weight, normed_out, right_out, weight_t, lay):
    rows, length, channels = pair.shape
    weight_t[...] = weight[:, 2 * channels : 4 * channels].astype(F32).T.astype(BF16)

    def row(i):
        hat, _ = norm_parts(pair[i].astype(F32), -1)
        yield
        normed = (hat * gain[...]).astype(BF16)
        normed_out[i] = normed
        projected = mmt(weight_t[...], normed)
        yield
        right = sigmoid(projected[channels:]) * projected[:channels] * live[pl.ds(i, 1), :]
        lay[pl.ds(i, channels, stride=rows), :] = right

    over_rows(rows, 4, row)
    right_out[...] = lay[...].reshape(channels, rows, length).astype(BF16)


def left_kernel(parts, *refs):
    normed_parts = refs[:parts]
    live, weight, gating = refs[parts : parts + 3]
    normed_out, left_out, gate_out, weight_t, lay = refs[parts + 3 :]
    rows, length, channels = normed_out.shape
    half = rows // parts
    weight_t[...] = weight[:, : 2 * channels].astype(F32).T.astype(BF16)
    for part in range(parts):

        def row(i, part=part):
            normed = normed_parts[part][i]
            at = i + part * half
            normed_out[at] = normed
            projected = mmt(weight_t[...], normed)
            gate = mm(normed, gating[...])
            yield
            left = sigmoid(projected[channels:]) * projected[:channels] * live[pl.ds(at, 1), :]
            lay[pl.ds(at, channels, stride=rows), :] = left
            gate_out[at] = sigmoid(gate).astype(BF16)

        over_rows(half, 4, row)
    left_out[...] = lay[...].reshape(channels, rows, length).astype(BF16)


def product_kernel(count, place_ref, *refs):
    blocks = refs[: 2 * count]
    (left, pair, gate, gain2_col, gain3, output_w, bias_w) = refs[2 * count : 2 * count + 7]
    (right_all, normed2_out, scale2_out, update_out, middle_out, normed3_out, bias_out) = refs[
        2 * count + 7 : 2 * count + 14
    ]
    product, bias_scr = refs[2 * count + 14 :]
    channels, rows, length = left.shape
    heads = bias_w.shape[1]
    half = rows // 2
    starts = [
        pl.multiple_of((place_ref[0] ^ (index // 2)) * rows + (index % 2) * half, half)
        for index in range(2 * count)
    ]

    def channel(c, carry):
        for start, ref in zip(starts, blocks):
            right_all[c, pl.ds(start, half), :] = ref[c]
        return carry

    lax.fori_loop(0, channels, channel, 0, unroll=4)

    def multiply(c, carry):
        product[pl.ds(c, rows, stride=channels), :] = mmt(left[c], right_all[c])
        return carry

    lax.fori_loop(0, channels, multiply, 0, unroll=8)
    eye = identity(channels)
    gain2 = jnp.broadcast_to(gain2_col[...], (channels, length))
    bias_t = jnp.concatenate(
        [bias_w[...].astype(F32).T, jnp.zeros((HEAD_ROWS - heads, channels), F32)], axis=0
    ).astype(BF16)

    def row(i):
        hat, scale = norm_parts(product[pl.ds(i * channels, channels), :], 0)
        yield
        normed2_t = (hat * gain2).astype(BF16)
        normed2_out[i] = normed2_t
        scale2_out[pl.ds(i, 1), :] = scale
        normed2 = mmt(eye, normed2_t).astype(BF16)
        yield
        update = mm(normed2, output_w[...])
        yield
        update_out[i] = update.astype(BF16)
        middle = (pair[i].astype(F32) + gate[i].astype(F32) * update).astype(BF16)
        middle_out[i] = middle
        hat3, _ = norm_parts(middle.astype(F32), -1)
        yield
        normed3 = (hat3 * gain3[...]).astype(BF16)
        normed3_out[i] = normed3
        bias_scr[pl.ds(i * HEAD_ROWS, HEAD_ROWS), :] = mmt(bias_t, normed3)

    over_rows(rows, 4, row)
    for h in range(heads):
        head = bias_scr[pl.ds(h, rows, stride=HEAD_ROWS), :]
        bias_out[:, h * length : (h + 1) * length] = head.astype(BF16)


def attend_kernel(
    count, block, place_ref, table, *refs
):
    bias_refs = refs[:count]
    (types_row, types_col, live, normed3, middle, cotangent, input_w, output_w) = refs[
        count : count + 8
    ]
    (pair_out, d_projected, d_output, d_table) = refs[count + 8 : count + 12]
    d_bias_outs = refs[count + 12 : 2 * count + 12]
    bias, d_bias, head_mask, weight_t, weight_qg = refs[2 * count + 12 :]
    length, channels = normed3.shape[1:]
    types = table.shape[1]
    heads = table.shape[0] // types
    size = channels // heads
    own = bias_refs[0].shape[0]
    factor = size ** -0.5
    place = place_ref[0]
    step = pl.program_id(0)

    def spans(h):
        return slice(h * length, (h + 1) * length)

    @pl.when(step == 0)
    def _():
        for offset in range(count):
            start = pl.multiple_of((place ^ offset) * own, own)
            bias[pl.ds(start, own), :] = bias_refs[offset][...].astype(F32)
        row_types = types_row[...]
        col_types = types_col[...]
        for h in range(heads):
            total = jnp.zeros((length, length), F32)
            for a in range(types):
                values = jnp.zeros((1, length), F32)
                for b in range(types):
                    values = jnp.where(row_types == b, table[h * types + a, b], values)
                total = jnp.where(col_types == a, values, total)
            bias[:, spans(h)] = bias[:, spans(h)] + total
        d_bias[...] = jnp.zeros_like(d_bias)
        d_output[...] = jnp.zeros_like(d_output)
        rows = lax.broadcasted_iota(jnp.int32, head_mask.shape, 0) // size
        columns = lax.broadcasted_iota(jnp.int32, head_mask.shape, 1) // length
        head_mask[...] = (rows == columns).astype(F32).astype(BF16)
        weight_t[...] = input_w[:, : 3 * channels].astype(F32).T.astype(BF16)
        weight_qg[:, :channels] = input_w[:, :channels]
        weight_qg[:, channels:] = input_w[:, 3 * channels :]

    eye = identity(channels)

    def row(i):
        live_row = live[pl.ds(step * block + i, 1), :]
        live_wide = jnp.concatenate([live_row.astype(BF16)] * heads, axis=1)
        normed = normed3[i]
        projected_t = mmt(weight_t[...], normed)
        projected = mm(normed, weight_qg[...])
        d_gated = mmt(cotangent[i], output_w[...])
        yield
        query_t = (projected_t[:channels] * factor).astype(BF16)
        key_t = projected_t[channels : 2 * channels].astype(BF16)
        value_t = projected_t[2 * channels :].astype(BF16)
        query = (projected[:, :channels] * factor).astype(BF16)
        gate = sigmoid(projected[:, channels:])
        mask = head_mask[...]
        ones = mask * live_wide
        keys = jnp.concatenate([key_t] * heads, axis=1) * mask
        values = jnp.concatenate(
            [jnp.concatenate([value_t] * heads, axis=1) * ones, ones], axis=0
        )
        score = mm(query, keys)
        yield
        expo = jnp.exp(score + bias[...])
        expo_b = expo.astype(BF16)
        sums = mmt(expo_b, values)
        yield
        total = sums[:, channels:]
        inverse = 1.0 / jnp.maximum(total, 1.0)
        attended = sums[:, :channels] * inverse
        gated = (gate * attended).astype(BF16)
        d_attended = d_gated * gate * inverse
        d_gate = d_gated * attended * gate * (1.0 - gate)
        slope = jnp.where(total > 1.0, 1.0, jnp.where(total == 1.0, 0.5, 0.0))
        d_attended_b = d_attended.astype(BF16)
        both = jnp.concatenate(
            [d_attended_b, (-d_attended * attended * slope).astype(BF16)], axis=1
        )
        d_expo = mm(both, values)
        turned = mmt(
            eye, jnp.concatenate([d_attended_b, d_gate.astype(BF16), gated], axis=0)
        ).astype(BF16)
        yield
        update = mm(gated, output_w[...])
        d_score = expo * d_expo
        d_score_b = d_score.astype(BF16)
        d_query_t = mmt(keys, d_score_b) * factor
        d_key_t = mm(query_t, d_score_b)
        d_value_t = mm(turned[:, :length], expo_b)
        yield
        pair_out[i] = (middle[i].astype(F32) + update).astype(BF16)

        def diagonal(full):
            return jnp.concatenate(
                [full[h * size : (h + 1) * size, spans(h)] for h in range(heads)], axis=0
            )

        d_projected[i, :channels] = d_query_t.astype(BF16)
        d_projected[i, channels : 2 * channels] = diagonal(d_key_t).astype(BF16)
        d_projected[i, 2 * channels : 3 * channels] = (diagonal(d_value_t) * live_row).astype(BF16)
        d_projected[i, 3 * channels :] = turned[:, length : 2 * length]
        return turned[:, 2 * length :], cotangent[i], d_score

    def finish(results):
        gated_t, cots, d_scores = zip(*results)
        d_output[...] += mm(jnp.concatenate(gated_t, axis=1), jnp.concatenate(cots, axis=0))
        d_bias[...] += sum(d_scores)

    over_rows(block, 2, row, finish)

    @pl.when(step == pl.num_programs(0) - 1)
    def _():
        for offset in range(count):
            start = pl.multiple_of((place ^ offset) * own, own)
            ref = d_bias_outs[offset]
            ref[...] = d_bias[pl.ds(start, own), :].astype(ref.dtype)
        high = d_bias[...].astype(BF16)
        low = (d_bias[...] - high.astype(F32)).astype(BF16)
        kinds = lax.broadcasted_iota(jnp.int32, (HEAD_ROWS, length), 0)
        picks = (types_row[...] == kinds).astype(F32).astype(BF16)
        by_row = mm(picks, high) + mm(picks, low)
        lanes = lax.broadcasted_iota(jnp.int32, (HEAD_ROWS, channels), 1)
        grad = jnp.zeros((HEAD_ROWS, channels), F32)
        for h in range(heads):
            part = by_row[:, spans(h)]
            for b in range(types):
                one = jnp.sum(jnp.where(types_row[...] == b, part, 0.0), axis=1, keepdims=True)
                grad = jnp.where(lanes == h * types + b, one, grad)
        d_table[...] = grad


def projection_kernel(d_projected, normed3, input_w, d_output, d_table, d_normed, packed, total):
    block = normed3.shape[0]
    wide, length = d_projected.shape[1:]
    channels = normed3.shape[2]
    step = pl.program_id(0)

    @pl.when(step == 0)
    def _():
        total[...] = jnp.zeros_like(total)

    def rows(index, carry):
        at = [4 * index + one for one in range(4)]
        both = jnp.concatenate([d_projected[one] for one in at], axis=1)
        total[...] += mm(both, jnp.concatenate([normed3[one] for one in at], axis=0))
        d_both = mm(input_w[...], both)
        for order, one in enumerate(at):
            d_normed[one] = d_both[:, order * length : (order + 1) * length]
        return carry

    lax.fori_loop(0, block // 4, rows, 0, unroll=2)

    @pl.when(step == pl.num_programs(0) - 1)
    def _():
        packed[:wide] = total[...].astype(BF16)
        packed[wide : wide + channels] = d_output[...].astype(BF16)
        high = d_table[...].astype(BF16)
        packed[wide + channels : wide + channels + HEAD_ROWS] = high
        packed[wide + channels + HEAD_ROWS :] = (d_table[...] - high.astype(F32)).astype(BF16)


def middle_kernel(count, place_ref, *refs):
    arrived = refs[:count]
    (d_normed3, normed3, middle, cotangent, gain3_col, bias_w) = refs[count : count + 6]
    (normed2, scale2, update, gate, gain2_col, output_w) = refs[count + 6 : count + 12]
    (d_middle_out, d_gate_out, d_product_out, grad_out) = refs[count + 12 : count + 16]
    send_outs = refs[count + 16 : 2 * count + 16]
    d_bias, lay = refs[2 * count + 16 :]
    rows, length, channels = middle.shape
    heads = bias_w.shape[1]
    place = place_ref[0]
    eye = identity(channels)
    total = arrived[0][...]
    for ref in arrived[1:]:
        total = total + ref[...].astype(F32)
    d_bias[...] = jnp.zeros_like(d_bias)
    for h in range(heads):
        d_bias[pl.ds(h, rows, stride=HEAD_ROWS), :] = total[:, h * length : (h + 1) * length]
    bias_wide = jnp.concatenate(
        [bias_w[...].astype(F32), jnp.zeros((channels, HEAD_ROWS - heads), F32)], axis=1
    ).astype(BF16)
    gain3 = jnp.broadcast_to(gain3_col[...], (channels, length))
    gain2 = jnp.broadcast_to(gain2_col[...], (channels, length))
    inverse2 = 1.0 / gain2
    grad_out[...] = jnp.zeros_like(grad_out)

    def row(i):
        bias_rows = d_bias[pl.ds(i * HEAD_ROWS, HEAD_ROWS), :].astype(BF16)
        d_normed = d_normed3[i] + mm(bias_wide, bias_rows)
        hat3, scale3 = norm_parts(mmt(eye, middle[i]), 0)
        yield
        d_mid_t = norm_back(d_normed * gain3, hat3, scale3, 0).astype(BF16)
        d_mid_b = mmt(eye, d_mid_t)
        yield
        d_mid = (cotangent[i].astype(F32) + d_mid_b).astype(BF16)
        d_middle_out[i] = d_mid
        gates = gate[i].astype(F32)
        d_mid = d_mid.astype(F32)
        d_up = d_mid * gates
        d_gate_out[i] = (d_up * update[i].astype(F32) * (1.0 - gates)).astype(BF16)
        d_up = d_up.astype(BF16)
        normed2_t = normed2[i]
        d_hat2 = mmt(output_w[...], d_up)
        yield
        hat2 = normed2_t.astype(F32) * inverse2
        lay[pl.ds(i, channels, stride=rows), :] = norm_back(
            d_hat2 * gain2, hat2, scale2[pl.ds(i, 1), :], 0
        )
        return normed2_t, d_up, bias_rows, normed3[i]

    def finish(results):
        normed2_t, d_up, bias_rows, normed = zip(*results)
        grad_out[:channels] += mm(
            jnp.concatenate(normed2_t, axis=1), jnp.concatenate(d_up, axis=0)
        )
        grad_out[channels:] += mm(
            jnp.concatenate(bias_rows, axis=1), jnp.concatenate(normed, axis=0)
        )

    over_rows(rows, 4, row, finish)
    line = lax.broadcasted_iota(jnp.int32, (length, length), 0)
    source = ((line // rows) ^ place) * rows + line % rows
    shuffled = (
        (source == lax.broadcasted_iota(jnp.int32, (length, length), 1)).astype(F32).astype(BF16)
    )

    def group(g, carry):
        block = lay[pl.ds(g * length, length), :].astype(BF16)
        d_product_out[pl.ds(g * length, length), :] = block
        turned = mmt(shuffled, block).astype(BF16)
        for offset in range(count):
            send_outs[offset][g] = turned[offset * rows : (offset + 1) * rows]
        return carry

    lax.fori_loop(0, channels * rows // length, group, 0, unroll=4)


def gate_back(projected, d_out, live_row, channels):
    value, pre = projected[:channels], projected[channels:]
    gate = sigmoid(pre)
    d_value = d_out * live_row * gate
    d_pre = d_value * value * (1.0 - gate)
    return jnp.concatenate([d_value.astype(BF16), d_pre.astype(BF16)], axis=0)


def left_back_kernel(
    right_all, d_product, normed1, live, input_w, d_gate, grad_middle, d_projected_out, packed, lay, grad
):
    rows, length, channels = normed1.shape

    def channel(c, carry):
        lay[pl.ds(c, rows, stride=channels), :] = mm(
            d_product[pl.ds(c * rows, rows), :], right_all[c]
        )
        return carry

    lax.fori_loop(0, channels, channel, 0, unroll=8)
    eye = identity(channels)
    weight_t = input_w[:, : 2 * channels].astype(F32).T.astype(BF16)
    grad[...] = jnp.zeros_like(grad)

    def row(i):
        normed = normed1[i]
        projected = mmt(weight_t, normed)
        d_gate_t = mmt(eye, d_gate[i]).astype(BF16)
        yield
        d_projected = gate_back(
            projected, lay[pl.ds(i * channels, channels), :], live[pl.ds(i, 1), :], channels
        )
        d_projected = jnp.concatenate([d_projected, d_gate_t], axis=0)
        d_projected_out[i] = d_projected
        return d_projected, normed

    def finish(results):
        d_projected, normed = zip(*results)
        grad[...] += mm(jnp.concatenate(d_projected, axis=1), jnp.concatenate(normed, axis=0))

    over_rows(rows, 4, row, finish)
    packed[: 3 * channels] = grad[...].astype(BF16)
    packed[3 * channels :] = grad_middle[...].astype(BF16)


def right_back_kernel(count, place_ref, *refs):
    arrived = refs[:count]
    left_blocks = refs[count : 2 * count]
    normed1, live, input_w, packed_a, packed_b = refs[2 * count : 2 * count + 5]
    d_projected_out = refs[2 * count + 5]
    sends = refs[2 * count + 6 : 3 * count + 6]
    lay, grad, packed = refs[3 * count + 6 :]
    rows, length, channels = normed1.shape
    per = length // rows
    same = (
        lax.broadcasted_iota(jnp.int32, (length, length), 0) // rows
        == lax.broadcasted_iota(jnp.int32, (length, length), 1) // rows
    )
    mask = same.astype(F32).astype(BF16)

    def group(g, carry):
        spread = jnp.concatenate(
            [jnp.concatenate([ref[g]] * per, axis=0) * mask for ref in arrived], axis=1
        )
        lefts = jnp.concatenate(
            [ref[pl.ds(g * per, per)].reshape(length, length) for ref in left_blocks], axis=0
        )
        lay[pl.ds(g * length, length), :] = mm(spread, lefts)
        return carry

    lax.fori_loop(0, channels // per, group, 0, unroll=4)
    weight_t = input_w[:, 2 * channels : 4 * channels].astype(F32).T.astype(BF16)
    grad[...] = jnp.zeros_like(grad)

    def row(i):
        normed = normed1[i]
        projected = mmt(weight_t, normed)
        yield
        d_projected = gate_back(
            projected,
            lay[pl.ds(i, channels, stride=rows), :],
            live[pl.ds(i, 1), :],
            channels,
        )
        d_projected_out[i] = d_projected
        return d_projected, normed

    def finish(results):
        d_projected, normed = zip(*results)
        grad[...] += mm(jnp.concatenate(d_projected, axis=1), jnp.concatenate(normed, axis=0))

    over_rows(rows, 4, row, finish)
    first, second = packed_a.shape[0], packed_b.shape[0]
    packed[:first] = packed_a[...]
    packed[first : first + second] = packed_b[...]
    packed[first + second : first + second + 2 * channels] = grad[...].astype(BF16)
    packed[first + second + 2 * channels :] = jnp.zeros_like(
        packed[first + second + 2 * channels :]
    )
    size = sends[0].shape[0]
    for offset in range(count):
        start = pl.multiple_of((place_ref[0] ^ offset) * size, HEAD_ROWS)
        sends[offset][...] = packed[pl.ds(start, size), :]


def input_back_kernel(d_left, d_right, pair, d_middle, gain_col, input_w, gating, pair_grad):
    rows, length, channels = pair.shape
    eye = identity(channels)
    weight = jnp.concatenate(
        [input_w[:, : 2 * channels], gating[...], input_w[:, 2 * channels :]], axis=1
    )
    gain = jnp.broadcast_to(gain_col[...], (channels, length))

    def row(i):
        hat, scale = norm_parts(mmt(eye, pair[i]), 0)
        d_normed = mm(weight, jnp.concatenate([d_left[i], d_right[i]], axis=0))
        yield
        d_pair = mmt(eye, norm_back(d_normed * gain, hat, scale, 0).astype(BF16))
        yield
        pair_grad[i] = (d_middle[i].astype(F32) + d_pair).astype(BF16)

    over_rows(rows, 4, row)


def finish_kernel(count, factor, place_ref, *refs):
    blocks = refs[:count]
    (input1, gating, output1, bias_w, input3, gain1, gain2, gain3) = refs[count : count + 8]
    (
        gain1_out,
        input1_out,
        gating_out,
        gain2_out,
        output1_out,
        gain3_out,
        bias_out,
        input3_out,
        output3_out,
        table_out,
        packed,
    ) = refs[count + 8 :]
    channels = gating.shape[0]
    heads, types = table_out.shape[:2]
    size = blocks[0].shape[0]
    for offset in range(count):
        start = pl.multiple_of((place_ref[0] ^ offset) * size, HEAD_ROWS)
        packed[pl.ds(start, size), :] = blocks[offset][...].astype(F32) * factor
    at = 0

    def take(rows):
        nonlocal at
        at += rows
        return packed[at - rows : at, :]

    input3_t, output3 = take(4 * channels), take(channels)
    table = take(HEAD_ROWS) + take(HEAD_ROWS)
    left_t, gating_t, output1_grad = take(2 * channels), take(channels), take(channels)
    bias_t, right_t = take(HEAD_ROWS), take(2 * channels)
    input1_t = jnp.concatenate([left_t, right_t], axis=0)

    def dots(weight, grad_t):
        return jnp.sum(weight[...].astype(F32).T * grad_t, axis=0, keepdims=True)

    gain1_out[...] = (dots(input1, input1_t) + dots(gating, gating_t)) / gain1[...]
    output_t = (output1[...].astype(F32) * output1_grad).T
    gain2_out[...] = jnp.sum(output_t, axis=0, keepdims=True) / gain2[...]
    gain3_out[...] = (dots(input3, input3_t) + dots(bias_w, bias_t[:heads])) / gain3[...]
    input1_out[...] = input1_t.T
    gating_out[...] = gating_t.T
    output1_out[...] = output1_grad
    bias_out[...] = bias_t.T[:, :heads]
    input3_out[...] = input3_t.T
    output3_out[...] = output3
    for h in range(heads):
        table_out[h] = table[:types, h * types : (h + 1) * types]


def swap(value, axis, step):
    count = lax.axis_size(axis)
    return lax.ppermute(value, axis, [(index, index ^ step) for index in range(count)])


def gather_blocks(block, axis):
    return gather_near(block, swap(block, axis, lax.axis_size(axis) // 2), axis)


def gather_near(block, far, axis):
    half = lax.axis_size(axis) // 2
    blocks = {0: block, half: far}
    for bit in reversed(range(half.bit_length() - 1)):
        step = 1 << bit
        for offset, held in list(blocks.items()):
            blocks[offset ^ step] = swap(held, axis, step)
    return [blocks[offset] for offset in range(len(blocks))]


def sum_over(value, axis):
    step = 1
    while step < lax.axis_size(axis):
        value = value + swap(value, axis, step)
        step *= 2
    return value


def per_device(
    pair_rep,
    cotangent,
    tok_mask,
    tok_types,
    pair_mask,
    triangle_gain,
    triangle_input,
    triangle_gating,
    product_gain,
    triangle_output,
    attend_gain,
    attend_bias,
    attend_input,
    attend_output,
    type_table,
):
    slab = pair_rep[0]
    cot = cotangent[0]
    rows, length, channels = slab.shape
    heads, types = type_table.shape[:2]
    count = lax.axis_size("dap")
    place = lax.axis_index("dap")
    place_arg = place.reshape(1).astype(jnp.int32)
    tokens = tok_mask[0].astype(F32)
    row_tokens = lax.dynamic_slice_in_dim(tokens, place * rows, rows)
    live = pair_mask[0].astype(F32) * row_tokens[:, None] * tokens[None, :]
    gain1_row, gain3_row = triangle_gain[None, :], attend_gain[None, :]
    gain1_col, gain2_col, gain3_col = (
        triangle_gain[:, None],
        product_gain[:, None],
        attend_gain[:, None],
    )
    vmem = pl.BlockSpec(memory_space=pltpu.VMEM)
    anywhere = pl.BlockSpec(memory_space=pl.ANY)
    smem = pl.BlockSpec(memory_space=pltpu.SMEM)
    cells = (rows, length, channels)
    turned = (rows, channels, length)

    half = rows // 2
    normed1_halves, right_halves = [], []
    for part in range(2):
        normed_part, right_part = call(
            right_kernel,
            [((half, length, channels), BF16), ((channels, half, length), BF16)],
            [slab, live, gain1_row, triangle_input],
            grid=(1,),
            in_specs=[
                pl.BlockSpec((half, length, channels), lambda step, part=part: (part, 0, 0)),
                pl.BlockSpec((half, length), lambda step, part=part: (part, 0)),
                vmem,
                vmem,
            ],
            scratch=[
                pltpu.VMEM((2 * channels, channels), BF16),
                pltpu.VMEM((channels * half, length), F32),
            ],
            us=3.0,
            name="right_projection",
        )
        normed1_halves.append(normed_part)
        right_halves.append(right_part)
    normed1, left, gate = call(
        partial(left_kernel, 2),
        [(cells, BF16), ((channels, rows, length), BF16), (cells, BF16)],
        [*normed1_halves, live, triangle_input, triangle_gating],
        scratch=[
            pltpu.VMEM((2 * channels, channels), BF16),
            pltpu.VMEM((channels * rows, length), F32),
        ],
        us=5.0,
        name="left_projection",
    )
    far = [swap(part, "dap", count // 2) for part in right_halves]
    left, *far = lax.optimization_barrier((left, *far))
    right_halves = [
        gather_near(part, other, "dap") for part, other in zip(right_halves, far)
    ]
    right_blocks = [right_halves[index % 2][index // 2] for index in range(2 * count)]
    right_all, normed2, scale2, update, middle, normed3, bias_rows = call(
        partial(product_kernel, count),
        [
            ((channels, length, length), BF16),
            (turned, BF16),
            ((rows, length), F32),
            (cells, BF16),
            (cells, BF16),
            (cells, BF16),
            ((rows, heads * length), BF16),
        ],
        [place_arg, *right_blocks, left, slab, gate, gain2_col, gain3_row]
        + [triangle_output, attend_bias],
        in_specs=[smem] + [vmem] * (2 * count + 7),
        scratch=[
            pltpu.VMEM((rows * channels, length), F32),
            pltpu.VMEM((rows * HEAD_ROWS, length), F32),
        ],
        us=14.0,
        name="product_and_norms",
    )
    bias_blocks = gather_blocks(bias_rows, "dap")
    left, bias_blocks[-1] = lax.optimization_barrier((left, bias_blocks[-1]))
    left_blocks = gather_blocks(left, "dap")

    block = 8
    steps = rows // block
    by_row = pl.BlockSpec((block, length, channels), lambda step: (step, 0, 0))
    by_row_wide = pl.BlockSpec((block, 4 * channels, length), lambda step: (step, 0, 0))

    def fixed(*shape):
        return pl.BlockSpec(shape, lambda step: (0,) * len(shape))

    attend_outs = call(
        partial(attend_kernel, count, block),
        [
            (cells, BF16),
            ((rows, 4 * channels, length), BF16),
            ((channels, channels), F32),
            ((HEAD_ROWS, channels), F32),
            ((rows, heads * length), F32),
        ]
        + [((rows, heads * length), BF16)] * (count - 1),
        [place_arg, type_table.reshape(heads * types, types), *bias_blocks]
        + [tok_types, tok_types.reshape(length, 1), live, normed3, middle, cot]
        + [attend_input, attend_output],
        grid=(steps,),
        in_specs=[smem, smem]
        + [fixed(rows, heads * length)] * count
        + [fixed(1, length), fixed(length, 1), fixed(rows, length), by_row, by_row, by_row]
        + [fixed(channels, 4 * channels), fixed(channels, channels)],
        out_specs=[by_row, by_row_wide, fixed(channels, channels), fixed(HEAD_ROWS, channels)]
        + [fixed(rows, heads * length)] * count,
        scratch=[
            pltpu.VMEM((length, heads * length), F32),
            pltpu.VMEM((length, heads * length), F32),
            pltpu.VMEM((channels, heads * length), BF16),
            pltpu.VMEM((3 * channels, channels), BF16),
            pltpu.VMEM((channels, 2 * channels), BF16),
        ],
        us=30.0,
        name="attention",
    )
    pair_out, d_projected3, d_output, d_table = attend_outs[:4]
    d_bias_parts = [attend_outs[4]] + [
        swap(attend_outs[4 + offset], "dap", offset) for offset in range(1, count)
    ]
    d_normed3, packed_a = call(
        projection_kernel,
        [(turned, F32), ((4 * channels + channels + 2 * HEAD_ROWS, channels), BF16)],
        [d_projected3, normed3, attend_input, d_output, d_table],
        grid=(steps,),
        in_specs=[by_row_wide, by_row, fixed(channels, 4 * channels)]
        + [fixed(channels, channels), fixed(HEAD_ROWS, channels)],
        out_specs=[
            pl.BlockSpec((block, channels, length), lambda step: (step, 0, 0)),
            fixed(5 * channels + 2 * HEAD_ROWS, channels),
        ],
        scratch=[pltpu.VMEM((4 * channels, channels), F32)],
        us=6.0,
        name="projection_back",
    )
    groups = channels * rows // length
    middle_outs = call(
        partial(middle_kernel, count),
        [
            (cells, BF16),
            (cells, BF16),
            ((channels * rows, length), BF16),
            ((channels + HEAD_ROWS, channels), F32),
        ]
        + [((groups, rows, length), BF16)] * count,
        [place_arg, *d_bias_parts, d_normed3, normed3, middle, cot, gain3_col, attend_bias]
        + [normed2, scale2, update, gate, gain2_col, triangle_output],
        in_specs=[smem] + [vmem] * (count + 12),
        scratch=[
            pltpu.VMEM((rows * HEAD_ROWS, length), F32),
            pltpu.VMEM((channels * rows, length), F32),
        ],
        us=12.0,
        name="middle_back",
    )
    d_middle, d_gate, d_product, grad_middle = middle_outs[:4]
    product_parts = [middle_outs[4]] + [
        swap(middle_outs[4 + offset], "dap", offset) for offset in range(1, count)
    ]
    d_left, packed_b = call(
        left_back_kernel,
        [((rows, 3 * channels, length), BF16), ((4 * channels + HEAD_ROWS, channels), BF16)],
        [right_all, d_product, normed1, live, triangle_input, d_gate, grad_middle],
        scratch=[
            pltpu.VMEM((rows * channels, length), F32),
            pltpu.VMEM((3 * channels, channels), F32),
        ],
        us=10.0,
        name="left_back",
    )
    used = packed_a.shape[0] + packed_b.shape[0] + 2 * channels
    share = -(-used // (count * HEAD_ROWS)) * HEAD_ROWS
    right_outs = call(
        partial(right_back_kernel, count),
        [((rows, 2 * channels, length), BF16)] + [((share, channels), BF16)] * count,
        [place_arg, *product_parts, *left_blocks, normed1, live, triangle_input]
        + [packed_a, packed_b],
        in_specs=[smem] + [vmem] * (2 * count + 5),
        scratch=[
            pltpu.VMEM((channels * rows, length), F32),
            pltpu.VMEM((2 * channels, channels), F32),
            pltpu.VMEM((share * count, channels), BF16),
        ],
        us=7.0,
        name="right_back",
    )
    d_right = right_outs[0]
    grad_share = right_outs[1].astype(F32)
    for offset in range(1, count):
        grad_share = grad_share + swap(right_outs[1 + offset], "dap", offset).astype(F32)
    grad_share = sum_over(grad_share.astype(BF16), "dp")
    grad_blocks = [grad_share] + [
        swap(grad_share, "dap", offset) for offset in range(1, count)
    ]
    (pair_grad,) = call(
        input_back_kernel,
        [(cells, BF16)],
        [d_left, d_right, slab, d_middle, gain1_col, triangle_input, triangle_gating],
        us=6.0,
        name="input_back",
    )
    weights = (triangle_input, triangle_gating, triangle_output, attend_bias, attend_input)
    gains = (gain1_row, product_gain[None, :], gain3_row)
    grads = call(
        partial(finish_kernel, count, (length * length * lax.axis_size("dp")) ** (-0.5)),
        [
            ((1, channels), F32),
            (triangle_input.shape, F32),
            (triangle_gating.shape, F32),
            ((1, channels), F32),
            (triangle_output.shape, F32),
            ((1, channels), F32),
            (attend_bias.shape, F32),
            (attend_input.shape, F32),
            (attend_output.shape, F32),
            (type_table.shape, F32),
        ],
        [place_arg, *grad_blocks, *weights, *gains],
        in_specs=[smem] + [vmem] * (count + 8),
        scratch=[pltpu.VMEM((share * count, channels), F32)],
        us=3.0,
        name="scale_gradients",
    )
    grads = [grad[0] if grad.shape[0] == 1 else grad for grad in grads]
    return (pair_out[None], pair_grad[None], *grads)


def solution(mesh):
    return jax.shard_map(
        per_device,
        mesh=mesh,
        in_specs=(
            P("dp", "dap", None, None),
            P("dp", "dap", None, None),
            P("dp", None),
            P("dp", None),
            P("dp", "dap", None),
        )
        + (P(),) * 10,
        out_specs=(
            P("dp", "dap", None, None),
            P("dp", "dap", None, None),
        )
        + (P(),) * 10,
        check_vma=False,
    )
```

profile of v0, /device:TPU:0, one launch (start us, length us, event | category | flops | bytes accessed | tf_op | source)
XLA Modules:
  0.0 165.1 jit_solution(3652932063963903237)
XLA Ops:
  5.0 2.2 %right_projection.2 = (bf16[16,128,128]{2,1,0:T(8,128)(2,1)S(1)}, bf16[128,16,128]{2,1,0:T(8,128)(2,1)S(1)}) custom-call(bf16[32,128,128]{2,1,0:T(8,128)(2,1)S(1)} %bitcast.36, f32[32,128]{1,0:T(8,128)S(1)} %fusion.live.refs_2_.refs_6_.refs_9_, f32[1,128]{1,0:T(1,128)S(1)} %bitcast.25, bf16[128,512]{1,0:T(8,128)(2,1)S(1)} %copy-done.12), custom_call_target="tpu_custom_call" | custom-call | flops 3000000000 | bytes 9000000 | tf_op jit(solution)/shard_map/right_projection/pallas_call | solution.py:74
  7.2 3.0 %collective-permute-start.2 = (bf16[128,16,128]{2,1,0:T(8,128)(2,1)S(1)}, bf16[128,16,128]{2,1,0:T(8,128)(2,1)S(1)}, u32[]{:S(2)}, u32[]{:S(2)}) collective-permute-start(bf16[128,16,128]{2,1,0:T(8,128)(2,1)S(1)} %get-tuple-element.66.refs_0_), channel_id=1, source_target_pairs={{0,16},{8,24},{16,0},{24,8},{1,17},{9,25},{17,1},{25,9},{2,18},{10... | collective-permute-start | bytes 1572872 | tf_op jit(solution)/shard_map/ppermute | solution.py:610
  10.2 3.0 %right_projection.3 = (bf16[16,128,128]{2,1,0:T(8,128)(2,1)S(1)}, bf16[128,16,128]{2,1,0:T(8,128)(2,1)}) custom-call(bf16[32,128,128]{2,1,0:T(8,128)(2,1)S(1)} %bitcast.37, f32[32,128]{1,0:T(8,128)S(1)} %fusion.live.refs_2_.refs_6_.refs_9_, f32[1,128]{1,0:T(1,128)S(1)} %bitcast.26, bf16[128,512]{1,0:T(8,128)(2,1)S(1)} %copy-done.12), custom_call_target="tpu_custom_call" | custom-call | flops 3000000000 | bytes 9000000 | tf_op jit(solution)/shard_map/right_projection/pallas_call | solution.py:74
  13.8 4.2 %left_projection.1 = (bf16[32,128,128]{2,1,0:T(8,128)(2,1)S(1)}, bf16[128,32,128]{2,1,0:T(8,128)(2,1)S(1)}, bf16[32,128,128]{2,1,0:T(8,128)(2,1)S(1)}) custom-call(bf16[16,128,128]{2,1,0:T(8,128)(2,1)S(1)} %get-tuple-element.68.refs_0_, bf16[16,128,128]{2,1,0:T(8,128)(2,1)S(1)} %get-tuple-element.69.refs_1_, f32[32,128]{1,0:T(8,128)S(1)} %fusion.live.refs_2_.refs_6_.refs_9_, ...), custom_call_target="tpu_custom_call" | custom-call | flops 5000000000 | bytes 15000000 | tf_op jit(solution)/shard_map/left_projection/pallas_call | solution.py:74
  19.9 3.0 %collective-permute-done.2.refs_4_ = bf16[128,16,128]{2,1,0:T(8,128)(2,1)S(1)} collective-permute-done((bf16[128,16,128]{2,1,0:T(8,128)(2,1)S(1)}, bf16[128,16,128]{2,1,0:T(8,128)(2,1)S(1)}, u32[]{:S(2)}, u32[]{:S(2)}) %collective-permute-start.2) | collective-permute-done | bytes 524320 | tf_op jit(solution)/shard_map/ppermute | solution.py:610
  23.0 10.5 %collective-permute-done.3.refs_5_ = bf16[128,16,128]{2,1,0:T(8,128)(2,1)} collective-permute-done((bf16[128,16,128]{2,1,0:T(8,128)(2,1)}, bf16[128,16,128]{2,1,0:T(8,128)(2,1)}, u32[]{:S(2)}, u32[]{:S(2)}) %collective-permute-start.3) | collective-permute-done | bytes 524320 | tf_op jit(solution)/shard_map/ppermute | solution.py:610
  40.0 13.8 %product_and_norms.1 = (bf16[128,128,128]{2,1,0:T(8,128)(2,1)S(1)}, bf16[32,128,128]{2,1,0:T(8,128)(2,1)S(1)}, f32[32,128]{1,0:T(8,128)S(1)}, bf16[32,128,128]{2...) custom-call(s32[1]{0:T(128)} %bitcast.place_ref, ...), custom_call_target="tpu_custom_call" | custom-call | flops 14000000000 | bytes 42000000 | tf_op jit(solution)/shard_map/product_and_norms/pallas_call | solution.py:74
  53.8 2.0 %copy-done.30 = bf16[128,128,128]{2,1,0:T(8,128)(2,1)} copy-done((bf16[128,128,128]{2,1,0:T(8,128)(2,1)}, bf16[128,128,128]{2,1,0:T(8,128)(2,1)S(1)}, u32[]{:S(2)}) %copy-start.30) | copy-done | bytes 4194328
  59.9 1.8 %collective-permute-start.7 = (bf16[32,512]{1,0:T(8,128)(2,1)}, bf16[32,512]{1,0:T(8,128)(2,1)}, u32[]{:S(2)}, u32[]{:S(2)}) collective-permute-start(bf16[32,512]{1,0:T(8,128)(2,1)} %get-tuple-element.75.refs_0_), channel_id=1, source_target_pairs={{0,16},{8,24},{16,0},{24,8},{1,17},{9,25},{17,1},{25,9},{2,18},{10... | collective-permute-start | bytes 98312 | tf_op jit(solution)/shard_map/ppermute | solution.py:610
  61.7 2.5 %collective-permute-done.7.refs_2_ = bf16[32,512]{1,0:T(8,128)(2,1)} collective-permute-done((bf16[32,512]{1,0:T(8,128)(2,1)}, bf16[32,512]{1,0:T(8,128)(2,1)}, u32[]{:S(2)}, u32[]{:S(2)}) %collective-permute-start.7) | collective-permute-done | bytes 32800 | tf_op jit(solution)/shard_map/ppermute | solution.py:610
  71.8 19.8 %attention.1 = (bf16[32,128,128]{2,1,0:T(8,128)(2,1)}, bf16[32,512,128]{2,1,0:T(8,128)(2,1)S(1)}, f32[128,128]{1,0:T(8,128)S(1)}, f32[16,128]{1,0:T(8,128)S(1)},...) custom-call(s32[1]{0:T(128)} %bitcast.place_ref, ...), custom_call_target="tpu_custom_call" | custom-call | flops 30000001024 | bytes 90000000 | tf_op jit(solution)/shard_map/attention/pallas_call | solution.py:74
  93.4 2.4 %projection_back.1 = (f32[32,128,128]{2,1,0:T(8,128)S(1)}, bf16[672,128]{1,0:T(8,128)(2,1)S(1)}) custom-call(bf16[32,512,128]{2,1,0:T(8,128)(2,1)S(1)} %get-tuple-element.85.d_projected, bf16[32,128,128]{2,1,0:T(8,128)(2,1)S(1)} %copy-done.33, bf16[128,512]{1,0:T(8,128)(2,1)S(1)} %copy-done.15, f32[128,128]{1,0:T(8,128)S(1)} %get-tuple-element.86.d_output, ...), custom_call_target="tpu_custom_call" | custom-call | flops 6000000000 | bytes 18000000 | tf_op jit(solution)/shard_map/projection_back/pallas_call | solution.py:74
  96.3 9.5 %middle_back.1 = (bf16[32,128,128]{2,1,0:T(8,128)(2,1)S(1)}, bf16[32,128,128]{2,1,0:T(8,128)(2,1)S(1)}, bf16[4096,128]{1,0:T(8,128)(2,1)S(1)}, f32[144,128]{1,0:...) custom-call(s32[1]{0:T(128)} %bitcast.place_ref, ...), custom_call_target="tpu_custom_call" | custom-call | flops 12000000000 | bytes 36000000 | tf_op jit(solution)/shard_map/middle_back/pallas_call | solution.py:74
  108.7 7.8 %left_back.1 = (bf16[32,384,128]{2,1,0:T(8,128)(2,1)S(1)}, bf16[528,128]{1,0:T(8,128)(2,1)S(1)}) custom-call(bf16[128,128,128]{2,1,0:T(8,128)(2,1)S(1)} %copy-done.31, bf16[4096,128]{1,0:T(8,128)(2,1)S(1)} %get-tuple-element.92.d_product, bf16[32,128,128]{2,1,0:T(8,128)(2,1)S(1)} %copy-done.36, f32[32,128]{1,0:T(8,128)S(1)} %fusion.live.refs_2_.refs_6_.refs_9_, ...), custom_call_target="tpu_custom_call" | custom-call | flops 10000000000 | bytes 30000000 | tf_op jit(solution)/shard_map/left_back/pallas_call | solution.py:74
  118.2 2.4 %collective-permute-done.14.refs_3_ = bf16[32,32,128]{2,1,0:T(8,128)(2,1)S(1)} collective-permute-done((bf16[32,32,128]{2,1,0:T(8,128)(2,1)S(1)}, bf16[32,32,128]{2,1,0:T(8,128)(2,1)S(1)}, u32[]{:S(2)}, u32[]{:S(2)}) %collective-permute-start.14) | collective-permute-done | bytes 262176 | tf_op jit(solution)/shard_map/ppermute | solution.py:610
  120.6 6.7 %right_back.1 = (bf16[32,256,128]{2,1,0:T(8,128)(2,1)S(1)}, bf16[368,128]{1,0:T(8,128)(2,1)S(1)}, bf16[368,128]{1,0:T(8,128)(2,1)S(1)}, bf16[368,128]{1,0:T(8,128)(2,1)S(1)}, bf16[368,128]{1,0:T(8,128)(2,1)S(1)}) custom-call(s32[1]{0:T(128)} %bitcast.place_ref, bf16[32,32,128]{2,1,0:T(8,128)(2,1)S(1)} %get-tuple-element.97.refs_0_, ...), custom_call_target="tpu_custom_call" | custom-call | flops 7000000000 | bytes 21000000 | tf_op jit(solution)/shard_map/right_back/pallas_call | solution.py:74
  130.7 2.5 %collective-permute-done.20 = bf16[368,128]{1,0:T(8,128)(2,1)S(1)} collective-permute-done((bf16[368,128]{1,0:T(8,128)(2,1)S(1)}, bf16[368,128]{1,0:T(8,128)(2,1)S(1)}, u32[]{:S(2)}, u32[]{:S(2)}) %collective-permute-start.20) | collective-permute-done | bytes 94240 | tf_op jit(solution)/shard_map/ppermute | solution.py:610
  133.2 2.5 %collective-permute-done.19 = bf16[368,128]{1,0:T(8,128)(2,1)S(1)} collective-permute-done((bf16[368,128]{1,0:T(8,128)(2,1)S(1)}, bf16[368,128]{1,0:T(8,128)(2,1)S(1)}, u32[]{:S(2)}, u32[]{:S(2)}) %collective-permute-start.19) | collective-permute-done | bytes 94240 | tf_op jit(solution)/shard_map/ppermute | solution.py:610
  137.3 3.1 %collective-permute-done.21 = bf16[368,128]{1,0:T(8,128)(2,1)S(1)} collective-permute-done((bf16[368,128]{1,0:T(8,128)(2,1)S(1)}, bf16[368,128]{1,0:T(8,128)(2,1)S(1)}, u32[]{:S(2)}, u32[]{:S(2)}) %collective-permute-start.21) | collective-permute-done | bytes 94240 | tf_op jit(solution)/shard_map/ppermute | solution.py:610
  142.1 3.0 %collective-permute-done.22 = bf16[368,128]{1,0:T(8,128)(2,1)S(1)} collective-permute-done((bf16[368,128]{1,0:T(8,128)(2,1)S(1)}, bf16[368,128]{1,0:T(8,128)(2,1)S(1)}, u32[]{:S(2)}, u32[]{:S(2)}) %collective-permute-start.22) | collective-permute-done | bytes 94240 | tf_op jit(solution)/shard_map/ppermute | solution.py:610
  145.1 2.8 %collective-permute-start.23 = (bf16[368,128]{1,0:T(8,128)(2,1)S(1)}, bf16[368,128]{1,0:T(8,128)(2,1)S(1)}, u32[]{:S(2)}, u32[]{:S(2)}) collective-permute-start(bf16[368,128]{1,0:T(8,128)(2,1)S(1)} %add.26), channel_id=1, source_target_pairs={{0,4},{1,5},{2,6},{3,7},{4,0},{5,1},{6,2},{7,3},{8,12},{9,13},{10,... | collective-permute-start | bytes 282632 | tf_op jit(solution)/shard_map/ppermute | solution.py:610
  148.0 2.7 %collective-permute-done.23 = bf16[368,128]{1,0:T(8,128)(2,1)S(1)} collective-permute-done((bf16[368,128]{1,0:T(8,128)(2,1)S(1)}, bf16[368,128]{1,0:T(8,128)(2,1)S(1)}, u32[]{:S(2)}, u32[]{:S(2)}) %collective-permute-start.23) | collective-permute-done | bytes 94240 | tf_op jit(solution)/shard_map/ppermute | solution.py:610
  152.6 1.9 %copy-done.25 = bf16[32,384,128]{2,1,0:T(8,128)(2,1)S(1)} copy-done((bf16[32,384,128]{2,1,0:T(8,128)(2,1)S(1)}, bf16[32,384,128]{2,1,0:T(8,128)(2,1)}, u32[]{:S(2)}) %copy-start.25) | copy-done | bytes 3145752
  157.3 5.9 %input_back.1 = bf16[32,128,128]{2,1,0:T(8,128)(2,1)} custom-call(bf16[32,384,128]{2,1,0:T(8,128)(2,1)S(1)} %copy-done.25, bf16[32,256,128]{2,1,0:T(8,128)(2,1)S(1)} %copy-done.27, bf16[32,128,128]{2,1,0:T(8,128)(2,1)S(1)} %bitcast.39, bf16[32,128,128]{2,1,0:T(8,128)(2,1)S(1)} %copy-done.29, f32[128,1]{1,0:T(8,128)S(1)} %copy.35.gain_col, ...), custom_call_target="tpu_custom_call" | custom-call | flops 6000000000 | bytes 18000000 | tf_op jit(solution)/shard_map/input_back/pallas_call | solution.py:74
  (154 shorter events, 45.2 us)
Async XLA Ops:
  7.2 15.8 %collective-permute-start.2 = (bf16[128,16,128]{2,1,0:T(8,128)(2,1)S(1)}, bf16[128,16,128]{2,1,0:T(8,128)(2,1)S(1)}, u32[]{:S(2)}, u32[]{:S(2)}) collective-permute-start(bf16[128,16,128]{2,1,0:T(8,128)(2,1)S(1)} %get-tuple-element.66.refs_0_), channel_id=1, source_target_pairs={{0,16},{8,24},{16,0},{24,8},{1,17},{9,25},{17,1},{25,9},{2,18},{10... | collective-permute-start | bytes 1572872 | tf_op jit(solution)/shard_map/ppermute | solution.py:610
  13.2 20.3 %collective-permute-start.3 = (bf16[128,16,128]{2,1,0:T(8,128)(2,1)}, bf16[128,16,128]{2,1,0:T(8,128)(2,1)}, u32[]{:S(2)}, u32[]{:S(2)}) collective-permute-start(bf16[128,16,128]{2,1,0:T(8,128)(2,1)} %get-tuple-element.67.refs_1_), channel_id=1, source_target_pairs={{0,16},{8,24},{16,0},{24,8},{1,17},{9,25},{17,1},{25,9},{2,18},{10... | collective-permute-start | bytes 1572872 | tf_op jit(solution)/shard_map/ppermute | solution.py:610
  13.2 21.8 %collective-permute-start = (bf16[128,16,128]{2,1,0:T(8,128)(2,1)S(1)}, bf16[128,16,128]{2,1,0:T(8,128)(2,1)}, u32[]{:S(2)}, u32[]{:S(2)}) collective-permute-start(bf16[128,16,128]{2,1,0:T(8,128)(2,1)S(1)} %get-tuple-element.66.refs_0_), channel_id=1, source_target_pairs={{0,8},{8,0},{16,24},{24,16},{1,9},{9,1},{17,25},{25,17},{2,10},{10... | collective-permute-start | bytes 1572872 | tf_op jit(solution)/shard_map/ppermute | solution.py:610
  13.2 21.8 %collective-permute-start.1 = (bf16[128,16,128]{2,1,0:T(8,128)(2,1)}, bf16[128,16,128]{2,1,0:T(8,128)(2,1)}, u32[]{:S(2)}, u32[]{:S(2)}) collective-permute-start(bf16[128,16,128]{2,1,0:T(8,128)(2,1)} %get-tuple-element.67.refs_1_), channel_id=1, source_target_pairs={{0,8},{8,0},{16,24},{24,16},{1,9},{9,1},{17,25},{25,17},{2,10},{10... | collective-permute-start | bytes 1572872 | tf_op jit(solution)/shard_map/ppermute | solution.py:610
  59.9 4.2 %collective-permute-start.7 = (bf16[32,512]{1,0:T(8,128)(2,1)}, bf16[32,512]{1,0:T(8,128)(2,1)}, u32[]{:S(2)}, u32[]{:S(2)}) collective-permute-start(bf16[32,512]{1,0:T(8,128)(2,1)} %get-tuple-element.75.refs_0_), channel_id=1, source_target_pairs={{0,16},{8,24},{16,0},{24,8},{1,17},{9,25},{17,1},{25,9},{2,18},{10... | collective-permute-start | bytes 98312 | tf_op jit(solution)/shard_map/ppermute | solution.py:610
  64.2 3.5 %collective-permute-start.6 = (bf16[32,512]{1,0:T(8,128)(2,1)}, bf16[32,512]{1,0:T(8,128)(2,1)}, u32[]{:S(2)}, u32[]{:S(2)}) collective-permute-start(bf16[32,512]{1,0:T(8,128)(2,1)} %get-tuple-element.75.refs_0_), channel_id=1, source_target_pairs={{0,8},{8,0},{16,24},{24,16},{1,9},{9,1},{17,25},{25,17},{2,10},{10... | collective-permute-start | bytes 98312 | tf_op jit(solution)/shard_map/ppermute | solution.py:610
  65.7 54.9 %collective-permute-start.15 = (bf16[128,32,128]{2,1,0:T(8,128)(2,1)S(1)}, bf16[128,32,128]{2,1,0:T(8,128)(2,1)S(1)}, u32[]{:S(2)}, u32[]{:S(2)}) collective-permute-start(bf16[128,32,128]{2,1,0:T(8,128)(2,1)S(1)} %get-tuple-element.101.refs_8_.refs_4_), channel_id=1, source_target_pairs={{0,8},{8,0},{16,24},{24,16},{1,9},{9,1},{17,25},{25,17},{2,10},{10... | collective-permute-start | bytes 3145736 | tf_op jit(solution)/shard_map/ppermute | solution.py:610
  65.9 30.0 %collective-permute-start.16 = (bf16[128,32,128]{2,1,0:T(8,128)(2,1)S(1)}, bf16[128,32,128]{2,1,0:T(8,128)(2,1)S(1)}, u32[]{:S(2)}, u32[]{:S(2)}) collective-permute-start(bf16[128,32,128]{2,1,0:T(8,128)(2,1)S(1)} %get-tuple-element.101.refs_8_.refs_4_), channel_id=1, source_target_pairs={{0,16},{8,24},{16,0},{24,8},{1,17},{9,25},{17,1},{25,9},{2,18},{10... | collective-permute-start | bytes 3145736 | tf_op jit(solution)/shard_map/ppermute | solution.py:610
  91.5 4.7 %collective-permute-start.9 = (bf16[32,512]{1,0:T(8,128)(2,1)S(1)}, bf16[32,512]{1,0:T(8,128)(2,1)S(1)}, u32[]{:S(2)}, u32[]{:S(2)}) collective-permute-start(bf16[32,512]{1,0:T(8,128)(2,1)S(1)} %get-tuple-element.82), channel_id=1, source_target_pairs={{0,8},{8,0},{16,24},{24,16},{1,9},{9,1},{17,25},{25,17},{2,10},{10... | collective-permute-start | bytes 98312 | tf_op jit(solution)/shard_map/ppermute | solution.py:610
  91.6 4.7 %collective-permute-start.10 = (bf16[32,512]{1,0:T(8,128)(2,1)S(1)}, bf16[32,512]{1,0:T(8,128)(2,1)S(1)}, u32[]{:S(2)}, u32[]{:S(2)}) collective-permute-start(bf16[32,512]{1,0:T(8,128)(2,1)S(1)} %get-tuple-element.83), channel_id=1, source_target_pairs={{0,16},{8,24},{16,0},{24,8},{1,17},{9,25},{17,1},{25,9},{2,18},{10... | collective-permute-start | bytes 98312 | tf_op jit(solution)/shard_map/ppermute | solution.py:610
  91.9 4.4 %collective-permute-start.11 = (bf16[32,512]{1,0:T(8,128)(2,1)S(1)}, bf16[32,512]{1,0:T(8,128)(2,1)S(1)}, u32[]{:S(2)}, u32[]{:S(2)}) collective-permute-start(bf16[32,512]{1,0:T(8,128)(2,1)S(1)} %get-tuple-element.84), channel_id=1, source_target_pairs={{0,24},{8,16},{16,8},{24,0},{1,25},{9,17},{17,9},{25,1},{2,26},{10... | collective-permute-start | bytes 98312 | tf_op jit(solution)/shard_map/ppermute | solution.py:610
  95.8 24.8 %collective-permute-start.17 = (bf16[128,32,128]{2,1,0:T(8,128)(2,1)S(1)}, bf16[128,32,128]{2,1,0:T(8,128)(2,1)S(1)}, u32[]{:S(2)}, u32[]{:S(2)}) collective-permute-start(bf16[128,32,128]{2,1,0:T(8,128)(2,1)S(1)} %collective-permute-done.16.refs_6_), channel_id=1, source_target_pairs={{0,8},{8,0},{16,24},{24,16},{1,9},{9,1},{17,25},{25,17},{2,10},{10... | collective-permute-start | bytes 3145736 | tf_op jit(solution)/shard_map/ppermute | solution.py:610
  106.8 11.3 %collective-permute-start.12 = (bf16[32,32,128]{2,1,0:T(8,128)(2,1)S(1)}, bf16[32,32,128]{2,1,0:T(8,128)(2,1)S(1)}, u32[]{:S(2)}, u32[]{:S(2)}) collective-permute-start(bf16[32,32,128]{2,1,0:T(8,128)(2,1)S(1)} %get-tuple-element.98), channel_id=1, source_target_pairs={{0,8},{8,0},{16,24},{24,16},{1,9},{9,1},{17,25},{25,17},{2,10},{10... | collective-permute-start | bytes 786440 | tf_op jit(solution)/shard_map/ppermute | solution.py:610
  107.0 11.2 %collective-permute-start.13 = (bf16[32,32,128]{2,1,0:T(8,128)(2,1)S(1)}, bf16[32,32,128]{2,1,0:T(8,128)(2,1)S(1)}, u32[]{:S(2)}, u32[]{:S(2)}) collective-permute-start(bf16[32,32,128]{2,1,0:T(8,128)(2,1)S(1)} %get-tuple-element.99), channel_id=1, source_target_pairs={{0,16},{8,24},{16,0},{24,8},{1,17},{9,25},{17,1},{25,9},{2,18},{10... | collective-permute-start | bytes 786440 | tf_op jit(solution)/shard_map/ppermute | solution.py:610
  107.7 12.9 %collective-permute-start.14 = (bf16[32,32,128]{2,1,0:T(8,128)(2,1)S(1)}, bf16[32,32,128]{2,1,0:T(8,128)(2,1)S(1)}, u32[]{:S(2)}, u32[]{:S(2)}) collective-permute-start(bf16[32,32,128]{2,1,0:T(8,128)(2,1)S(1)} %get-tuple-element.100), channel_id=1, source_target_pairs={{0,24},{8,16},{16,8},{24,0},{1,25},{9,17},{17,9},{25,1},{2,26},{10... | collective-permute-start | bytes 786440 | tf_op jit(solution)/shard_map/ppermute | solution.py:610
  128.6 4.6 %collective-permute-start.20 = (bf16[368,128]{1,0:T(8,128)(2,1)S(1)}, bf16[368,128]{1,0:T(8,128)(2,1)S(1)}, u32[]{:S(2)}, u32[]{:S(2)}) collective-permute-start(bf16[368,128]{1,0:T(8,128)(2,1)S(1)} %get-tuple-element.109), channel_id=1, source_target_pairs={{0,24},{8,16},{16,8},{24,0},{1,25},{9,17},{17,9},{25,1},{2,26},{10... | collective-permute-start | bytes 282632 | tf_op jit(solution)/shard_map/ppermute | solution.py:610
  129.3 6.4 %collective-permute-start.19 = (bf16[368,128]{1,0:T(8,128)(2,1)S(1)}, bf16[368,128]{1,0:T(8,128)(2,1)S(1)}, u32[]{:S(2)}, u32[]{:S(2)}) collective-permute-start(bf16[368,128]{1,0:T(8,128)(2,1)S(1)} %get-tuple-element.108), channel_id=1, source_target_pairs={{0,16},{8,24},{16,0},{24,8},{1,17},{9,25},{17,1},{25,9},{2,18},{10... | collective-permute-start | bytes 282632 | tf_op jit(solution)/shard_map/ppermute | solution.py:610
  130.7 5.0 %collective-permute-start.18 = (bf16[368,128]{1,0:T(8,128)(2,1)S(1)}, bf16[368,128]{1,0:T(8,128)(2,1)S(1)}, u32[]{:S(2)}, u32[]{:S(2)}) collective-permute-start(bf16[368,128]{1,0:T(8,128)(2,1)S(1)} %get-tuple-element.107), channel_id=1, source_target_pairs={{0,8},{8,0},{16,24},{24,16},{1,9},{9,1},{17,25},{25,17},{2,10},{10... | collective-permute-start | bytes 282632 | tf_op jit(solution)/shard_map/ppermute | solution.py:610
  135.8 4.6 %collective-permute-start.21 = (bf16[368,128]{1,0:T(8,128)(2,1)S(1)}, bf16[368,128]{1,0:T(8,128)(2,1)S(1)}, u32[]{:S(2)}, u32[]{:S(2)}) collective-permute-start(bf16[368,128]{1,0:T(8,128)(2,1)S(1)} %add_convert_fusion), channel_id=1, source_target_pairs={{0,1},{1,0},{2,3},{3,2},{4,5},{5,4},{6,7},{7,6},{8,9},{9,8},{10,11... | collective-permute-start | bytes 282632 | tf_op jit(solution)/shard_map/ppermute | solution.py:610
  140.4 4.6 %collective-permute-start.22 = (bf16[368,128]{1,0:T(8,128)(2,1)S(1)}, bf16[368,128]{1,0:T(8,128)(2,1)S(1)}, u32[]{:S(2)}, u32[]{:S(2)}) collective-permute-start(bf16[368,128]{1,0:T(8,128)(2,1)S(1)} %add.25), channel_id=1, source_target_pairs={{0,2},{1,3},{2,0},{3,1},{4,6},{5,7},{6,4},{7,5},{8,10},{9,11},{10,... | collective-permute-start | bytes 282632 | tf_op jit(solution)/shard_map/ppermute | solution.py:610
  145.1 5.5 %collective-permute-start.23 = (bf16[368,128]{1,0:T(8,128)(2,1)S(1)}, bf16[368,128]{1,0:T(8,128)(2,1)S(1)}, u32[]{:S(2)}, u32[]{:S(2)}) collective-permute-start(bf16[368,128]{1,0:T(8,128)(2,1)S(1)} %add.26), channel_id=1, source_target_pairs={{0,4},{1,5},{2,6},{3,7},{4,0},{5,1},{6,2},{7,3},{8,12},{9,13},{10,... | collective-permute-start | bytes 282632 | tf_op jit(solution)/shard_map/ppermute | solution.py:610
  150.7 12.5 %collective-permute-start.24 = (bf16[368,128]{1,0:T(8,128)(2,1)S(1)}, bf16[368,128]{1,0:T(8,128)(2,1)S(1)}, u32[]{:S(2)}, u32[]{:S(2)}) collective-permute-start(bf16[368,128]{1,0:T(8,128)(2,1)S(1)} %add.27.refs_0_), channel_id=1, source_target_pairs={{0,8},{8,0},{16,24},{24,16},{1,9},{9,1},{17,25},{25,17},{2,10},{10... | collective-permute-start | bytes 282632 | tf_op jit(solution)/shard_map/ppermute | solution.py:610
  150.7 12.5 %collective-permute-start.25 = (bf16[368,128]{1,0:T(8,128)(2,1)S(1)}, bf16[368,128]{1,0:T(8,128)(2,1)S(1)}, u32[]{:S(2)}, u32[]{:S(2)}) collective-permute-start(bf16[368,128]{1,0:T(8,128)(2,1)S(1)} %add.27.refs_0_), channel_id=1, source_target_pairs={{0,16},{8,24},{16,0},{24,8},{1,17},{9,25},{17,1},{25,9},{2,18},{10... | collective-permute-start | bytes 282632 | tf_op jit(solution)/shard_map/ppermute | solution.py:610
  151.4 11.8 %collective-permute-start.26 = (bf16[368,128]{1,0:T(8,128)(2,1)S(1)}, bf16[368,128]{1,0:T(8,128)(2,1)S(1)}, u32[]{:S(2)}, u32[]{:S(2)}) collective-permute-start(bf16[368,128]{1,0:T(8,128)(2,1)S(1)} %add.27.refs_0_), channel_id=1, source_target_pairs={{0,24},{8,16},{16,8},{24,0},{1,25},{9,17},{17,9},{25,1},{2,26},{10... | collective-permute-start | bytes 282632 | tf_op jit(solution)/shard_map/ppermute | solution.py:610
  (53 other events, 386.4 us)
where the time goes:
time: 166 us; the launch traced here: 165 us
  Pallas kernels  76.5 us (46%)
  waiting for transfers between devices  34.7 us (21%)
  local copies, waits for them, and re-layouts  29.1 us (18%)
  starting transfers between devices  22.3 us (13%)
    pallas_call x11, Pallas kernels, call(): pl.pallas_call(kernel, out_shape=[jax.ShapeDtypeStruct(shape, dtype) for...  76.5 us
    ppermute x27, waiting for transfers between devices, swap(): lax.ppermute(value, axis, [(index, index ^ step) for index in range(count)])  34.7 us
    unnamed x102, local copies, waits for them, and re-layouts  28.5 us
    ppermute x27, starting transfers between devices, swap(): lax.ppermute(value, axis, [(index, index ^ step) for index in range(count)])  22.3 us
  transfers between devices with their start and end apart: 27, of which 12 were waited for; matrix products, arithmetic and copies ran while one was open for 0% of the time, Pallas kernels for 32%

commit v1 on v0

v1 whole, which is shorter than its diff:
```python
import math
from functools import partial

import jax
import jax.numpy as jnp
from jax import lax
from jax.experimental import pallas as pl
from jax.experimental.pallas import tpu as pltpu
from jax.sharding import PartitionSpec as P

EPSILON = 1e-05
F32 = jnp.float32
BF16 = jnp.bfloat16
VMEM_MARGIN = 4 * 1024 * 1024
W_PRODUCT, W_ATTEND, W_MIDDLE = 8, 4, 8
HEAD_ROWS = 16


def mm(left, right):
    return lax.dot_general(left, right, (((1,), (0,)), ((), ())), preferred_element_type=F32)


def mmt(left, right):
    return lax.dot_general(left, right, (((1,), (1,)), ((), ())), preferred_element_type=F32)


def sigmoid(value):
    return 1.0 / (1.0 + jnp.exp(-value))


def identity(size):
    rows = lax.broadcasted_iota(jnp.int32, (size, size), 0)
    columns = lax.broadcasted_iota(jnp.int32, (size, size), 1)
    return (rows == columns).astype(F32).astype(BF16)


def norm_parts(values, axis):
    centred = values - jnp.mean(values, axis=axis, keepdims=True)
    spread = jnp.mean(centred * centred, axis=axis, keepdims=True)
    scale = lax.rsqrt(spread + EPSILON)
    return centred * scale, scale


def norm_back(d_hat, hat, scale, axis):
    first = jnp.mean(d_hat, axis=axis, keepdims=True)
    second = jnp.mean(d_hat * hat, axis=axis, keepdims=True)
    return scale * (d_hat - first - hat * second)


def lockstep(row, indices):
    going = [row(index) for index in indices]
    results = [None] * len(going)
    running = True
    while running:
        for at, one in enumerate(going):
            try:
                next(one)
            except StopIteration as stop:
                results[at] = stop.value
                running = False
    return results


def over_rows(count, width, row, finish=None, first=0):
    def some(index, carry):
        results = lockstep(row, [first + index * width + at for at in range(width)])
        if finish is not None:
            finish(results)
        return carry

    lax.fori_loop(0, count // width, some, 0)


def split_copies(source, target, sems, parts):
    size = source.shape[0] // parts
    return [
        pltpu.make_async_copy(
            source.at[pl.ds(part * size, size)], target.at[pl.ds(part * size, size)], sems.at[part]
        )
        for part in range(parts)
    ]


def start(copies):
    for copy in copies:
        copy.start()


def wait(copies):
    for copy in copies:
        copy.wait()


def call(kernel, outs, args, scratch=(), grid=(), in_specs=None, out_specs=None, us=5.0, name=None, aliases=None):
    whole = pl.BlockSpec(memory_space=pltpu.VMEM)
    in_specs = in_specs or [whole] * len(args)
    out_specs = out_specs or [whole] * len(outs)
    held = sum(
        math.prod(one.shape) * jnp.dtype(one.dtype).itemsize
        for one in scratch
        if getattr(one, "memory_space", None) == pltpu.VMEM
    )
    args = [
        pltpu.with_memory_space_constraint(arg, pltpu.HBM)
        if spec.memory_space == pltpu.HBM
        else arg
        for arg, spec in zip(args, in_specs)
    ]
    return pl.pallas_call(
        kernel,
        out_shape=[
            pltpu.HBM(shape, dtype)
            if spec.memory_space == pltpu.HBM
            else jax.ShapeDtypeStruct(shape, dtype)
            for (shape, dtype), spec in zip(outs, out_specs)
        ],
        grid=grid,
        in_specs=in_specs,
        out_specs=out_specs,
        scratch_shapes=list(scratch),
        compiler_params=pltpu.CompilerParams(vmem_limit_bytes=held + VMEM_MARGIN),
        cost_estimate=pl.CostEstimate(
            flops=int(us * 1.0e9), bytes_accessed=int(us * 3.0e6), transcendentals=0
        ),
        input_output_aliases=aliases or {},
        name=name,
    )(*args)


def right_kernel(
    part, pair_any, mask_any, tokens_any, gain_any, weight_any, normed_out, right_out, live_out, *scratch
):
    pair, mask, tokens, gain, weight, weight_t, lay, sems = scratch
    rows, length, channels = pair.shape
    place = lax.axis_index("dap")
    span = pl.ds(part * rows, rows)
    sources = [mask_any.at[span], tokens_any, gain_any, weight_any, pair_any.at[span]]
    copies = [
        pltpu.make_async_copy(source, target, sems.at[at])
        for at, (source, target) in enumerate(zip(sources, (mask, tokens, gain, weight, pair)))
    ]
    start(copies)
    wait(copies)
    first = place * (mask_any.shape[0]) + part * rows
    lines = lax.broadcasted_iota(jnp.int32, (rows, length), 0) + first
    lanes = lax.broadcasted_iota(jnp.int32, (rows, length), 1)
    wide = tokens[...].astype(F32)
    own = jnp.sum(jnp.where(lines == lanes, wide, 0.0), axis=1, keepdims=True)
    live_out[...] = mask[...].astype(F32) * own * wide
    weight_t[...] = weight[:, 2 * channels : 4 * channels].astype(F32).T.astype(BF16)

    def row(i):
        hat, _ = norm_parts(pair[i].astype(F32), -1)
        yield
        normed = (hat * gain[...]).astype(BF16)
        normed_out[i] = normed
        projected = mmt(weight_t[...], normed)
        yield
        right = sigmoid(projected[channels:]) * projected[:channels] * live_out[pl.ds(i, 1), :]
        lay[pl.ds(i, channels, stride=rows), :] = right

    over_rows(rows, 8, row)
    right_out[...] = lay[...].reshape(channels, rows, length).astype(BF16)


def gate_factors(projected, live_row, channels):
    value, pre = projected[:channels], projected[channels:]
    gate = sigmoid(pre)
    slope = gate * live_row
    out = slope * value
    factors = jnp.concatenate([slope.astype(BF16), (out * (1.0 - gate)).astype(BF16)], axis=0)
    return out, factors


def left_kernel(parts, *refs):
    normed_parts = refs[:parts]
    live_parts = refs[parts : 2 * parts]
    weight, gating = refs[2 * parts : 2 * parts + 2]
    normed_any, low_out, high_out, gate_any, live, factor_any = refs[2 * parts + 2 : 2 * parts + 8]
    weight_t, lay, gates, factors, sems = refs[2 * parts + 8 :]
    rows, length, channels = gates.shape
    half = rows // parts
    weight_t[...] = weight[:, : 2 * channels].astype(F32).T.astype(BF16)
    outs = []
    for part in range(parts):
        span = pl.ds(part * half, half)
        copy = pltpu.make_async_copy(normed_parts[part], normed_any.at[span], sems.at[0, part])
        copy.start()
        outs.append(copy)
        live[span, :] = live_parts[part][...]

        def row(i, part=part):
            normed = normed_parts[part][i]
            at = i + part * half
            projected = mmt(weight_t[...], normed)
            gate = mm(normed, gating[...])
            yield
            left, factors[at] = gate_factors(projected, live[pl.ds(at, 1), :], channels)
            lay[pl.ds(at, channels, stride=rows), :] = left
            gates[at] = sigmoid(gate)

        over_rows(half, 8, row)
        for index, (source, target) in enumerate(((gates, gate_any), (factors, factor_any))):
            copy = pltpu.make_async_copy(
                source.at[span], target.at[span], sems.at[1 + index, part]
            )
            copy.start()
            outs.append(copy)
    left = lay[...].reshape(channels, rows, length).astype(BF16)
    low_out[...] = left[: channels // 2]
    high_out[...] = left[channels // 2 :]
    wait(outs)


def factor_kernel(parts, *refs):
    normed_parts = refs[:parts]
    live, weight, output_w, cotangent_any, factor_any, d_gated_any = refs[parts : parts + 6]
    cotangent, factors, d_gated, in_sem, sems = refs[parts + 6 :]
    rows, length, channels = cotangent.shape
    half = rows // parts
    arrivals = split_copies(cotangent_any, cotangent, in_sem, parts)
    start(arrivals)
    weight_t = weight[:, 2 * channels : 4 * channels].astype(F32).T.astype(BF16)
    departures = [
        split_copies(factors, factor_any, sems.at[0], parts),
        split_copies(d_gated, d_gated_any, sems.at[1], parts),
    ]
    for part in range(parts):
        arrivals[part].wait()

        def row(i, part=part):
            at = i + part * half
            projected = mmt(weight_t, normed_parts[part][i])
            back = mmt(cotangent[at], output_w[...])
            yield
            _, factors[at] = gate_factors(projected, live[pl.ds(at, 1), :], channels)
            d_gated[at] = back.astype(BF16)

        over_rows(half, 8, row)
        start([copies[part] for copies in departures])
    for copies in departures:
        wait(copies)


def product_kernel(count, *refs):
    blocks = refs[: 2 * count]
    lefts = refs[2 * count : 2 * count + 2]
    (pair_any, gate_any, gain2_col, gain3, output_w, bias_w) = refs[2 * count + 2 : 2 * count + 8]
    row_outs = refs[2 * count + 8 : 2 * count + 12]
    right_any, scale2_out, bias_out = refs[2 * count + 12 : 2 * count + 15]
    product, bias_scr, right_all, pair, gate = refs[2 * count + 15 : 2 * count + 20]
    kept = refs[2 * count + 20 : 2 * count + 24]
    normed2_out, update_out, middle_out, normed3_out = kept
    in_sems, out_sems, right_sem = refs[2 * count + 24 :]
    rows, length, channels = pair.shape
    heads = bias_w.shape[1]
    half = rows // 2
    place = lax.axis_index("dap")
    arrivals = [
        pltpu.make_async_copy(pair_any, pair, in_sems.at[0]),
        pltpu.make_async_copy(gate_any, gate, in_sems.at[1]),
    ]
    start(arrivals)
    starts = [
        pl.multiple_of((place ^ (index // 2)) * rows + (index % 2) * half, half)
        for index in range(2 * count)
    ]

    def channel(c, carry):
        for begin, ref in zip(starts, blocks):
            right_all[c, pl.ds(begin, half), :] = ref[c]
        return carry

    lax.fori_loop(0, channels, channel, 0, unroll=4)
    right_copy = pltpu.make_async_copy(right_all, right_any, right_sem)
    right_copy.start()

    for part, left in enumerate(lefts):

        def multiply(c, carry, left=left, first=part * (channels // 2)):
            product[pl.ds(first + c, rows, stride=channels), :] = mmt(
                left[c], right_all[first + c]
            )
            return carry

        lax.fori_loop(0, channels // 2, multiply, 0, unroll=8)
    eye = identity(channels)
    gain2 = jnp.broadcast_to(gain2_col[...], (channels, length))
    bias_t = jnp.concatenate(
        [bias_w[...].astype(F32).T, jnp.zeros((HEAD_ROWS - heads, channels), F32)], axis=0
    ).astype(BF16)

    def row(i):
        hat, scale = norm_parts(product[pl.ds(i * channels, channels), :], 0)
        yield
        normed2_t = (hat * gain2).astype(BF16)
        normed2_out[i] = normed2_t
        scale2_out[pl.ds(i, 1), :] = scale
        normed2 = mmt(eye, normed2_t).astype(BF16)
        yield
        update = mm(normed2, output_w[...])
        yield
        update_out[i] = update.astype(BF16)
        middle = (pair[i].astype(F32) + gate[i] * update).astype(BF16)
        middle_out[i] = middle
        hat3, _ = norm_parts(middle.astype(F32), -1)
        yield
        normed3 = (hat3 * gain3[...]).astype(BF16)
        normed3_out[i] = normed3
        bias_scr[pl.ds(i * HEAD_ROWS, HEAD_ROWS), :] = mmt(bias_t, normed3)

    wait(arrivals)
    parts = 4
    departures = [
        split_copies(source, target, out_sems.at[at], parts)
        for at, (source, target) in enumerate(zip(kept, row_outs))
    ]
    for part in range(parts):
        over_rows(rows // parts, W_PRODUCT, row, first=part * (rows // parts))
        start([copies[part] for copies in departures])
    for h in range(heads):
        head = bias_scr[pl.ds(h, rows, stride=HEAD_ROWS), :]
        bias_out[:, h * length : (h + 1) * length] = head.astype(BF16)
    for copies in departures:
        wait(copies)
    right_copy.wait()


def project_kernel(factor, normed3_any, weight_any, projected_any, query_any, gate_any, *scratch):
    normed3, weight, weight_t, weight_qg, projected3, queries, gates, sems, out_sems, weight_sem = (
        scratch
    )
    rows, length, channels = normed3.shape
    kept = projected3.shape[1]
    parts = 4
    copy = pltpu.make_async_copy(weight_any, weight, weight_sem)
    copy.start()
    arrivals = split_copies(normed3_any, normed3, sems, parts)
    start(arrivals)
    copy.wait()
    weight_t[...] = weight[:, :kept].astype(F32).T.astype(BF16)
    weight_qg[:, :channels] = weight[:, :channels]
    weight_qg[:, channels:] = weight[:, kept:]

    def row(i):
        normed = normed3[i]
        projected_t = mmt(weight_t[...], normed)
        projected = mm(normed, weight_qg[...])
        yield
        projected3[i, :channels] = (projected_t[:channels] * factor).astype(BF16)
        projected3[i, channels:] = projected_t[channels:].astype(BF16)
        queries[i] = (projected[:, :channels] * factor).astype(BF16)
        gates[i] = sigmoid(projected[:, channels:])

    departures = [
        split_copies(source, target, out_sems.at[at], parts)
        for at, (source, target) in enumerate(
            ((projected3, projected_any), (queries, query_any), (gates, gate_any))
        )
    ]
    for part in range(parts):
        arrivals[part].wait()
        over_rows(rows // parts, 8, row, first=part * (rows // parts))
        start([copies[part] for copies in departures])
    for copies in departures:
        wait(copies)


def attend_kernel(count, table, *refs):
    bias_refs = refs[:count]
    types_row, types_col, live, output_w = refs[count : count + 4]
    row_arrays = refs[count + 4 : count + 10]
    (pair_out_any, d_projected, d_output, d_table) = refs[count + 10 : count + 14]
    d_bias_outs = refs[count + 14 : 2 * count + 14]
    bias, d_bias, head_mask = refs[2 * count + 14 : 2 * count + 17]
    fetched = refs[2 * count + 17 : 2 * count + 23]
    projected, queries, gates, d_gateds, cotangent, middle = fetched
    pair_out, in_sems, out_sems = refs[2 * count + 23 :]
    rows, length, channels = middle.shape
    types = table.shape[1]
    heads = table.shape[0] // types
    size = channels // heads
    own = bias_refs[0].shape[0]
    factor = size ** -0.5
    place = lax.axis_index("dap")
    parts = rows // W_ATTEND
    arrivals = [
        split_copies(source, target, in_sems.at[at], parts)
        for at, (source, target) in enumerate(zip(row_arrays, fetched))
    ]
    for part in range(parts):
        start([copies[part] for copies in arrivals])

    def spans(h):
        return slice(h * length, (h + 1) * length)

    for offset in range(count):
        begin = pl.multiple_of((place ^ offset) * own, own)
        bias[pl.ds(begin, own), :] = bias_refs[offset][...].astype(F32)
    row_types = types_row[...]
    col_types = types_col[...]
    for h in range(heads):
        total = jnp.zeros((length, length), F32)
        for a in range(types):
            values = jnp.zeros((1, length), F32)
            for b in range(types):
                values = jnp.where(row_types == b, table[h * types + a, b], values)
            total = jnp.where(col_types == a, values, total)
        bias[:, spans(h)] = bias[:, spans(h)] + total
    d_bias[...] = jnp.zeros_like(d_bias)
    d_output[...] = jnp.zeros_like(d_output)
    lines = lax.broadcasted_iota(jnp.int32, head_mask.shape, 0) // size
    columns = lax.broadcasted_iota(jnp.int32, head_mask.shape, 1) // length
    head_mask[...] = (lines == columns).astype(F32).astype(BF16)

    eye = identity(channels)

    def row(i):
        live_row = live[pl.ds(i, 1), :]
        live_wide = jnp.concatenate([live_row.astype(BF16)] * heads, axis=1)
        query_t = projected[i, :channels]
        key_t = projected[i, channels : 2 * channels]
        value_t = projected[i, 2 * channels :]
        gate = gates[i]
        d_gated = d_gateds[i].astype(F32)
        mask = head_mask[...]
        ones = mask * live_wide
        keys = jnp.concatenate([key_t] * heads, axis=1) * mask
        values = jnp.concatenate(
            [jnp.concatenate([value_t] * heads, axis=1) * ones, ones], axis=0
        )
        score = mm(queries[i], keys)
        yield
        expo = jnp.exp(score + bias[...])
        expo_b = expo.astype(BF16)
        sums = mmt(expo_b, values)
        yield
        total = sums[:, channels:]
        inverse = 1.0 / jnp.maximum(total, 1.0)
        attended = sums[:, :channels] * inverse
        gated = (gate * attended).astype(BF16)
        d_attended = d_gated * gate * inverse
        d_gate = d_gated * attended * gate * (1.0 - gate)
        slope = jnp.where(total > 1.0, 1.0, jnp.where(total == 1.0, 0.5, 0.0))
        d_attended_b = d_attended.astype(BF16)
        both = jnp.concatenate(
            [d_attended_b, (-d_attended * attended * slope).astype(BF16)], axis=1
        )
        d_expo = mm(both, values)
        turned = mmt(
            eye, jnp.concatenate([d_attended_b, d_gate.astype(BF16), gated], axis=0)
        ).astype(BF16)
        yield
        update = mm(gated, output_w[...])
        d_score = expo * d_expo
        d_score_b = d_score.astype(BF16)
        d_query_t = mmt(keys, d_score_b) * factor
        d_key_t = mm(query_t, d_score_b)
        d_value_t = mm(turned[:, :length], expo_b)
        yield
        pair_out[i] = (middle[i].astype(F32) + update).astype(BF16)

        def diagonal(full):
            return jnp.concatenate(
                [full[h * size : (h + 1) * size, spans(h)] for h in range(heads)], axis=0
            )

        d_projected[i, :channels] = d_query_t.astype(BF16)
        d_projected[i, channels : 2 * channels] = diagonal(d_key_t).astype(BF16)
        d_projected[i, 2 * channels : 3 * channels] = (diagonal(d_value_t) * live_row).astype(BF16)
        d_projected[i, 3 * channels :] = turned[:, length : 2 * length]
        return turned[:, 2 * length :], cotangent[i], d_score

    def finish(results):
        gated_t, cots, d_scores = zip(*results)
        d_output[...] += mm(jnp.concatenate(gated_t, axis=1), jnp.concatenate(cots, axis=0))
        d_bias[...] += sum(d_scores)

    departures = split_copies(pair_out, pair_out_any, out_sems, parts)
    for part in range(parts):
        wait([copies[part] for copies in arrivals])
        over_rows(rows // parts, W_ATTEND, row, finish, first=part * (rows // parts))
        departures[part].start()

    for offset in range(count):
        begin = pl.multiple_of((place ^ offset) * own, own)
        ref = d_bias_outs[offset]
        ref[...] = d_bias[pl.ds(begin, own), :].astype(ref.dtype)
    high = d_bias[...].astype(BF16)
    low = (d_bias[...] - high.astype(F32)).astype(BF16)
    kinds = lax.broadcasted_iota(jnp.int32, (HEAD_ROWS, length), 0)
    picks = (types_row[...] == kinds).astype(F32).astype(BF16)
    by_row = mm(picks, high) + mm(picks, low)
    lanes = lax.broadcasted_iota(jnp.int32, (HEAD_ROWS, channels), 1)
    grad = jnp.zeros((HEAD_ROWS, channels), F32)
    for h in range(heads):
        part = by_row[:, spans(h)]
        for b in range(types):
            one = jnp.sum(jnp.where(types_row[...] == b, part, 0.0), axis=1, keepdims=True)
            grad = jnp.where(lanes == h * types + b, one, grad)
    d_table[...] = grad
    wait(departures)


def projection_kernel(d_projected, normed3, input_w, d_output, d_table, d_normed, packed, total):
    block = normed3.shape[0]
    wide, length = d_projected.shape[1:]
    channels = normed3.shape[2]
    step = pl.program_id(0)

    @pl.when(step == 0)
    def _():
        total[...] = jnp.zeros_like(total)

    def rows(index, carry):
        at = [4 * index + one for one in range(4)]
        both = jnp.concatenate([d_projected[one] for one in at], axis=1)
        total[...] += mm(both, jnp.concatenate([normed3[one] for one in at], axis=0))
        d_both = mm(input_w[...], both)
        for order, one in enumerate(at):
            d_normed[one] = d_both[:, order * length : (order + 1) * length]
        return carry

    lax.fori_loop(0, block // 4, rows, 0, unroll=2)

    @pl.when(step == pl.num_programs(0) - 1)
    def _():
        packed[:wide] = total[...].astype(BF16)
        packed[wide : wide + channels] = d_output[...].astype(BF16)
        high = d_table[...].astype(BF16)
        packed[wide + channels : wide + channels + HEAD_ROWS] = high
        packed[wide + channels + HEAD_ROWS :] = (d_table[...] - high.astype(F32)).astype(BF16)


def middle_kernel(count, *refs):
    arrived = refs[:count]
    (d_normed3, normed3, middle, cotangent, gain3_col, bias_w) = refs[count : count + 6]
    (normed2, scale2, update, gate, gain2_col, output_w) = refs[count + 6 : count + 12]
    (d_middle_any, d_gate_any, d_product_any, grad_out) = refs[count + 12 : count + 16]
    send_any = refs[count + 16 : 2 * count + 16]
    d_bias, lay, d_middle_out, d_gate_out, d_product_out = refs[2 * count + 16 : 2 * count + 21]
    send_outs = refs[2 * count + 21 : 3 * count + 21]
    row_sems, product_sems, send_sems = refs[3 * count + 21 :]
    rows, length, channels = middle.shape
    heads = bias_w.shape[1]
    place = lax.axis_index("dap")
    eye = identity(channels)
    total = arrived[0][...]
    for ref in arrived[1:]:
        total = total + ref[...].astype(F32)
    d_bias[...] = jnp.zeros_like(d_bias)
    for h in range(heads):
        d_bias[pl.ds(h, rows, stride=HEAD_ROWS), :] = total[:, h * length : (h + 1) * length]
    bias_wide = jnp.concatenate(
        [bias_w[...].astype(F32), jnp.zeros((channels, HEAD_ROWS - heads), F32)], axis=1
    ).astype(BF16)
    gain3 = jnp.broadcast_to(gain3_col[...], (channels, length))
    gain2 = jnp.broadcast_to(gain2_col[...], (channels, length))
    inverse2 = 1.0 / gain2
    grad_out[...] = jnp.zeros_like(grad_out)

    def row(i):
        bias_rows = d_bias[pl.ds(i * HEAD_ROWS, HEAD_ROWS), :].astype(BF16)
        d_normed = d_normed3[i] + mm(bias_wide, bias_rows)
        hat3, scale3 = norm_parts(mmt(eye, middle[i]), 0)
        yield
        d_mid_t = norm_back(d_normed * gain3, hat3, scale3, 0).astype(BF16)
        d_mid_b = mmt(eye, d_mid_t)
        yield
        d_mid = (cotangent[i].astype(F32) + d_mid_b).astype(BF16)
        d_middle_out[i] = d_mid
        gates = gate[i]
        d_mid = d_mid.astype(F32)
        d_up = d_mid * gates
        d_gate_out[i] = (d_up * update[i].astype(F32) * (1.0 - gates)).astype(BF16)
        d_up = d_up.astype(BF16)
        normed2_t = normed2[i]
        d_hat2 = mmt(output_w[...], d_up)
        yield
        hat2 = normed2_t.astype(F32) * inverse2
        lay[pl.ds(i, channels, stride=rows), :] = norm_back(
            d_hat2 * gain2, hat2, scale2[pl.ds(i, 1), :], 0
        )
        return normed2_t, d_up, bias_rows, normed3[i]

    def finish(results):
        normed2_t, d_up, bias_rows, normed = zip(*results)
        grad_out[:channels] += mm(
            jnp.concatenate(normed2_t, axis=1), jnp.concatenate(d_up, axis=0)
        )
        grad_out[channels:] += mm(
            jnp.concatenate(bias_rows, axis=1), jnp.concatenate(normed, axis=0)
        )

    over_rows(rows, W_MIDDLE, row, finish)
    departures = [
        pltpu.make_async_copy(d_middle_out, d_middle_any, row_sems.at[0]),
        pltpu.make_async_copy(d_gate_out, d_gate_any, row_sems.at[1]),
    ]
    start(departures)
    line = lax.broadcasted_iota(jnp.int32, (length, length), 0)
    source = ((line // rows) ^ place) * rows + line % rows
    shuffled = (
        (source == lax.broadcasted_iota(jnp.int32, (length, length), 1)).astype(F32).astype(BF16)
    )

    def group(g, carry):
        block = lay[pl.ds(g * length, length), :].astype(BF16)
        d_product_out[pl.ds(g * length, length), :] = block
        turned = mmt(shuffled, block).astype(BF16)
        for offset in range(count):
            send_outs[offset][g] = turned[offset * rows : (offset + 1) * rows]
        return carry

    parts = 4
    copies = [split_copies(d_product_out, d_product_any, product_sems, parts)] + [
        split_copies(source, target, send_sems.at[at], parts)
        for at, (source, target) in enumerate(zip(send_outs, send_any))
    ]
    share = channels * rows // length // parts
    for part in range(parts):
        lax.fori_loop(part * share, (part + 1) * share, group, 0, unroll=4)
        start([one[part] for one in copies])
    for one in copies:
        wait(one)
    wait(departures)


def gate_back(factors, d_out):
    channels = d_out.shape[0]
    d_value = d_out * factors[:channels].astype(F32)
    d_pre = d_out * factors[channels:].astype(F32)
    return jnp.concatenate([d_value.astype(BF16), d_pre.astype(BF16)], axis=0)


def left_back_kernel(
    right_any, d_product_any, normed1_any, factors_any, d_gate_any, grad_middle, *refs
):
    d_projected_any, packed, lay, grad, d_projected_out, sems = refs[:6]
    right_all, d_product, normed1, factors, d_gate, right_sems, product_sems, in_sems = refs[6:]
    rows, length, channels = normed1.shape
    parts = 4
    first_arrivals = [
        split_copies(right_any, right_all, right_sems, parts),
        split_copies(d_product_any, d_product, product_sems, parts),
    ]
    for part in range(parts):
        start([copies[part] for copies in first_arrivals])
    arrivals = [
        pltpu.make_async_copy(normed1_any, normed1, in_sems.at[0]),
        pltpu.make_async_copy(factors_any, factors, in_sems.at[1]),
        pltpu.make_async_copy(d_gate_any, d_gate, in_sems.at[2]),
    ]
    start(arrivals)

    def channel(c, carry):
        lay[pl.ds(c, rows, stride=channels), :] = mm(
            d_product[pl.ds(c * rows, rows), :], right_all[c]
        )
        return carry

    share = channels // parts
    for part in range(parts):
        wait([copies[part] for copies in first_arrivals])
        lax.fori_loop(part * share, (part + 1) * share, channel, 0, unroll=8)
    wait(arrivals)
    eye = identity(channels)
    grad[...] = jnp.zeros_like(grad)

    def row(i):
        normed = normed1[i]
        d_gate_t = mmt(eye, d_gate[i]).astype(BF16)
        d_projected = gate_back(factors[i], lay[pl.ds(i * channels, channels), :])
        yield
        d_projected = jnp.concatenate([d_projected, d_gate_t], axis=0)
        d_projected_out[i] = d_projected
        return d_projected, normed

    def finish(results):
        d_projected, normed = zip(*results)
        grad[...] += mm(jnp.concatenate(d_projected, axis=1), jnp.concatenate(normed, axis=0))

    parts = 4
    departures = split_copies(d_projected_out, d_projected_any, sems, parts)
    for part in range(parts):
        over_rows(rows // parts, 8, row, finish, first=part * (rows // parts))
        departures[part].start()
    packed[: 3 * channels] = grad[...].astype(BF16)
    packed[3 * channels :] = grad_middle[...].astype(BF16)
    wait(departures)


def right_back_kernel(count, *refs):
    arrived = refs[:count]
    left_halves = refs[count : 2 * count], refs[2 * count : 3 * count]
    refs = refs[count:]
    normed1_any, factors_any, packed_a, packed_b = refs[2 * count : 2 * count + 4]
    d_projected_any = refs[2 * count + 4]
    sends = refs[2 * count + 5 : 3 * count + 5]
    lay, grad, packed, d_projected_out, sems, normed1, factors, in_sems = refs[3 * count + 5 :]
    rows, length, channels = normed1.shape
    arrivals = [
        pltpu.make_async_copy(normed1_any, normed1, in_sems.at[0]),
        pltpu.make_async_copy(factors_any, factors, in_sems.at[1]),
    ]
    start(arrivals)
    per = length // rows
    same = (
        lax.broadcasted_iota(jnp.int32, (length, length), 0) // rows
        == lax.broadcasted_iota(jnp.int32, (length, length), 1) // rows
    )
    mask = same.astype(F32).astype(BF16)

    half = channels // per // 2
    for part, left_blocks in enumerate(left_halves):

        def group(g, carry, left_blocks=left_blocks, first=part * half):
            at = first + g
            spread = jnp.concatenate(
                [jnp.concatenate([ref[at]] * per, axis=0) * mask for ref in arrived], axis=1
            )
            lefts = jnp.concatenate(
                [ref[pl.ds(g * per, per)].reshape(length, length) for ref in left_blocks], axis=0
            )
            lay[pl.ds(at * length, length), :] = mm(spread, lefts)
            return carry

        lax.fori_loop(0, half, group, 0, unroll=4)
    wait(arrivals)
    grad[...] = jnp.zeros_like(grad)

    def row(i):
        normed = normed1[i]
        d_projected = gate_back(factors[i], lay[pl.ds(i, channels, stride=rows), :])
        yield
        d_projected_out[i] = d_projected
        return d_projected, normed

    def finish(results):
        d_projected, normed = zip(*results)
        grad[...] += mm(jnp.concatenate(d_projected, axis=1), jnp.concatenate(normed, axis=0))

    parts = 4
    departures = split_copies(d_projected_out, d_projected_any, sems, parts)
    for part in range(parts):
        over_rows(rows // parts, 8, row, finish, first=part * (rows // parts))
        departures[part].start()
    first, second = packed_a.shape[0], packed_b.shape[0]
    packed[:first] = packed_a[...]
    packed[first : first + second] = packed_b[...]
    packed[first + second : first + second + 2 * channels] = grad[...].astype(BF16)
    packed[first + second + 2 * channels :] = jnp.zeros_like(
        packed[first + second + 2 * channels :]
    )
    size = sends[0].shape[0]
    for offset in range(count):
        begin = pl.multiple_of((lax.axis_index("dap") ^ offset) * size, HEAD_ROWS)
        sends[offset][...] = packed[pl.ds(begin, size), :]
    wait(departures)


def input_back_kernel(part, parts, *refs):
    sources = refs[:4]
    gain_col, input_w, gating = refs[4:7]
    pair_grad_any = refs[-8]
    d_left, d_right, pair, d_middle, pair_grad, sems, out_sem = refs[-7:]
    rows, length, channels = pair.shape
    span = pl.ds(part * rows, rows)
    arrivals = [
        pltpu.make_async_copy(source.at[span], target, sems.at[at])
        for at, (source, target) in enumerate(zip(sources, (d_left, d_right, pair, d_middle)))
    ]
    start(arrivals)
    eye = identity(channels)
    weight = jnp.concatenate(
        [input_w[:, : 2 * channels], gating[...], input_w[:, 2 * channels :]], axis=1
    )
    gain = jnp.broadcast_to(gain_col[...], (channels, length))

    def row(i):
        hat, scale = norm_parts(mmt(eye, pair[i]), 0)
        d_normed = mm(weight, jnp.concatenate([d_left[i], d_right[i]], axis=0))
        yield
        d_pair = mmt(eye, norm_back(d_normed * gain, hat, scale, 0).astype(BF16))
        yield
        pair_grad[i] = (d_middle[i].astype(F32) + d_pair).astype(BF16)

    wait(arrivals)
    over_rows(rows, 8, row)
    departure = pltpu.make_async_copy(pair_grad, pair_grad_any.at[span], out_sem)
    departure.start()
    departure.wait()


def finish_kernel(count, factor, *refs):
    blocks = refs[:count]
    (input1, gating, output1, bias_w, input3, gain1, gain2, gain3) = refs[count : count + 8]
    (
        gain1_out,
        input1_out,
        gating_out,
        gain2_out,
        output1_out,
        gain3_out,
        bias_out,
        input3_out,
        output3_out,
        table_out,
        packed,
    ) = refs[count + 8 :]
    channels = gating.shape[0]
    heads, types = table_out.shape[:2]
    size = blocks[0].shape[0]
    for offset in range(count):
        begin = pl.multiple_of((lax.axis_index("dap") ^ offset) * size, HEAD_ROWS)
        packed[pl.ds(begin, size), :] = blocks[offset][...].astype(F32) * factor
    at = 0

    def take(rows):
        nonlocal at
        at += rows
        return packed[at - rows : at, :]

    input3_t, output3 = take(4 * channels), take(channels)
    table = take(HEAD_ROWS) + take(HEAD_ROWS)
    left_t, gating_t, output1_grad = take(2 * channels), take(channels), take(channels)
    bias_t, right_t = take(HEAD_ROWS), take(2 * channels)
    input1_t = jnp.concatenate([left_t, right_t], axis=0)

    def dots(weight, grad_t):
        return jnp.sum(weight[...].astype(F32).T * grad_t, axis=0, keepdims=True)

    gain1_out[...] = (dots(input1, input1_t) + dots(gating, gating_t)) / gain1[...]
    output_t = (output1[...].astype(F32) * output1_grad).T
    gain2_out[...] = jnp.sum(output_t, axis=0, keepdims=True) / gain2[...]
    gain3_out[...] = (dots(input3, input3_t) + dots(bias_w, bias_t[:heads])) / gain3[...]
    input1_out[...] = input1_t.T
    gating_out[...] = gating_t.T
    output1_out[...] = output1_grad
    bias_out[...] = bias_t.T[:, :heads]
    input3_out[...] = input3_t.T
    output3_out[...] = output3
    for h in range(heads):
        table_out[h] = table[:types, h * types : (h + 1) * types]


def swap(value, axis, step):
    count = lax.axis_size(axis)
    return lax.ppermute(value, axis, [(index, index ^ step) for index in range(count)])


def gather_blocks(block, axis):
    return gather_near(block, swap(block, axis, lax.axis_size(axis) // 2), axis)


def gather_near(block, far, axis):
    half = lax.axis_size(axis) // 2
    blocks = {0: block, half: far}
    for bit in reversed(range(half.bit_length() - 1)):
        step = 1 << bit
        for offset, held in list(blocks.items()):
            blocks[offset ^ step] = swap(held, axis, step)
    return [blocks[offset] for offset in range(len(blocks))]


def sum_over(value, axis):
    step = 1
    while step < lax.axis_size(axis):
        value = value + swap(value, axis, step)
        step *= 2
    return value


def per_device(
    pair_rep,
    cotangent,
    tok_mask,
    tok_types,
    pair_mask,
    triangle_gain,
    triangle_input,
    triangle_gating,
    product_gain,
    triangle_output,
    attend_gain,
    attend_bias,
    attend_input,
    attend_output,
    type_table,
):
    slab = pair_rep[0]
    cot = cotangent[0]
    rows, length, channels = slab.shape
    heads, types = type_table.shape[:2]
    count = lax.axis_size("dap")
    gain1_row, gain3_row = triangle_gain[None, :], attend_gain[None, :]
    gain1_col, gain2_col, gain3_col = (
        triangle_gain[:, None],
        product_gain[:, None],
        attend_gain[:, None],
    )
    vmem = pl.BlockSpec(memory_space=pltpu.VMEM)
    anywhere = pl.BlockSpec(memory_space=pltpu.HBM)
    smem = pl.BlockSpec(memory_space=pltpu.SMEM)
    cell_buffer = pltpu.VMEM((rows, length, channels), BF16)
    cells = (rows, length, channels)
    turned = (rows, channels, length)

    half = rows // 2
    normed1_halves, right_halves, live_halves = [], [], []
    for part in range(2):
        normed_part, right_part, live_part = call(
            partial(right_kernel, part),
            [
                ((half, length, channels), BF16),
                ((channels, half, length), BF16),
                ((half, length), F32),
            ],
            [slab, pair_mask[0], tok_mask, gain1_row, triangle_input],
            in_specs=[anywhere] * 5,
            scratch=[
                pltpu.VMEM((half, length, channels), BF16),
                pltpu.VMEM((half, length), jnp.int32),
                pltpu.VMEM((1, length), jnp.int32),
                pltpu.VMEM((1, channels), F32),
                pltpu.VMEM((channels, 4 * channels), BF16),
                pltpu.VMEM((2 * channels, channels), BF16),
                pltpu.VMEM((channels * half, length), F32),
                pltpu.SemaphoreType.DMA((5,)),
            ],
            us=3.0,
            name="right_projection",
        )
        normed1_halves.append(normed_part)
        right_halves.append(right_part)
        live_halves.append(live_part)
    normed1, left_low, left_high, gate, live, left_factors = call(
        partial(left_kernel, 2),
        [
            (cells, BF16),
            ((channels // 2, rows, length), BF16),
            ((channels // 2, rows, length), BF16),
            (cells, F32),
            ((rows, length), F32),
            ((rows, 2 * channels, length), BF16),
        ],
        [*normed1_halves, *live_halves, triangle_input, triangle_gating],
        out_specs=[anywhere, vmem, vmem, anywhere, vmem, anywhere],
        scratch=[
            pltpu.VMEM((2 * channels, channels), BF16),
            pltpu.VMEM((channels * rows, length), F32),
            pltpu.VMEM(cells, F32),
            pltpu.VMEM((rows, 2 * channels, length), BF16),
            pltpu.SemaphoreType.DMA((3, 2)),
        ],
        us=6.0,
        name="left_projection",
    )
    far = [swap(part, "dap", count // 2) for part in right_halves]
    live, far[0] = lax.optimization_barrier((live, far[0]))
    right_factors, d_gated = call(
        partial(factor_kernel, 2),
        [((rows, 2 * channels, length), BF16), (cells, BF16)],
        [*normed1_halves, live, triangle_input, attend_output, cot],
        in_specs=[vmem] * 5 + [anywhere],
        out_specs=[anywhere] * 2,
        scratch=[
            cell_buffer,
            pltpu.VMEM((rows, 2 * channels, length), BF16),
            cell_buffer,
            pltpu.SemaphoreType.DMA((2,)),
            pltpu.SemaphoreType.DMA((2, 2)),
        ],
        us=5.0,
        name="right_factors",
    )
    right_factors, far[1] = lax.optimization_barrier((right_factors, far[1]))
    left_low_sent, _ = lax.optimization_barrier((left_low, far[1]))
    low_far = swap(left_low_sent, "dap", count // 2)
    right_halves = [
        gather_near(part, other, "dap") for part, other in zip(right_halves, far)
    ]
    right_blocks = [right_halves[index % 2][index // 2] for index in range(2 * count)]
    normed2, update, middle, normed3, right_all, scale2, bias_rows = call(
        partial(product_kernel, count),
        [
            (turned, BF16),
            (cells, BF16),
            (cells, BF16),
            (cells, BF16),
            ((channels, length, length), BF16),
            ((rows, length), F32),
            ((rows, heads * length), BF16),
        ],
        [*right_blocks, left_low, left_high, slab, gate, gain2_col, gain3_row, triangle_output, attend_bias],
        in_specs=[vmem] * (2 * count + 2) + [anywhere] * 2 + [vmem] * 4,
        out_specs=[anywhere] * 5 + [vmem] * 2,
        scratch=[
            pltpu.VMEM((rows * channels, length), F32),
            pltpu.VMEM((rows * HEAD_ROWS, length), F32),
            pltpu.VMEM((channels, length, length), BF16),
        ]
        + [cell_buffer, pltpu.VMEM(cells, F32)]
        + [pltpu.VMEM(turned, BF16)]
        + [cell_buffer] * 3
        + [
            pltpu.SemaphoreType.DMA((2,)),
            pltpu.SemaphoreType.DMA((4, 4)),
            pltpu.SemaphoreType.DMA,
        ],
        us=14.0,
        name="product_and_norms",
    )
    normed3, low_far = lax.optimization_barrier((normed3, low_far))
    bias_far = swap(bias_rows, "dap", count // 2)

    block = 8
    steps = rows // block
    by_row = pl.BlockSpec((block, length, channels), lambda step: (step, 0, 0))
    by_row_wide = pl.BlockSpec((block, 4 * channels, length), lambda step: (step, 0, 0))

    def fixed(*shape):
        return pl.BlockSpec(shape, lambda step: (0,) * len(shape))

    projected3, query, gate3 = call(
        partial(project_kernel, (channels // heads) ** -0.5),
        [((rows, 3 * channels, length), BF16), (cells, BF16), (cells, F32)],
        [normed3, attend_input],
        in_specs=[anywhere] * 2,
        scratch=[
            cell_buffer,
            pltpu.VMEM((channels, 4 * channels), BF16),
            pltpu.VMEM((3 * channels, channels), BF16),
            pltpu.VMEM((channels, 2 * channels), BF16),
            pltpu.VMEM((rows, 3 * channels, length), BF16),
            cell_buffer,
            pltpu.VMEM(cells, F32),
            pltpu.SemaphoreType.DMA((4,)),
            pltpu.SemaphoreType.DMA((3, 4)),
            pltpu.SemaphoreType.DMA,
        ],
        out_specs=[anywhere] * 3,
        us=5.0,
        name="attention_projections",
    )
    projected3, bias_far = lax.optimization_barrier((projected3, bias_far))
    bias_blocks = gather_near(bias_rows, bias_far, "dap")
    left_high_sent, _ = lax.optimization_barrier((left_high, bias_far))
    high_far = swap(left_high_sent, "dap", count // 2)
    attend_outs = call(
        partial(attend_kernel, count),
        [
            (cells, BF16),
            ((rows, 4 * channels, length), BF16),
            ((channels, channels), F32),
            ((HEAD_ROWS, channels), F32),
            ((rows, heads * length), F32),
        ]
        + [((rows, heads * length), BF16)] * (count - 1),
        [type_table.reshape(heads * types, types), *bias_blocks]
        + [tok_types, tok_types.reshape(length, 1), live, attend_output]
        + [projected3, query, gate3, d_gated, cot, middle],
        in_specs=[smem] + [vmem] * (count + 4) + [anywhere] * 6,
        out_specs=[anywhere] + [vmem] * (count + 3),
        scratch=[
            pltpu.VMEM((length, heads * length), F32),
            pltpu.VMEM((length, heads * length), F32),
            pltpu.VMEM((channels, heads * length), BF16),
        ]
        + [pltpu.VMEM((rows, 3 * channels, length), BF16), cell_buffer, pltpu.VMEM(cells, F32)]
        + [cell_buffer] * 4
        + [
            pltpu.SemaphoreType.DMA((6, rows // W_ATTEND)),
            pltpu.SemaphoreType.DMA((rows // W_ATTEND,)),
        ],
        us=20.0,
        name="attention",
    )
    pair_out, d_projected3, d_output, d_table = attend_outs[:4]
    d_table, high_far = lax.optimization_barrier((d_table, high_far))
    d_bias_parts = [attend_outs[4]] + [
        swap(attend_outs[4 + offset], "dap", offset) for offset in range(1, count)
    ]
    d_normed3, packed_a = call(
        projection_kernel,
        [(turned, F32), ((4 * channels + channels + 2 * HEAD_ROWS, channels), BF16)],
        [d_projected3, normed3, attend_input, d_output, d_table],
        grid=(steps,),
        in_specs=[by_row_wide, by_row, fixed(channels, 4 * channels)]
        + [fixed(channels, channels), fixed(HEAD_ROWS, channels)],
        out_specs=[
            pl.BlockSpec((block, channels, length), lambda step: (step, 0, 0)),
            fixed(5 * channels + 2 * HEAD_ROWS, channels),
        ],
        scratch=[pltpu.VMEM((4 * channels, channels), F32)],
        us=6.0,
        name="projection_back",
    )
    groups = channels * rows // length
    middle_outs = call(
        partial(middle_kernel, count),
        [
            (cells, BF16),
            (cells, BF16),
            ((channels * rows, length), BF16),
            ((channels + HEAD_ROWS, channels), F32),
        ]
        + [((groups, rows, length), BF16)] * count,
        [*d_bias_parts, d_normed3, normed3, middle, cot, gain3_col, attend_bias]
        + [normed2, scale2, update, gate, gain2_col, triangle_output],
        out_specs=[anywhere] * 3 + [vmem] + [anywhere] * count,
        scratch=[
            pltpu.VMEM((rows * HEAD_ROWS, length), F32),
            pltpu.VMEM((channels * rows, length), F32),
            cell_buffer,
            cell_buffer,
            pltpu.VMEM((channels * rows, length), BF16),
        ]
        + [pltpu.VMEM((groups, rows, length), BF16)] * count
        + [
            pltpu.SemaphoreType.DMA((2,)),
            pltpu.SemaphoreType.DMA((4,)),
            pltpu.SemaphoreType.DMA((count, 4)),
        ],
        us=12.0,
        name="middle_back",
    )
    d_middle, d_gate, d_product, grad_middle = middle_outs[:4]
    d_middle, low_far, high_far = lax.optimization_barrier((d_middle, low_far, high_far))
    left_blocks = gather_near(left_low, low_far, "dap") + gather_near(left_high, high_far, "dap")
    product_parts = [middle_outs[4]] + [
        swap(middle_outs[4 + offset], "dap", offset) for offset in range(1, count)
    ]
    d_left, packed_b = call(
        left_back_kernel,
        [((rows, 3 * channels, length), BF16), ((4 * channels + HEAD_ROWS, channels), BF16)],
        [right_all, d_product, normed1, left_factors, d_gate, grad_middle],
        scratch=[
            pltpu.VMEM((rows * channels, length), F32),
            pltpu.VMEM((3 * channels, channels), F32),
            pltpu.VMEM((rows, 3 * channels, length), BF16),
            pltpu.SemaphoreType.DMA((4,)),
            pltpu.VMEM((channels, length, length), BF16),
            pltpu.VMEM((channels * rows, length), BF16),
            cell_buffer,
            pltpu.VMEM((rows, 2 * channels, length), BF16),
            cell_buffer,
            pltpu.SemaphoreType.DMA((4,)),
            pltpu.SemaphoreType.DMA((4,)),
            pltpu.SemaphoreType.DMA((3,)),
        ],
        in_specs=[anywhere] * 5 + [vmem],
        out_specs=[anywhere, vmem],
        us=10.0,
        name="left_back",
    )
    used = packed_a.shape[0] + packed_b.shape[0] + 2 * channels
    share = -(-used // (count * HEAD_ROWS)) * HEAD_ROWS
    right_outs = call(
        partial(right_back_kernel, count),
        [((rows, 2 * channels, length), BF16)] + [((share, channels), BF16)] * count,
        [*product_parts, *left_blocks, normed1, right_factors, packed_a, packed_b],
        in_specs=[vmem] * (3 * count) + [anywhere] * 2 + [vmem] * 2,
        out_specs=[anywhere] + [vmem] * count,
        scratch=[
            pltpu.VMEM((channels * rows, length), F32),
            pltpu.VMEM((2 * channels, channels), F32),
            pltpu.VMEM((share * count, channels), BF16),
            pltpu.VMEM((rows, 2 * channels, length), BF16),
            pltpu.SemaphoreType.DMA((4,)),
            cell_buffer,
            pltpu.VMEM((rows, 2 * channels, length), BF16),
            pltpu.SemaphoreType.DMA((2,)),
        ],
        us=7.0,
        name="right_back",
    )
    d_right = right_outs[0]
    parts = 4
    some = (rows // parts, length, channels)
    pair_grad = None

    def input_back(part, pair_grad):
        given = [] if pair_grad is None else [pair_grad]
        (pair_grad,) = call(
            partial(input_back_kernel, part, parts),
            [(cells, BF16)],
            [d_left, d_right, slab, d_middle, gain1_col, triangle_input, triangle_gating, *given],
            in_specs=[anywhere] * 4 + [vmem] * 3 + [anywhere] * len(given),
            out_specs=[anywhere],
            scratch=[
                pltpu.VMEM((rows // parts, 3 * channels, length), BF16),
                pltpu.VMEM((rows // parts, 2 * channels, length), BF16),
                pltpu.VMEM(some, BF16),
                pltpu.VMEM(some, BF16),
                pltpu.VMEM(some, BF16),
                pltpu.SemaphoreType.DMA((4,)),
                pltpu.SemaphoreType.DMA,
            ],
            aliases={7: 0} if given else None,
            us=3.0,
            name="input_back",
        )
        return pair_grad

    grad_share = right_outs[1].astype(F32)
    for offset in range(1, count):
        grad_share = grad_share + swap(right_outs[1 + offset], "dap", offset).astype(F32)
    grad_share = grad_share.astype(BF16)
    done = 0
    step = 1
    while step < lax.axis_size("dp"):
        if done < parts - 1:
            pair_grad = input_back(done, pair_grad)
            grad_share, pair_grad = lax.optimization_barrier((grad_share, pair_grad))
            done += 1
        grad_share = grad_share + swap(grad_share, "dp", step)
        step *= 2
    grad_blocks = [grad_share] + [
        swap(grad_share, "dap", offset) for offset in range(1, count)
    ]
    while done < parts:
        pair_grad = input_back(done, pair_grad)
        done += 1
    pair_grad, *grad_blocks = lax.optimization_barrier((pair_grad, *grad_blocks))
    weights = (triangle_input, triangle_gating, triangle_output, attend_bias, attend_input)
    gains = (gain1_row, product_gain[None, :], gain3_row)
    grads = call(
        partial(finish_kernel, count, (length * length * lax.axis_size("dp")) ** (-0.5)),
        [
            ((1, channels), F32),
            (triangle_input.shape, F32),
            (triangle_gating.shape, F32),
            ((1, channels), F32),
            (triangle_output.shape, F32),
            ((1, channels), F32),
            (attend_bias.shape, F32),
            (attend_input.shape, F32),
            (attend_output.shape, F32),
            (type_table.shape, F32),
        ],
        [*grad_blocks, *weights, *gains],
        scratch=[pltpu.VMEM((share * count, channels), F32)],
        us=3.0,
        name="scale_gradients",
    )
    grads = [grad[0] if grad.shape[0] == 1 else grad for grad in grads]
    return (pair_out[None], pair_grad[None], *grads)


def solution(mesh):
    return jax.shard_map(
        per_device,
        mesh=mesh,
        in_specs=(
            P("dp", "dap", None, None),
            P("dp", "dap", None, None),
            P("dp", None),
            P("dp", None),
            P("dp", "dap", None),
        )
        + (P(),) * 10,
        out_specs=(
            P("dp", "dap", None, None),
            P("dp", "dap", None, None),
        )
        + (P(),) * 10,
        check_vma=False,
    )
```

time: 166 us -> 134 us (0.81)
  local copies, waits for them, and re-layouts: 29.1 us -> 1.35 us
  waiting for transfers between devices: 34.7 us -> 23.5 us
  Pallas kernels: 76.5 us -> 84.7 us
    unnamed x102 -> x48, local copies, waits for them, and re-layouts: 28.5 us -> 0.9 us
    ppermute x27 -> x30, waiting for transfers between devices: 34.7 us -> 23.5 us  [swap(): lax.ppermute(value, axis, [(index, index ^ step) for index in range(count)])]
    pallas_call x11 -> x16, Pallas kernels: 76.5 us -> 84.7 us  [call(): pl.pallas_call(kernel, out_shape=[pltpu.HBM(shape, dtype) if spec.memory_...]
    ppermute x27 -> x30, starting transfers between devices: 22.3 us -> 23.1 us  [swap(): lax.ppermute(value, axis, [(index, index ^ step) for index in range(count)])]
  transfers between devices with their start and end apart: 27 -> 30, of which waited for: 12 -> 11; matrix products, arithmetic and copies ran while one was open for 0% -> 0% of each run, Pallas kernels for 32% -> 56%
where the time goes in v1:
time: 134 us
  Pallas kernels  84.7 us (63%)
  waiting for transfers between devices  23.5 us (18%)
  starting transfers between devices  23.1 us (17%)
  local copies, waits for them, and re-layouts  1.35 us (1%)
    pallas_call x16, Pallas kernels, call(): pl.pallas_call(kernel, out_shape=[pltpu.HBM(shape, dtype) if spec.memory_...  84.7 us
    ppermute x30, waiting for transfers between devices, swap(): lax.ppermute(value, axis, [(index, index ^ step) for index in range(count)])  23.5 us
    ppermute x30, starting transfers between devices, swap(): lax.ppermute(value, axis, [(index, index ^ step) for index in range(count)])  23.1 us
  transfers between devices with their start and end apart: 30, of which 11 were waited for; matrix products, arithmetic and copies ran while one was open for 0% of the time, Pallas kernels for 56%

profile of v1, /device:TPU:0, one launch (start us, length us, event | category | flops | bytes accessed | tf_op | source)
XLA Modules:
  0.0 133.9 jit_solution(11905723261572379988)
XLA Ops:
  0.6 2.8 %right_projection.2 = (bf16[16,128,128]{2,1,0:T(8,128)(2,1)S(1)}, bf16[128,16,128]{2,1,0:T(8,128)(2,1)S(1)}, f32[16,128]{1,0:T(8,128)S(1)}) custom-call(bf16[32,128,128]{2,1,0:T(8,128)(2,1)} %bitcast.30, s32[32,128]{1,0:T(8,128)} %bitcast.37, s32[1,128]{1,0:T(1,128)} %tokens_any.3, f32[1,128]{1,0:T(1,128)} %bitcast.17, bf16[128,512]{1,0:T(8,128)(2,1)} %refs_4_.7), custom_call_target="tpu_custom_call" | custom-call | flops 3000000000 | bytes 9000000 | tf_op jit(solution)/shard_map/right_projection/pallas_call | solution.py:109
  4.0 2.6 %collective-permute-start.2 = (bf16[128,16,128]{2,1,0:T(8,128)(2,1)S(1)}, bf16[128,16,128]{2,1,0:T(8,128)(2,1)S(1)}, u32[]{:S(2)}, u32[]{:S(2)}) collective-permute-start(bf16[128,16,128]{2,1,0:T(8,128)(2,1)S(1)} %get-tuple-element.97.refs_0_), channel_id=1, source_target_pairs={{0,16},{8,24},{16,0},{24,8},{1,17},{9,25},{17,1},{25,9},{2,18},{10... | collective-permute-start | bytes 1572872 | tf_op jit(solution)/shard_map/ppermute | solution.py:849
  6.6 3.6 %right_projection.3 = (bf16[16,128,128]{2,1,0:T(8,128)(2,1)S(1)}, bf16[128,16,128]{2,1,0:T(8,128)(2,1)}, f32[16,128]{1,0:T(8,128)S(1)}) custom-call(bf16[32,128,128]{2,1,0:T(8,128)(2,1)} %bitcast.31, s32[32,128]{1,0:T(8,128)} %bitcast.38, s32[1,128]{1,0:T(1,128)} %tokens_any.3, f32[1,128]{1,0:T(1,128)} %bitcast.18, bf16[128,512]{1,0:T(8,128)(2,1)} %refs_4_.7), custom_call_target="tpu_custom_call" | custom-call | flops 3000000000 | bytes 9000000 | tf_op jit(solution)/shard_map/right_projection/pallas_call | solution.py:109
  10.7 5.0 %left_projection.1 = (bf16[32,128,128]{2,1,0:T(8,128)(2,1)}, bf16[64,32,128]{2,1,0:T(8,128)(2,1)S(1)}, bf16[64,32,128]{2,1,0:T(8,128)(2,1)S(1)}, f32[32,128,128]...) custom-call(bf16[16,128,128]{2,1,0:T(8,128)(2,1)S(1)} %get-tuple-element.99.refs_0_, ...), custom_call_target="tpu_custom_call" | custom-call | flops 6000000000 | bytes 18000000 | tf_op jit(solution)/shard_map/left_projection/pallas_call | solution.py:109
  15.7 3.6 %collective-permute-done.2.refs_4_ = bf16[128,16,128]{2,1,0:T(8,128)(2,1)S(1)} collective-permute-done((bf16[128,16,128]{2,1,0:T(8,128)(2,1)S(1)}, bf16[128,16,128]{2,1,0:T(8,128)(2,1)S(1)}, u32[]{:S(2)}, u32[]{:S(2)}) %collective-permute-start.2) | collective-permute-done | bytes 524320 | tf_op jit(solution)/shard_map/ppermute | solution.py:849
  19.4 4.3 %right_factors.1 = (bf16[32,256,128]{2,1,0:T(8,128)(2,1)}, bf16[32,128,128]{2,1,0:T(8,128)(2,1)}) custom-call(bf16[16,128,128]{2,1,0:T(8,128)(2,1)S(1)} %get-tuple-element.99.refs_0_, bf16[16,128,128]{2,1,0:T(8,128)(2,1)S(1)} %get-tuple-element.100.refs_1_, f32[32,128]{1,0:T(8,128)S(1)} %get-tuple-element.105.refs_2_.refs_6_, ...), custom_call_target="tpu_custom_call" | custom-call | flops 5000000000 | bytes 15000000 | tf_op jit(solution)/shard_map/right_factors/pallas_call | solution.py:109
  23.6 6.8 %collective-permute-done.3.refs_5_ = bf16[128,16,128]{2,1,0:T(8,128)(2,1)} collective-permute-done((bf16[128,16,128]{2,1,0:T(8,128)(2,1)}, bf16[128,16,128]{2,1,0:T(8,128)(2,1)}, u32[]{:S(2)}, u32[]{:S(2)}) %collective-permute-start.3) | collective-permute-done | bytes 524320 | tf_op jit(solution)/shard_map/ppermute | solution.py:849
  31.2 1.8 %collective-permute-start.7 = (bf16[64,32,128]{2,1,0:T(8,128)(2,1)S(1)}, bf16[64,32,128]{2,1,0:T(8,128)(2,1)S(1)}, u32[]{:S(2)}, u32[]{:S(2)}) collective-permute-start(bf16[64,32,128]{2,1,0:T(8,128)(2,1)S(1)} %get-tuple-element.113.refs_8_.refs_4_), channel_id=1, source_target_pairs={{0,16},{8,24},{16,0},{24,8},{1,17},{9,25},{17,1},{25,9},{2,18},{10... | collective-permute-start | bytes 1572872 | tf_op jit(solution)/shard_map/ppermute | solution.py:849
  33.4 11.6 %product_and_norms.1 = (bf16[32,128,128]{2,1,0:T(8,128)(2,1)}, bf16[32,128,128]{2,1,0:T(8,128)(2,1)}, bf16[32,128,128]{2,1,0:T(8,128)(2,1)}, bf16[32,128,128]{2,...) custom-call(bf16[128,16,128]{2,1,0:T(8,128)(2,1)S(1)} %get-tuple-element.97.refs_0, ...), custom_call_target="tpu_custom_call" | custom-call | flops 14000000000 | bytes 42000000 | tf_op jit(solution)/shard_map/product_and_norms/pallas_call | solution.py:109
  47.0 4.6 %attention_projections.1 = (bf16[32,384,128]{2,1,0:T(8,128)(2,1)}, bf16[32,128,128]{2,1,0:T(8,128)(2,1)}, f32[32,128,128]{2,1,0:T(8,128)}) custom-call(bf16[32,128,128]{2,1,0:T(8,128)(2,1)} %get-tuple-element.114.normed3_any.normed3.refs_5_, bf16[128,512]{1,0:T(8,128)(2,1)} %refs_8_.1), custom_call_target="tpu_custom_call" | custom-call | flops 5000000000 | bytes 15000000 | tf_op jit(solution)/shard_map/attention_projections/pallas_call | solution.py:109
  53.1 14.9 %attention.1 = (bf16[32,128,128]{2,1,0:T(8,128)(2,1)}, bf16[32,512,128]{2,1,0:T(8,128)(2,1)S(1)}, f32[128,128]{1,0:T(8,128)S(1)}, f32[16,128]{1,0:T(8,128)S(1)},...) custom-call(f32[16,4]{1,0:T(8,128)S(1)} %bitcast.29, ...), custom_call_target="tpu_custom_call" | custom-call | flops 20000000000 | bytes 60000000 | tf_op jit(solution)/shard_map/attention/pallas_call | solution.py:109
  70.1 2.4 %projection_back.1 = (f32[32,128,128]{2,1,0:T(8,128)S(1)}, bf16[672,128]{1,0:T(8,128)(2,1)S(1)}) custom-call(bf16[32,512,128]{2,1,0:T(8,128)(2,1)S(1)} %get-tuple-element.128.d_projected, bf16[32,128,128]{2,1,0:T(8,128)(2,1)S(1)} %copy-done.13, bf16[128,512]{1,0:T(8,128)(2,1)S(1)} %copy-done.7, f32[128,128]{1,0:T(8,128)S(1)} %get-tuple-element.129.d_output, ...), custom_call_target="tpu_custom_call" | custom-call | flops 6000000000 | bytes 18000000 | tf_op jit(solution)/shard_map/projection_back/pallas_call | solution.py:109
  73.5 8.7 %middle_back.1 = (bf16[32,128,128]{2,1,0:T(8,128)(2,1)}, bf16[32,128,128]{2,1,0:T(8,128)(2,1)}, bf16[4096,128]{1,0:T(8,128)(2,1)}, f32[144,128]{1,0:T(8,128)S(1)...) custom-call(f32[32,512]{1,0:T(8,128)S(1)} %get-tuple-element.124.ref, ...), custom_call_target="tpu_custom_call" | custom-call | flops 12000000000 | bytes 36000000 | tf_op jit(solution)/shard_map/middle_back/pallas_call | solution.py:109
  84.7 7.8 %left_back.1 = (bf16[32,384,128]{2,1,0:T(8,128)(2,1)}, bf16[528,128]{1,0:T(8,128)(2,1)S(1)}) custom-call(bf16[128,128,128]{2,1,0:T(8,128)(2,1)} %get-tuple-element.123.right_any, bf16[4096,128]{1,0:T(8,128)(2,1)} %get-tuple-element.137.d_product_any, bf16[32,128,128]{2,1,0:T(8,128)(2,1)} %get-tuple-element.138.normed1_any.refs_12_, ...), custom_call_target="tpu_custom_call" | custom-call | flops 10000000000 | bytes 30000000 | tf_op jit(solution)/shard_map/left_back/pallas_call | solution.py:109
  92.6 3.7 %collective-permute-done.16.refs_3_ = bf16[32,32,128]{2,1,0:T(8,128)(2,1)S(1)} collective-permute-done((bf16[32,32,128]{2,1,0:T(8,128)(2,1)}, bf16[32,32,128]{2,1,0:T(8,128)(2,1)S(1)}, u32[]{:S(2)}, u32[]{:S(2)}) %collective-permute-start.16) | collective-permute-done | bytes 262176 | tf_op jit(solution)/shard_map/ppermute | solution.py:849
  96.3 5.7 %right_back.1 = (bf16[32,256,128]{2,1,0:T(8,128)(2,1)}, bf16[368,128]{1,0:T(8,128)(2,1)S(1)}, bf16[368,128]{1,0:T(8,128)(2,1)S(1)}, bf16[368,128]{1,0:T(8,128)(2,1)S(1)}, bf16[368,128]{1,0:T(8,128)(2,1)S(1)}) custom-call(bf16[32,32,128]{2,1,0:T(8,128)(2,1)S(1)} %copy-done.14, bf16[32,32,128]{2,1,0:T(8,128)(2,1)S(1)} %collective-permute-done.14.refs_1_, ...), custom_call_target="tpu_custom_call" | custom-call | flops 7000000000 | bytes 21000000 | tf_op jit(solution)/shard_map/right_back/pallas_call | solution.py:109
  104.1 3.0 %input_back.4.refs_7_ = bf16[32,128,128]{2,1,0:T(8,128)(2,1)} custom-call(bf16[32,384,128]{2,1,0:T(8,128)(2,1)} %get-tuple-element.142.refs_0_, bf16[32,256,128]{2,1,0:T(8,128)(2,1)} %get-tuple-element.155.refs_1_, bf16[32,128,128]{2,1,0:T(8,128)(2,1)} %bitcast.33, bf16[32,128,128]{2,1,0:T(8,128)(2,1)} %get-tuple-element.156.refs_3_, ...), custom_call_target="tpu_custom_call" | custom-call | flops 3000000000 | bytes 9000000 | tf_op jit(solution)/shard_map/input_back/pallas_call | solution.py:109
  107.2 2.0 %collective-permute-done.22 = bf16[368,128]{1,0:T(8,128)(2,1)S(1)} collective-permute-done((bf16[368,128]{1,0:T(8,128)(2,1)S(1)}, bf16[368,128]{1,0:T(8,128)(2,1)S(1)}, u32[]{:S(2)}, u32[]{:S(2)}) %collective-permute-start.22) | collective-permute-done | bytes 94240 | tf_op jit(solution)/shard_map/ppermute | solution.py:849
  110.8 3.0 %input_back.5.refs_7_ = bf16[32,128,128]{2,1,0:T(8,128)(2,1)} custom-call(bf16[32,384,128]{2,1,0:T(8,128)(2,1)} %get-tuple-element.142.refs_0_, bf16[32,256,128]{2,1,0:T(8,128)(2,1)} %get-tuple-element.155.refs_1_, bf16[32,128,128]{2,1,0:T(8,128)(2,1)} %bitcast.34, bf16[32,128,128]{2,1,0:T(8,128)(2,1)} %get-tuple-element.156.refs_3_, ...), custom_call_target="tpu_custom_call", output_to_operand_aliasing={{}: (7, {})} | custom-call | flops 3000000000 | bytes 9000000 | tf_op jit(solution)/shard_map/input_back/pallas_call | solution.py:109
  115.5 3.0 %input_back.6.refs_7_ = bf16[32,128,128]{2,1,0:T(8,128)(2,1)} custom-call(bf16[32,384,128]{2,1,0:T(8,128)(2,1)} %get-tuple-element.142.refs_0_, bf16[32,256,128]{2,1,0:T(8,128)(2,1)} %get-tuple-element.155.refs_1_, bf16[32,128,128]{2,1,0:T(8,128)(2,1)} %bitcast.35, bf16[32,128,128]{2,1,0:T(8,128)(2,1)} %get-tuple-element.156.refs_3_, ...), custom_call_target="tpu_custom_call", output_to_operand_aliasing={{}: (7, {})} | custom-call | flops 3000000000 | bytes 9000000 | tf_op jit(solution)/shard_map/input_back/pallas_call | solution.py:109
  118.6 2.7 %collective-permute-start.26 = (bf16[368,128]{1,0:T(8,128)(2,1)S(1)}, bf16[368,128]{1,0:T(8,128)(2,1)S(1)}, u32[]{:S(2)}, u32[]{:S(2)}) collective-permute-start(bf16[368,128]{1,0:T(8,128)(2,1)S(1)} %add.22), channel_id=1, source_target_pairs={{0,4},{1,5},{2,6},{3,7},{4,0},{5,1},{6,2},{7,3},{8,12},{9,13},{10,... | collective-permute-start | bytes 282632 | tf_op jit(solution)/shard_map/ppermute | solution.py:849
  121.2 4.0 %collective-permute-done.26 = bf16[368,128]{1,0:T(8,128)(2,1)S(1)} collective-permute-done((bf16[368,128]{1,0:T(8,128)(2,1)S(1)}, bf16[368,128]{1,0:T(8,128)(2,1)S(1)}, u32[]{:S(2)}, u32[]{:S(2)}) %collective-permute-start.26) | collective-permute-done | bytes 94240 | tf_op jit(solution)/shard_map/ppermute | solution.py:849
  125.4 1.8 %collective-permute-start.29 = (bf16[368,128]{1,0:T(8,128)(2,1)S(1)}, bf16[368,128]{1,0:T(8,128)(2,1)S(1)}, u32[]{:S(2)}, u32[]{:S(2)}) collective-permute-start(bf16[368,128]{1,0:T(8,128)(2,1)S(1)} %add.23.refs_0_), channel_id=1, source_target_pairs={{0,24},{8,16},{16,8},{24,0},{1,25},{9,17},{17,9},{25,1},{2,26},{10... | collective-permute-start | bytes 282632 | tf_op jit(solution)/shard_map/ppermute | solution.py:849
  127.2 3.0 %input_back.7 = bf16[32,128,128]{2,1,0:T(8,128)(2,1)} custom-call(bf16[32,384,128]{2,1,0:T(8,128)(2,1)} %get-tuple-element.142.refs_0_, bf16[32,256,128]{2,1,0:T(8,128)(2,1)} %get-tuple-element.155.refs_1_, bf16[32,128,128]{2,1,0:T(8,128)(2,1)} %bitcast.36, bf16[32,128,128]{2,1,0:T(8,128)(2,1)} %get-tuple-element.156.refs_3_, ...), custom_call_target="tpu_custom_call", output_to_operand_aliasing={{}: (7, {})} | custom-call | flops 3000000000 | bytes 9000000 | tf_op jit(solution)/shard_map/input_back/pallas_call | solution.py:109
  (108 shorter events, 20.3 us)
Async XLA Ops:
  3.5 29.5 %collective-permute-start = (bf16[128,16,128]{2,1,0:T(8,128)(2,1)S(1)}, bf16[128,16,128]{2,1,0:T(8,128)(2,1)S(1)}, u32[]{:S(2)}, u32[]{:S(2)}) collective-permute-start(bf16[128,16,128]{2,1,0:T(8,128)(2,1)S(1)} %get-tuple-element.97.refs_0_), channel_id=1, source_target_pairs={{0,8},{8,0},{16,24},{24,16},{1,9},{9,1},{17,25},{25,17},{2,10},{10... | collective-permute-start | bytes 1572872 | tf_op jit(solution)/shard_map/ppermute | solution.py:849
  4.0 15.3 %collective-permute-start.2 = (bf16[128,16,128]{2,1,0:T(8,128)(2,1)S(1)}, bf16[128,16,128]{2,1,0:T(8,128)(2,1)S(1)}, u32[]{:S(2)}, u32[]{:S(2)}) collective-permute-start(bf16[128,16,128]{2,1,0:T(8,128)(2,1)S(1)} %get-tuple-element.97.refs_0_), channel_id=1, source_target_pairs={{0,16},{8,24},{16,0},{24,8},{1,17},{9,25},{17,1},{25,9},{2,18},{10... | collective-permute-start | bytes 1572872 | tf_op jit(solution)/shard_map/ppermute | solution.py:849
  10.2 22.8 %collective-permute-start.1 = (bf16[128,16,128]{2,1,0:T(8,128)(2,1)}, bf16[128,16,128]{2,1,0:T(8,128)(2,1)}, u32[]{:S(2)}, u32[]{:S(2)}) collective-permute-start(bf16[128,16,128]{2,1,0:T(8,128)(2,1)} %get-tuple-element.98.refs_1_), channel_id=1, source_target_pairs={{0,8},{8,0},{16,24},{24,16},{1,9},{9,1},{17,25},{25,17},{2,10},{10... | collective-permute-start | bytes 1572872 | tf_op jit(solution)/shard_map/ppermute | solution.py:849
  10.4 20.0 %collective-permute-start.3 = (bf16[128,16,128]{2,1,0:T(8,128)(2,1)}, bf16[128,16,128]{2,1,0:T(8,128)(2,1)}, u32[]{:S(2)}, u32[]{:S(2)}) collective-permute-start(bf16[128,16,128]{2,1,0:T(8,128)(2,1)} %get-tuple-element.98.refs_1_), channel_id=1, source_target_pairs={{0,16},{8,24},{16,0},{24,8},{1,17},{9,25},{17,1},{25,9},{2,18},{10... | collective-permute-start | bytes 1572872 | tf_op jit(solution)/shard_map/ppermute | solution.py:849
  31.2 15.8 %collective-permute-start.7 = (bf16[64,32,128]{2,1,0:T(8,128)(2,1)S(1)}, bf16[64,32,128]{2,1,0:T(8,128)(2,1)S(1)}, u32[]{:S(2)}, u32[]{:S(2)}) collective-permute-start(bf16[64,32,128]{2,1,0:T(8,128)(2,1)S(1)} %get-tuple-element.113.refs_8_.refs_4_), channel_id=1, source_target_pairs={{0,16},{8,24},{16,0},{24,8},{1,17},{9,25},{17,1},{25,9},{2,18},{10... | collective-permute-start | bytes 1572872 | tf_op jit(solution)/shard_map/ppermute | solution.py:849
  45.0 8.0 %collective-permute-start.6 = (bf16[32,512]{1,0:T(8,128)(2,1)}, bf16[32,512]{1,0:T(8,128)(2,1)S(1)}, u32[]{:S(2)}, u32[]{:S(2)}) collective-permute-start(bf16[32,512]{1,0:T(8,128)(2,1)} %get-tuple-element.111.refs_0_), channel_id=1, source_target_pairs={{0,8},{8,0},{16,24},{24,16},{1,9},{9,1},{17,25},{25,17},{2,10},{10... | collective-permute-start | bytes 98312 | tf_op jit(solution)/shard_map/ppermute | solution.py:849
  45.2 6.4 %collective-permute-start.8 = (bf16[32,512]{1,0:T(8,128)(2,1)}, bf16[32,512]{1,0:T(8,128)(2,1)S(1)}, u32[]{:S(2)}, u32[]{:S(2)}) collective-permute-start(bf16[32,512]{1,0:T(8,128)(2,1)} %get-tuple-element.111.refs_0_), channel_id=1, source_target_pairs={{0,16},{8,24},{16,0},{24,8},{1,17},{9,25},{17,1},{25,9},{2,18},{10... | collective-permute-start | bytes 98312 | tf_op jit(solution)/shard_map/ppermute | solution.py:849
  51.8 32.4 %collective-permute-start.17 = (bf16[64,32,128]{2,1,0:T(8,128)(2,1)S(1)}, bf16[64,32,128]{2,1,0:T(8,128)(2,1)S(1)}, u32[]{:S(2)}, u32[]{:S(2)}) collective-permute-start(bf16[64,32,128]{2,1,0:T(8,128)(2,1)S(1)} %get-tuple-element.113.refs_8_.refs_4_), channel_id=1, source_target_pairs={{0,8},{8,0},{16,24},{24,16},{1,9},{9,1},{17,25},{25,17},{2,10},{10... | collective-permute-start | bytes 1572872 | tf_op jit(solution)/shard_map/ppermute | solution.py:849
  52.2 32.4 %collective-permute-start.19 = (bf16[64,32,128]{2,1,0:T(8,128)(2,1)S(1)}, bf16[64,32,128]{2,1,0:T(8,128)(2,1)S(1)}, u32[]{:S(2)}, u32[]{:S(2)}) collective-permute-start(bf16[64,32,128]{2,1,0:T(8,128)(2,1)S(1)} %get-tuple-element.131.refs_9_.refs_8_), channel_id=1, source_target_pairs={{0,8},{8,0},{16,24},{24,16},{1,9},{9,1},{17,25},{25,17},{2,10},{10... | collective-permute-start | bytes 1572872 | tf_op jit(solution)/shard_map/ppermute | solution.py:849
  52.7 17.3 %collective-permute-start.13 = (bf16[64,32,128]{2,1,0:T(8,128)(2,1)S(1)}, bf16[64,32,128]{2,1,0:T(8,128)(2,1)S(1)}, u32[]{:S(2)}, u32[]{:S(2)}) collective-permute-start(bf16[64,32,128]{2,1,0:T(8,128)(2,1)S(1)} %get-tuple-element.131.refs_9_.refs_8_), channel_id=1, source_target_pairs={{0,16},{8,24},{16,0},{24,8},{1,17},{9,25},{17,1},{25,9},{2,18},{10... | collective-permute-start | bytes 1572872 | tf_op jit(solution)/shard_map/ppermute | solution.py:849
  82.3 10.3 %collective-permute-start.14 = (bf16[32,32,128]{2,1,0:T(8,128)(2,1)}, bf16[32,32,128]{2,1,0:T(8,128)(2,1)S(1)}, u32[]{:S(2)}, u32[]{:S(2)}) collective-permute-start(bf16[32,32,128]{2,1,0:T(8,128)(2,1)} %get-tuple-element.144), channel_id=1, source_target_pairs={{0,8},{8,0},{16,24},{24,16},{1,9},{9,1},{17,25},{25,17},{2,10},{10... | collective-permute-start | bytes 786440 | tf_op jit(solution)/shard_map/ppermute | solution.py:849
  82.4 10.1 %collective-permute-start.15 = (bf16[32,32,128]{2,1,0:T(8,128)(2,1)}, bf16[32,32,128]{2,1,0:T(8,128)(2,1)S(1)}, u32[]{:S(2)}, u32[]{:S(2)}) collective-permute-start(bf16[32,32,128]{2,1,0:T(8,128)(2,1)} %get-tuple-element.145), channel_id=1, source_target_pairs={{0,16},{8,24},{16,0},{24,8},{1,17},{9,25},{17,1},{25,9},{2,18},{10... | collective-permute-start | bytes 786440 | tf_op jit(solution)/shard_map/ppermute | solution.py:849
  83.8 12.6 %collective-permute-start.16 = (bf16[32,32,128]{2,1,0:T(8,128)(2,1)}, bf16[32,32,128]{2,1,0:T(8,128)(2,1)S(1)}, u32[]{:S(2)}, u32[]{:S(2)}) collective-permute-start(bf16[32,32,128]{2,1,0:T(8,128)(2,1)} %get-tuple-element.146), channel_id=1, source_target_pairs={{0,24},{8,16},{16,8},{24,0},{1,25},{9,17},{17,9},{25,1},{2,26},{10... | collective-permute-start | bytes 786440 | tf_op jit(solution)/shard_map/ppermute | solution.py:849
  84.2 12.1 %collective-permute-start.18 = (bf16[64,32,128]{2,1,0:T(8,128)(2,1)S(1)}, bf16[64,32,128]{2,1,0:T(8,128)(2,1)S(1)}, u32[]{:S(2)}, u32[]{:S(2)}) collective-permute-start(bf16[64,32,128]{2,1,0:T(8,128)(2,1)S(1)} %collective-permute-done.7.refs_6_), channel_id=1, source_target_pairs={{0,8},{8,0},{16,24},{24,16},{1,9},{9,1},{17,25},{25,17},{2,10},{10... | collective-permute-start | bytes 1572872 | tf_op jit(solution)/shard_map/ppermute | solution.py:849
  84.6 11.7 %collective-permute-start.20 = (bf16[64,32,128]{2,1,0:T(8,128)(2,1)S(1)}, bf16[64,32,128]{2,1,0:T(8,128)(2,1)S(1)}, u32[]{:S(2)}, u32[]{:S(2)}) collective-permute-start(bf16[64,32,128]{2,1,0:T(8,128)(2,1)S(1)} %collective-permute-done.13.refs_10_), channel_id=1, source_target_pairs={{0,8},{8,0},{16,24},{24,16},{1,9},{9,1},{17,25},{25,17},{2,10},{10... | collective-permute-start | bytes 1572872 | tf_op jit(solution)/shard_map/ppermute | solution.py:849
  102.1 5.1 %collective-permute-start.23 = (bf16[368,128]{1,0:T(8,128)(2,1)S(1)}, bf16[368,128]{1,0:T(8,128)(2,1)S(1)}, u32[]{:S(2)}, u32[]{:S(2)}) collective-permute-start(bf16[368,128]{1,0:T(8,128)(2,1)S(1)} %get-tuple-element.160), channel_id=1, source_target_pairs={{0,24},{8,16},{16,8},{24,0},{1,25},{9,17},{17,9},{25,1},{2,26},{10... | collective-permute-start | bytes 282632 | tf_op jit(solution)/shard_map/ppermute | solution.py:849
  103.1 6.0 %collective-permute-start.22 = (bf16[368,128]{1,0:T(8,128)(2,1)S(1)}, bf16[368,128]{1,0:T(8,128)(2,1)S(1)}, u32[]{:S(2)}, u32[]{:S(2)}) collective-permute-start(bf16[368,128]{1,0:T(8,128)(2,1)S(1)} %get-tuple-element.159), channel_id=1, source_target_pairs={{0,16},{8,24},{16,0},{24,8},{1,17},{9,25},{17,1},{25,9},{2,18},{10... | collective-permute-start | bytes 282632 | tf_op jit(solution)/shard_map/ppermute | solution.py:849
  104.1 5.0 %collective-permute-start.21 = (bf16[368,128]{1,0:T(8,128)(2,1)S(1)}, bf16[368,128]{1,0:T(8,128)(2,1)S(1)}, u32[]{:S(2)}, u32[]{:S(2)}) collective-permute-start(bf16[368,128]{1,0:T(8,128)(2,1)S(1)} %get-tuple-element.158), channel_id=1, source_target_pairs={{0,8},{8,0},{16,24},{24,16},{1,9},{9,1},{17,25},{25,17},{2,10},{10... | collective-permute-start | bytes 282632 | tf_op jit(solution)/shard_map/ppermute | solution.py:849
  109.2 4.6 %collective-permute-start.24 = (bf16[368,128]{1,0:T(8,128)(2,1)S(1)}, bf16[368,128]{1,0:T(8,128)(2,1)S(1)}, u32[]{:S(2)}, u32[]{:S(2)}) collective-permute-start(bf16[368,128]{1,0:T(8,128)(2,1)S(1)} %add_convert_fusion), channel_id=1, source_target_pairs={{0,1},{1,0},{2,3},{3,2},{4,5},{5,4},{6,7},{7,6},{8,9},{9,8},{10,11... | collective-permute-start | bytes 282632 | tf_op jit(solution)/shard_map/ppermute | solution.py:849
  113.9 4.6 %collective-permute-start.25 = (bf16[368,128]{1,0:T(8,128)(2,1)S(1)}, bf16[368,128]{1,0:T(8,128)(2,1)S(1)}, u32[]{:S(2)}, u32[]{:S(2)}) collective-permute-start(bf16[368,128]{1,0:T(8,128)(2,1)S(1)} %add.21), channel_id=1, source_target_pairs={{0,2},{1,3},{2,0},{3,1},{4,6},{5,7},{6,4},{7,5},{8,10},{9,11},{10,... | collective-permute-start | bytes 282632 | tf_op jit(solution)/shard_map/ppermute | solution.py:849
  118.6 6.7 %collective-permute-start.26 = (bf16[368,128]{1,0:T(8,128)(2,1)S(1)}, bf16[368,128]{1,0:T(8,128)(2,1)S(1)}, u32[]{:S(2)}, u32[]{:S(2)}) collective-permute-start(bf16[368,128]{1,0:T(8,128)(2,1)S(1)} %add.22), channel_id=1, source_target_pairs={{0,4},{1,5},{2,6},{3,7},{4,0},{5,1},{6,2},{7,3},{8,12},{9,13},{10,... | collective-permute-start | bytes 282632 | tf_op jit(solution)/shard_map/ppermute | solution.py:849
  125.3 5.0 %collective-permute-start.27 = (bf16[368,128]{1,0:T(8,128)(2,1)S(1)}, bf16[368,128]{1,0:T(8,128)(2,1)S(1)}, u32[]{:S(2)}, u32[]{:S(2)}) collective-permute-start(bf16[368,128]{1,0:T(8,128)(2,1)S(1)} %add.23.refs_0_), channel_id=1, source_target_pairs={{0,8},{8,0},{16,24},{24,16},{1,9},{9,1},{17,25},{25,17},{2,10},{10... | collective-permute-start | bytes 282632 | tf_op jit(solution)/shard_map/ppermute | solution.py:849
  125.4 5.6 %collective-permute-start.28 = (bf16[368,128]{1,0:T(8,128)(2,1)S(1)}, bf16[368,128]{1,0:T(8,128)(2,1)S(1)}, u32[]{:S(2)}, u32[]{:S(2)}) collective-permute-start(bf16[368,128]{1,0:T(8,128)(2,1)S(1)} %add.23.refs_0_), channel_id=1, source_target_pairs={{0,16},{8,24},{16,0},{24,8},{1,17},{9,25},{17,1},{25,9},{2,18},{10... | collective-permute-start | bytes 282632 | tf_op jit(solution)/shard_map/ppermute | solution.py:849
  125.4 6.6 %collective-permute-start.29 = (bf16[368,128]{1,0:T(8,128)(2,1)S(1)}, bf16[368,128]{1,0:T(8,128)(2,1)S(1)}, u32[]{:S(2)}, u32[]{:S(2)}) collective-permute-start(bf16[368,128]{1,0:T(8,128)(2,1)S(1)} %add.23.refs_0_), channel_id=1, source_target_pairs={{0,24},{8,16},{16,8},{24,0},{1,25},{9,17},{17,9},{25,1},{2,26},{10... | collective-permute-start | bytes 282632 | tf_op jit(solution)/shard_map/ppermute | solution.py:849
  (29 other events, 205.2 us)

commit v2 on v1

--- a/solution.py
+++ b/solution.py
@@ -13,6 +13,7 @@
 BF16 = jnp.bfloat16
 VMEM_MARGIN = 4 * 1024 * 1024
 W_PRODUCT, W_ATTEND, W_MIDDLE = 8, 4, 8
+LOG2_E = math.log2(math.e)
 HEAD_ROWS = 16
 
 
@@ -25,13 +26,7 @@
 
 
 def sigmoid(value):
-    return 1.0 / (1.0 + jnp.exp(-value))
-
-
-def identity(size):
-    rows = lax.broadcasted_iota(jnp.int32, (size, size), 0)
-    columns = lax.broadcasted_iota(jnp.int32, (size, size), 1)
-    return (rows == columns).astype(F32).astype(BF16)
+    return 0.5 + 0.5 * jnp.tanh(0.5 * value)
 
 
 def norm_parts(values, axis):
@@ -69,6 +64,11 @@
         return carry
 
     lax.fori_loop(0, count // width, some, 0)
+
+
+def side_by_side(first, last, body, most=16):
+    unroll = max(one for one in range(1, most + 1) if (last - first) % one == 0)
+    lax.fori_loop(first, last, lambda index, carry: body(index), None, unroll=unroll)
 
 
 def split_copies(source, target, sems, parts):
@@ -127,10 +127,9 @@
     )(*args)
 
 
-def right_kernel(
-    part, pair_any, mask_any, tokens_any, gain_any, weight_any, normed_out, right_out, live_out, *scratch
-):
-    pair, mask, tokens, gain, weight, weight_t, lay, sems = scratch
+def right_kernel(part, pair_any, mask_any, tokens_any, gain_any, weight_any, *refs):
+    normed_any, right_out, live_out = refs[-12:-9]
+    pair, mask, tokens, gain, weight, weight_t, lay, normed_out, sems = refs[-9:]
     rows, length, channels = pair.shape
     place = lax.axis_index("dap")
     span = pl.ds(part * rows, rows)
@@ -160,7 +159,10 @@
         lay[pl.ds(i, channels, stride=rows), :] = right
 
     over_rows(rows, 8, row)
+    departure = pltpu.make_async_copy(normed_out, normed_any.at[span], sems.at[5])
+    departure.start()
     right_out[...] = lay[...].reshape(channels, rows, length).astype(BF16)
+    departure.wait()
 
 
 def gate_factors(projected, live_row, channels):
@@ -172,26 +174,25 @@
     return out, factors
 
 
-def left_kernel(parts, *refs):
-    normed_parts = refs[:parts]
-    live_parts = refs[parts : 2 * parts]
-    weight, gating = refs[2 * parts : 2 * parts + 2]
-    normed_any, low_out, high_out, gate_any, live, factor_any = refs[2 * parts + 2 : 2 * parts + 8]
-    weight_t, lay, gates, factors, sems = refs[2 * parts + 8 :]
+def left_kernel(parts, normed_any, *refs):
+    live_parts = refs[:parts]
+    weight, gating = refs[parts : parts + 2]
+    low_out, high_out, gate_any, live, factor_any = refs[parts + 2 : parts + 7]
+    weight_t, lay, gates, factors, normed1, in_sems, sems = refs[parts + 7 :]
+    arrivals = split_copies(normed_any, normed1, in_sems, parts)
+    start(arrivals)
     rows, length, channels = gates.shape
     half = rows // parts
     weight_t[...] = weight[:, : 2 * channels].astype(F32).T.astype(BF16)
     outs = []
     for part in range(parts):
         span = pl.ds(part * half, half)
-        copy = pltpu.make_async_copy(normed_parts[part], normed_any.at[span], sems.at[0, part])
-        copy.start()
-        outs.append(copy)
         live[span, :] = live_parts[part][...]
+        arrivals[part].wait()
 
         def row(i, part=part):
-            normed = normed_parts[part][i]
             at = i + part * half
+            normed = normed1[at]
             projected = mmt(weight_t[...], normed)
             gate = mm(normed, gating[...])
             yield
@@ -202,35 +203,39 @@
         over_rows(half, 8, row)
         for index, (source, target) in enumerate(((gates, gate_any), (factors, factor_any))):
             copy = pltpu.make_async_copy(
-                source.at[span], target.at[span], sems.at[1 + index, part]
+                source.at[span], target.at[span], sems.at[index, part]
             )
             copy.start()
             outs.append(copy)
     left = lay[...].reshape(channels, rows, length).astype(BF16)
-    low_out[...] = left[: channels // 2]
-    high_out[...] = left[channels // 2 :]
+    low = low_out.shape[0]
+    low_out[...] = left[:low]
+    high_out[...] = left[low:]
     wait(outs)
 
 
 def factor_kernel(parts, *refs):
-    normed_parts = refs[:parts]
-    live, weight, output_w, cotangent_any, factor_any, d_gated_any = refs[parts : parts + 6]
-    cotangent, factors, d_gated, in_sem, sems = refs[parts + 6 :]
+    live, weight, output_w, normed_any, cotangent_any, factor_any, d_gated_any = refs[:7]
+    normed1, cotangent, factors, d_gated, in_sems, sems = refs[7:]
     rows, length, channels = cotangent.shape
     half = rows // parts
-    arrivals = split_copies(cotangent_any, cotangent, in_sem, parts)
-    start(arrivals)
+    arrivals = [
+        split_copies(normed_any, normed1, in_sems.at[0], parts),
+        split_copies(cotangent_any, cotangent, in_sems.at[1], parts),
+    ]
+    for copies in arrivals:
+        start(copies)
     weight_t = weight[:, 2 * channels : 4 * channels].astype(F32).T.astype(BF16)
     departures = [
         split_copies(factors, factor_any, sems.at[0], parts),
         split_copies(d_gated, d_gated_any, sems.at[1], parts),
     ]
     for part in range(parts):
-        arrivals[part].wait()
+        wait([copies[part] for copies in arrivals])
 
         def row(i, part=part):
             at = i + part * half
-            projected = mmt(weight_t, normed_parts[part][i])
+            projected = mmt(weight_t, normed1[at])
             back = mmt(cotangent[at], output_w[...])
             yield
             _, factors[at] = gate_factors(projected, live[pl.ds(at, 1), :], channels)
@@ -242,87 +247,130 @@
         wait(copies)
 
 
-def product_kernel(count, *refs):
-    blocks = refs[: 2 * count]
-    lefts = refs[2 * count : 2 * count + 2]
-    (pair_any, gate_any, gain2_col, gain3, output_w, bias_w) = refs[2 * count + 2 : 2 * count + 8]
-    row_outs = refs[2 * count + 8 : 2 * count + 12]
-    right_any, scale2_out, bias_out = refs[2 * count + 12 : 2 * count + 15]
-    product, bias_scr, right_all, pair, gate = refs[2 * count + 15 : 2 * count + 20]
-    kept = refs[2 * count + 20 : 2 * count + 24]
+def product_kernel(count, side, *refs):
+    near = count // 2
+    blocks = refs[: 2 * near]
+    lefts = refs[2 * near : 2 * near + 2]
+    (pair_any, gate_any, gain2_col, gain3, output_w, bias_w) = refs[2 * near + 2 : 2 * near + 8]
+    rest = refs[2 * near + 8 :]
+    if side:
+        bias_any, rest = rest[0], rest[5:]
+    row_outs = rest[:4]
+    right_any, scale2_out, bias_out, product, bias_scr, right_side, pair, gate = rest[4:12]
+    kept = rest[12:16]
     normed2_out, update_out, middle_out, normed3_out = kept
-    in_sems, out_sems, right_sem = refs[2 * count + 24 :]
-    rows, length, channels = pair.shape
+    in_sems, out_sems, right_sem, bias_sem, bias_near = rest[16:]
+    rows, wide, channels = pair.shape
+    length = 2 * wide
+    lines = rows // 2
     heads = bias_w.shape[1]
-    half = rows // 2
     place = lax.axis_index("dap")
+    chip = place // near
+    span = pl.ds(pl.multiple_of((chip ^ side) * wide, wide), wide)
     arrivals = [
-        pltpu.make_async_copy(pair_any, pair, in_sems.at[0]),
-        pltpu.make_async_copy(gate_any, gate, in_sems.at[1]),
+        pltpu.make_async_copy(pair_any.at[:, span, :], pair, in_sems.at[0]),
+        pltpu.make_async_copy(gate_any.at[:, span, :], gate, in_sems.at[1]),
     ]
     start(arrivals)
+    if side:
+        bias_copy = pltpu.make_async_copy(bias_any, bias_near, bias_sem)
+        bias_copy.start()
+    size = blocks[0].shape[1]
     starts = [
-        pl.multiple_of((place ^ (index // 2)) * rows + (index % 2) * half, half)
-        for index in range(2 * count)
-    ]
-
-    def channel(c, carry):
+        pl.multiple_of(((place ^ (index // 2)) % near) * rows + (index % 2) * size, size)
+        for index in range(2 * near)
+    ]
+
+    def channel(c):
         for begin, ref in zip(starts, blocks):
-            right_all[c, pl.ds(begin, half), :] = ref[c]
-        return carry
-
-    lax.fori_loop(0, channels, channel, 0, unroll=4)
-    right_copy = pltpu.make_async_copy(right_all, right_any, right_sem)
+            right_side[c, pl.ds(begin, size), :] = ref[c]
+
+    side_by_side(0, channels, channel)
+    right_copy = pltpu.make_async_copy(right_side, right_any, right_sem)
     right_copy.start()
-
-    for part, left in enumerate(lefts):
-
-        def multiply(c, carry, left=left, first=part * (channels // 2)):
-            product[pl.ds(first + c, rows, stride=channels), :] = mmt(
-                left[c], right_all[first + c]
+    for left, first in zip(lefts, (0, lefts[0].shape[0])):
+
+        def multiply(pair_of, left=left, first=first):
+            c = 2 * pair_of
+            cells = mmt(
+                left[pl.ds(c, 2)].reshape(2 * rows, length),
+                right_side[pl.ds(first + c, 2)].reshape(length, length),
             )
-            return carry
-
-        lax.fori_loop(0, channels // 2, multiply, 0, unroll=8)
-    eye = identity(channels)
+            for one in range(2):
+                mine = cells[one * rows : (one + 1) * rows, one * wide : (one + 1) * wide]
+                product[pl.ds(first + c + one, lines, stride=channels), :] = jnp.concatenate(
+                    [mine[:lines], mine[lines:]], axis=1
+                )
+
+        side_by_side(0, left.shape[0] // 2, multiply)
     gain2 = jnp.broadcast_to(gain2_col[...], (channels, length))
     bias_t = jnp.concatenate(
         [bias_w[...].astype(F32).T, jnp.zeros((HEAD_ROWS - heads, channels), F32)], axis=0
     ).astype(BF16)
 
-    def row(i):
-        hat, scale = norm_parts(product[pl.ds(i * channels, channels), :], 0)
+    def tile(p):
+        hat, scale = norm_parts(product[pl.ds(p * channels, channels), :], 0)
         yield
         normed2_t = (hat * gain2).astype(BF16)
-        normed2_out[i] = normed2_t
-        scale2_out[pl.ds(i, 1), :] = scale
-        normed2 = mmt(eye, normed2_t).astype(BF16)
+        normed2_out[p] = normed2_t
+        scale2_out[pl.ds(p, 1), :] = scale
+        normed2 = normed2_t.T
         yield
         update = mm(normed2, output_w[...])
         yield
-        update_out[i] = update.astype(BF16)
-        middle = (pair[i].astype(F32) + gate[i] * update).astype(BF16)
-        middle_out[i] = middle
+        update_b = update.astype(BF16)
+        gates = jnp.concatenate([gate[p], gate[p + lines]], axis=0)
+        pairs = jnp.concatenate([pair[p], pair[p + lines]], axis=0)
+        middle = (pairs.astype(F32) + gates * update).astype(BF16)
         hat3, _ = norm_parts(middle.astype(F32), -1)
         yield
         normed3 = (hat3 * gain3[...]).astype(BF16)
-        normed3_out[i] = normed3
-        bias_scr[pl.ds(i * HEAD_ROWS, HEAD_ROWS), :] = mmt(bias_t, normed3)
+        bias_scr[pl.ds(p * HEAD_ROWS, HEAD_ROWS), :] = mmt(bias_t, normed3)
+        for out, value in ((update_out, update_b), (middle_out, middle), (normed3_out, normed3)):
+            out[p] = value[:wide]
+            out[p + lines] = value[wide:]
 
     wait(arrivals)
-    parts = 4
-    departures = [
-        split_copies(source, target, out_sems.at[at], parts)
-        for at, (source, target) in enumerate(zip(kept, row_outs))
-    ]
+    parts = 2
+    run = lines // parts
+    departures = []
     for part in range(parts):
-        over_rows(rows // parts, W_PRODUCT, row, first=part * (rows // parts))
-        start([copies[part] for copies in departures])
-    for h in range(heads):
-        head = bias_scr[pl.ds(h, rows, stride=HEAD_ROWS), :]
-        bias_out[:, h * length : (h + 1) * length] = head.astype(BF16)
-    for copies in departures:
-        wait(copies)
+        over_rows(run, W_PRODUCT, tile, first=part * run)
+        some = pl.ds(part * run, run)
+        copies = [
+            pltpu.make_async_copy(
+                normed2_out.at[some], row_outs[0].at[side, some], out_sems.at[0, part]
+            )
+        ]
+        for at in range(1, 4):
+            for group in range(2):
+                some = pl.ds(group * lines + part * run, run)
+                copies.append(
+                    pltpu.make_async_copy(
+                        kept[at].at[some],
+                        row_outs[at].at[some, span, :],
+                        out_sems.at[at, 2 * part + group],
+                    )
+                )
+        start(copies)
+        departures += copies
+    if not side:
+        copy = pltpu.make_async_copy(bias_scr, bias_out, bias_sem)
+        copy.start()
+        departures.append(copy)
+    else:
+        bias_copy.wait()
+        for h in range(heads):
+            mine = bias_near[pl.ds(h, lines, stride=HEAD_ROWS), :]
+            other = bias_scr[pl.ds(h, lines, stride=HEAD_ROWS), :]
+            first = jnp.where(chip == 0, mine, other)
+            second = jnp.where(chip == 0, other, mine)
+            head = slice(h * length, (h + 1) * length)
+            low = jnp.concatenate([first[:, :wide], second[:, :wide]], axis=1)
+            high = jnp.concatenate([first[:, wide:], second[:, wide:]], axis=1)
+            bias_out[:lines, head] = low.astype(BF16)
+            bias_out[lines:, head] = high.astype(BF16)
+    wait(departures)
     right_copy.wait()
 
 
@@ -349,7 +397,7 @@
         yield
         projected3[i, :channels] = (projected_t[:channels] * factor).astype(BF16)
         projected3[i, channels:] = projected_t[channels:].astype(BF16)
-        queries[i] = (projected[:, :channels] * factor).astype(BF16)
+        queries[i] = (projected[:, :channels] * (factor * LOG2_E)).astype(BF16)
         gates[i] = sigmoid(projected[:, channels:])
 
     departures = [
@@ -406,14 +454,13 @@
             for b in range(types):
                 values = jnp.where(row_types == b, table[h * types + a, b], values)
             total = jnp.where(col_types == a, values, total)
-        bias[:, spans(h)] = bias[:, spans(h)] + total
+        bias[:, spans(h)] = (bias[:, spans(h)] + total) * LOG2_E
     d_bias[...] = jnp.zeros_like(d_bias)
     d_output[...] = jnp.zeros_like(d_output)
     lines = lax.broadcasted_iota(jnp.int32, head_mask.shape, 0) // size
     columns = lax.broadcasted_iota(jnp.int32, head_mask.shape, 1) // length
     head_mask[...] = (lines == columns).astype(F32).astype(BF16)
 
-    eye = identity(channels)
 
     def row(i):
         live_row = live[pl.ds(i, 1), :]
@@ -431,7 +478,7 @@
         )
         score = mm(queries[i], keys)
         yield
-        expo = jnp.exp(score + bias[...])
+        expo = jnp.exp2(score + bias[...])
         expo_b = expo.astype(BF16)
         sums = mmt(expo_b, values)
         yield
@@ -447,9 +494,7 @@
             [d_attended_b, (-d_attended * attended * slope).astype(BF16)], axis=1
         )
         d_expo = mm(both, values)
-        turned = mmt(
-            eye, jnp.concatenate([d_attended_b, d_gate.astype(BF16), gated], axis=0)
-        ).astype(BF16)
+        turned = jnp.concatenate([d_attended_b.T, d_gate.astype(BF16).T, gated.T], axis=1)
         yield
         update = mm(gated, output_w[...])
         d_score = expo * d_expo
@@ -535,7 +580,9 @@
 def middle_kernel(count, *refs):
     arrived = refs[:count]
     (d_normed3, normed3, middle, cotangent, gain3_col, bias_w) = refs[count : count + 6]
-    (normed2, scale2, update, gate, gain2_col, output_w) = refs[count + 6 : count + 12]
+    normed2, *scales = refs[count + 6 : count + 9]
+    refs = refs[1:]
+    (update, gate, gain2_col, output_w) = refs[count + 8 : count + 12]
     (d_middle_any, d_gate_any, d_product_any, grad_out) = refs[count + 12 : count + 16]
     send_any = refs[count + 16 : 2 * count + 16]
     d_bias, lay, d_middle_out, d_gate_out, d_product_out = refs[2 * count + 16 : 2 * count + 21]
@@ -544,7 +591,8 @@
     rows, length, channels = middle.shape
     heads = bias_w.shape[1]
     place = lax.axis_index("dap")
-    eye = identity(channels)
+    chip = place // (count // 2)
+    lines, wide = rows // 2, length // 2
     total = arrived[0][...]
     for ref in arrived[1:]:
         total = total + ref[...].astype(F32)
@@ -562,10 +610,10 @@
     def row(i):
         bias_rows = d_bias[pl.ds(i * HEAD_ROWS, HEAD_ROWS), :].astype(BF16)
         d_normed = d_normed3[i] + mm(bias_wide, bias_rows)
-        hat3, scale3 = norm_parts(mmt(eye, middle[i]), 0)
+        hat3, scale3 = norm_parts(middle[i].T.astype(F32), 0)
         yield
         d_mid_t = norm_back(d_normed * gain3, hat3, scale3, 0).astype(BF16)
-        d_mid_b = mmt(eye, d_mid_t)
+        d_mid_b = d_mid_t.T.astype(F32)
         yield
         d_mid = (cotangent[i].astype(F32) + d_mid_b).astype(BF16)
         d_middle_out[i] = d_mid
@@ -573,26 +621,48 @@
         d_mid = d_mid.astype(F32)
         d_up = d_mid * gates
         d_gate_out[i] = (d_up * update[i].astype(F32) * (1.0 - gates)).astype(BF16)
-        d_up = d_up.astype(BF16)
-        normed2_t = normed2[i]
-        d_hat2 = mmt(output_w[...], d_up)
-        yield
-        hat2 = normed2_t.astype(F32) * inverse2
-        lay[pl.ds(i, channels, stride=rows), :] = norm_back(
-            d_hat2 * gain2, hat2, scale2[pl.ds(i, 1), :], 0
-        )
-        return normed2_t, d_up, bias_rows, normed3[i]
+        return d_up.astype(BF16), bias_rows, normed3[i]
+
+    def two_rows(p):
+        low, high = row(p), row(p + lines)
+        for _ in range(2):
+            next(low)
+            next(high)
+            yield
+        low, high = [lockstep(lambda one: one, [one])[0] for one in (low, high)]
+        tiles = []
+        for t in range(2):
+            d_up = jnp.concatenate(
+                [one[0][t * wide : (t + 1) * wide] for one in (low, high)], axis=0
+            )
+            tiles.append((normed2[chip ^ t, p], d_up, mmt(output_w[...], d_up)))
+        yield
+        backs = []
+        for t, (normed2_t, _, d_hat2) in enumerate(tiles):
+            scale2 = jnp.where(
+                chip == t, scales[0][pl.ds(p, 1), :], scales[1][pl.ds(p, 1), :]
+            )
+            hat2 = normed2_t.astype(F32) * inverse2
+            backs.append(norm_back(d_hat2 * gain2, hat2, scale2, 0))
+        yield
+        for group, i in enumerate((p, p + lines)):
+            part = slice(group * wide, (group + 1) * wide)
+            lay[pl.ds(i, channels, stride=rows), :] = jnp.concatenate(
+                [back[:, part] for back in backs], axis=1
+            )
+        return tiles, (low[1], high[1]), (low[2], high[2])
 
     def finish(results):
-        normed2_t, d_up, bias_rows, normed = zip(*results)
+        tiles, bias_rows, normed = [sum((tuple(one) for one in each), ()) for each in zip(*results)]
         grad_out[:channels] += mm(
-            jnp.concatenate(normed2_t, axis=1), jnp.concatenate(d_up, axis=0)
+            jnp.concatenate([one[0] for one in tiles], axis=1),
+            jnp.concatenate([one[1] for one in tiles], axis=0),
         )
         grad_out[channels:] += mm(
             jnp.concatenate(bias_rows, axis=1), jnp.concatenate(normed, axis=0)
         )
 
-    over_rows(rows, W_MIDDLE, row, finish)
+    over_rows(lines, W_MIDDLE // 2, two_rows, finish)
     departures = [
         pltpu.make_async_copy(d_middle_out, d_middle_any, row_sems.at[0]),
         pltpu.make_async_copy(d_gate_out, d_gate_any, row_sems.at[1]),
@@ -604,13 +674,12 @@
         (source == lax.broadcasted_iota(jnp.int32, (length, length), 1)).astype(F32).astype(BF16)
     )
 
-    def group(g, carry):
+    def group(g):
         block = lay[pl.ds(g * length, length), :].astype(BF16)
         d_product_out[pl.ds(g * length, length), :] = block
         turned = mmt(shuffled, block).astype(BF16)
         for offset in range(count):
             send_outs[offset][g] = turned[offset * rows : (offset + 1) * rows]
-        return carry
 
     parts = 4
     copies = [split_copies(d_product_out, d_product_any, product_sems, parts)] + [
@@ -619,7 +688,7 @@
     ]
     share = channels * rows // length // parts
     for part in range(parts):
-        lax.fori_loop(part * share, (part + 1) * share, group, 0, unroll=4)
+        side_by_side(part * share, (part + 1) * share, group)
         start([one[part] for one in copies])
     for one in copies:
         wait(one)
@@ -634,14 +703,27 @@
 
 
 def left_back_kernel(
-    right_any, d_product_any, normed1_any, factors_any, d_gate_any, grad_middle, *refs
+    near_any, other_any, d_product_any, normed1_any, factors_any, d_gate_any, grad_middle, input_w, gating, *refs
 ):
-    d_projected_any, packed, lay, grad, d_projected_out, sems = refs[:6]
+    d_normed_any, packed, lay, grad, d_normed, sems = refs[:6]
     right_all, d_product, normed1, factors, d_gate, right_sems, product_sems, in_sems = refs[6:]
     rows, length, channels = normed1.shape
     parts = 4
+    share = channels // parts
+    wide = length // 2
+    chip = lax.axis_index("dap") // (lax.axis_size("dap") // 2)
+    spans = [pl.ds(pl.multiple_of((chip ^ side) * wide, wide), wide) for side in range(2)]
     first_arrivals = [
-        split_copies(right_any, right_all, right_sems, parts),
+        [
+            pltpu.make_async_copy(
+                ref.at[pl.ds(part * share, share)],
+                right_all.at[pl.ds(part * share, share), span, :],
+                right_sems.at[side, part],
+            )
+            for part in range(parts)
+        ]
+        for side, (ref, span) in enumerate(zip((near_any, other_any), spans))
+    ] + [
         split_copies(d_product_any, d_product, product_sems, parts),
     ]
     for part in range(parts):
@@ -653,27 +735,25 @@
     ]
     start(arrivals)
 
-    def channel(c, carry):
+    def channel(c):
         lay[pl.ds(c, rows, stride=channels), :] = mm(
             d_product[pl.ds(c * rows, rows), :], right_all[c]
         )
-        return carry
-
-    share = channels // parts
+
     for part in range(parts):
         wait([copies[part] for copies in first_arrivals])
-        lax.fori_loop(part * share, (part + 1) * share, channel, 0, unroll=8)
+        side_by_side(part * share, (part + 1) * share, channel)
     wait(arrivals)
-    eye = identity(channels)
+    weight = jnp.concatenate([input_w[:, : 2 * channels], gating[...]], axis=1)
     grad[...] = jnp.zeros_like(grad)
 
     def row(i):
         normed = normed1[i]
-        d_gate_t = mmt(eye, d_gate[i]).astype(BF16)
+        d_gate_t = d_gate[i].T
         d_projected = gate_back(factors[i], lay[pl.ds(i * channels, channels), :])
         yield
         d_projected = jnp.concatenate([d_projected, d_gate_t], axis=0)
-        d_projected_out[i] = d_projected
+        d_normed[i] = mm(weight, d_projected)
         return d_projected, normed
 
     def finish(results):
@@ -681,7 +761,7 @@
         grad[...] += mm(jnp.concatenate(d_projected, axis=1), jnp.concatenate(normed, axis=0))
 
     parts = 4
-    departures = split_copies(d_projected_out, d_projected_any, sems, parts)
+    departures = split_copies(d_normed, d_normed_any, sems, parts)
     for part in range(parts):
         over_rows(rows // parts, 8, row, finish, first=part * (rows // parts))
         departures[part].start()
@@ -711,10 +791,9 @@
     )
     mask = same.astype(F32).astype(BF16)
 
-    half = channels // per // 2
-    for part, left_blocks in enumerate(left_halves):
-
-        def group(g, carry, left_blocks=left_blocks, first=part * half):
+    for left_blocks, first in zip(left_halves, (0, left_halves[0][0].shape[0] // per)):
+
+        def group(g, left_blocks=left_blocks, first=first):
             at = first + g
             spread = jnp.concatenate(
                 [jnp.concatenate([ref[at]] * per, axis=0) * mask for ref in arrived], axis=1
@@ -723,9 +802,8 @@
                 [ref[pl.ds(g * per, per)].reshape(length, length) for ref in left_blocks], axis=0
             )
             lay[pl.ds(at * length, length), :] = mm(spread, lefts)
-            return carry
-
-        lax.fori_loop(0, half, group, 0, unroll=4)
+
+        side_by_side(0, left_blocks[0].shape[0] // per, group)
     wait(arrivals)
     grad[...] = jnp.zeros_like(grad)
 
@@ -761,7 +839,7 @@
 
 def input_back_kernel(part, parts, *refs):
     sources = refs[:4]
-    gain_col, input_w, gating = refs[4:7]
+    gain_col, input_w = refs[4:6]
     pair_grad_any = refs[-8]
     d_left, d_right, pair, d_middle, pair_grad, sems, out_sem = refs[-7:]
     rows, length, channels = pair.shape
@@ -771,17 +849,14 @@
         for at, (source, target) in enumerate(zip(sources, (d_left, d_right, pair, d_middle)))
     ]
     start(arrivals)
-    eye = identity(channels)
-    weight = jnp.concatenate(
-        [input_w[:, : 2 * channels], gating[...], input_w[:, 2 * channels :]], axis=1
-    )
+    weight = input_w[:, 2 * channels :]
     gain = jnp.broadcast_to(gain_col[...], (channels, length))
 
     def row(i):
-        hat, scale = norm_parts(mmt(eye, pair[i]), 0)
-        d_normed = mm(weight, jnp.concatenate([d_left[i], d_right[i]], axis=0))
-        yield
-        d_pair = mmt(eye, norm_back(d_normed * gain, hat, scale, 0).astype(BF16))
+        hat, scale = norm_parts(pair[i].T.astype(F32), 0)
+        d_normed = d_left[i] + mm(weight, d_right[i])
+        yield
+        d_pair = norm_back(d_normed * gain, hat, scale, 0).astype(BF16).T.astype(F32)
         yield
         pair_grad[i] = (d_middle[i].astype(F32) + d_pair).astype(BF16)
 
@@ -837,7 +912,7 @@
     input1_out[...] = input1_t.T
     gating_out[...] = gating_t.T
     output1_out[...] = output1_grad
-    bias_out[...] = bias_t.T[:, :heads]
+    bias_out[...] = bias_t[:heads]
     input3_out[...] = input3_t.T
     output3_out[...] = output3
     for h in range(heads):
@@ -854,8 +929,12 @@
 
 
 def gather_near(block, far, axis):
+    return near_blocks(block, axis) + near_blocks(far, axis)
+
+
+def near_blocks(block, axis):
     half = lax.axis_size(axis) // 2
-    blocks = {0: block, half: far}
+    blocks = {0: block}
     for bit in reversed(range(half.bit_length() - 1)):
         step = 1 << bit
         for offset, held in list(blocks.items()):
@@ -907,17 +986,20 @@
     turned = (rows, channels, length)
 
     half = rows // 2
-    normed1_halves, right_halves, live_halves = [], [], []
+    normed1, right_halves, live_halves = None, [], []
     for part in range(2):
-        normed_part, right_part, live_part = call(
+        given = [] if normed1 is None else [normed1]
+        normed1, right_part, live_part = call(
             partial(right_kernel, part),
             [
-                ((half, length, channels), BF16),
+                (cells, BF16),
                 ((channels, half, length), BF16),
                 ((half, length), F32),
             ],
-            [slab, pair_mask[0], tok_mask, gain1_row, triangle_input],
-            in_specs=[anywhere] * 5,
+            [slab, pair_mask[0], tok_mask, gain1_row, triangle_input, *given],
+            in_specs=[anywhere] * (5 + len(given)),
+            out_specs=[anywhere, vmem, vmem],
+            aliases={5: 0} if given else None,
             scratch=[
                 pltpu.VMEM((half, length, channels), BF16),
                 pltpu.VMEM((half, length), jnp.int32),
@@ -926,32 +1008,35 @@
                 pltpu.VMEM((channels, 4 * channels), BF16),
                 pltpu.VMEM((2 * channels, channels), BF16),
                 pltpu.VMEM((channels * half, length), F32),
-                pltpu.SemaphoreType.DMA((5,)),
+                pltpu.VMEM((half, length, channels), BF16),
+                pltpu.SemaphoreType.DMA((6,)),
             ],
             us=3.0,
             name="right_projection",
         )
-        normed1_halves.append(normed_part)
         right_halves.append(right_part)
         live_halves.append(live_part)
-    normed1, left_low, left_high, gate, live, left_factors = call(
+    low_count = 5 * channels // 16
+    left_low, left_high, gate, live, left_factors = call(
         partial(left_kernel, 2),
         [
-            (cells, BF16),
-            ((channels // 2, rows, length), BF16),
-            ((channels // 2, rows, length), BF16),
+            ((low_count, rows, length), BF16),
+            ((channels - low_count, rows, length), BF16),
             (cells, F32),
             ((rows, length), F32),
             ((rows, 2 * channels, length), BF16),
         ],
-        [*normed1_halves, *live_halves, triangle_input, triangle_gating],
-        out_specs=[anywhere, vmem, vmem, anywhere, vmem, anywhere],
+        [normed1, *live_halves, triangle_input, triangle_gating],
+        in_specs=[anywhere] + [vmem] * 4,
+        out_specs=[vmem, vmem, anywhere, vmem, anywhere],
         scratch=[
             pltpu.VMEM((2 * channels, channels), BF16),
             pltpu.VMEM((channels * rows, length), F32),
             pltpu.VMEM(cells, F32),
             pltpu.VMEM((rows, 2 * channels, length), BF16),
-            pltpu.SemaphoreType.DMA((3, 2)),
+            cell_buffer,
+            pltpu.SemaphoreType.DMA((2,)),
+            pltpu.SemaphoreType.DMA((2, 2)),
         ],
         us=6.0,
         name="left_projection",
@@ -961,58 +1046,78 @@
     right_factors, d_gated = call(
         partial(factor_kernel, 2),
         [((rows, 2 * channels, length), BF16), (cells, BF16)],
-        [*normed1_halves, live, triangle_input, attend_output, cot],
-        in_specs=[vmem] * 5 + [anywhere],
+        [live, triangle_input, attend_output, normed1, cot],
+        in_specs=[vmem] * 3 + [anywhere] * 2,
         out_specs=[anywhere] * 2,
         scratch=[
             cell_buffer,
+            cell_buffer,
             pltpu.VMEM((rows, 2 * channels, length), BF16),
             cell_buffer,
-            pltpu.SemaphoreType.DMA((2,)),
+            pltpu.SemaphoreType.DMA((2, 2)),
             pltpu.SemaphoreType.DMA((2, 2)),
         ],
         us=5.0,
         name="right_factors",
     )
-    right_factors, far[1] = lax.optimization_barrier((right_factors, far[1]))
+    lines, wide = rows // 2, length // 2
+
+    def product_side(side, halves, given=()):
+        blocks = [halves[index % 2][index // 2] for index in range(count)]
+        return call(
+            partial(product_kernel, count, side),
+            [
+                ((2, lines, channels, length), BF16),
+                (cells, BF16),
+                (cells, BF16),
+                (cells, BF16),
+                ((channels, wide, length), BF16),
+                ((lines, length), F32),
+                ((rows, heads * length), BF16) if side else ((lines * HEAD_ROWS, length), F32),
+            ],
+            [*blocks, left_low, left_high, slab, gate, gain2_col, gain3_row]
+            + [triangle_output, attend_bias, *given],
+            in_specs=[vmem] * (count + 2)
+            + [anywhere] * 2
+            + [vmem] * 4
+            + [anywhere] * (5 if side else 0),
+            out_specs=[anywhere] * 5 + [vmem, vmem if side else anywhere],
+            scratch=[
+                pltpu.VMEM((lines * channels, length), F32),
+                pltpu.VMEM((lines * HEAD_ROWS, length), F32),
+                pltpu.VMEM((channels, wide, length), BF16),
+                pltpu.VMEM((rows, wide, channels), BF16),
+                pltpu.VMEM((rows, wide, channels), F32),
+                pltpu.VMEM((lines, channels, length), BF16),
+            ]
+            + [pltpu.VMEM((rows, wide, channels), BF16)] * 3
+            + [
+                pltpu.SemaphoreType.DMA((2,)),
+                pltpu.SemaphoreType.DMA((4, 4)),
+                pltpu.SemaphoreType.DMA,
+                pltpu.SemaphoreType.DMA,
+                pltpu.VMEM((lines * HEAD_ROWS, length), F32),
+            ],
+            aliases={count + 9 + at: at for at in range(4)} if side else None,
+            us=7.0,
+            name="product_other" if side else "product_near",
+        )
+
+    *shared, right_near, scale2_near, bias_near = product_side(
+        0, [near_blocks(part, "dap") for part in right_halves]
+    )
+    shared[0], d_gated, far[1] = lax.optimization_barrier((shared[0], d_gated, far[1]))
     left_low_sent, _ = lax.optimization_barrier((left_low, far[1]))
     low_far = swap(left_low_sent, "dap", count // 2)
-    right_halves = [
-        gather_near(part, other, "dap") for part, other in zip(right_halves, far)
-    ]
-    right_blocks = [right_halves[index % 2][index // 2] for index in range(2 * count)]
-    normed2, update, middle, normed3, right_all, scale2, bias_rows = call(
-        partial(product_kernel, count),
-        [
-            (turned, BF16),
-            (cells, BF16),
-            (cells, BF16),
-            (cells, BF16),
-            ((channels, length, length), BF16),
-            ((rows, length), F32),
-            ((rows, heads * length), BF16),
-        ],
-        [*right_blocks, left_low, left_high, slab, gate, gain2_col, gain3_row, triangle_output, attend_bias],
-        in_specs=[vmem] * (2 * count + 2) + [anywhere] * 2 + [vmem] * 4,
-        out_specs=[anywhere] * 5 + [vmem] * 2,
-        scratch=[
-            pltpu.VMEM((rows * channels, length), F32),
-            pltpu.VMEM((rows * HEAD_ROWS, length), F32),
-            pltpu.VMEM((channels, length, length), BF16),
-        ]
-        + [cell_buffer, pltpu.VMEM(cells, F32)]
-        + [pltpu.VMEM(turned, BF16)]
-        + [cell_buffer] * 3
-        + [
-            pltpu.SemaphoreType.DMA((2,)),
-            pltpu.SemaphoreType.DMA((4, 4)),
-            pltpu.SemaphoreType.DMA,
-        ],
-        us=14.0,
-        name="product_and_norms",
-    )
+    *shared, right_other, scale2_other, bias_rows = product_side(
+        1, [near_blocks(part, "dap") for part in far], [bias_near, *shared]
+    )
+    normed2, update, middle, normed3 = shared
+    right_sides = [right_near, right_other]
     normed3, low_far = lax.optimization_barrier((normed3, low_far))
-    bias_far = swap(bias_rows, "dap", count // 2)
+    bias_blocks = [bias_rows] + [
+        swap(bias_rows, "dap", offset) for offset in reversed(range(1, count))
+    ][::-1]
 
     block = 8
     steps = rows // block
@@ -1043,9 +1148,8 @@
         us=5.0,
         name="attention_projections",
     )
-    projected3, bias_far = lax.optimization_barrier((projected3, bias_far))
-    bias_blocks = gather_near(bias_rows, bias_far, "dap")
-    left_high_sent, _ = lax.optimization_barrier((left_high, bias_far))
+    projected3, *bias_blocks = lax.optimization_barrier((projected3, *bias_blocks))
+    left_high_sent, _ = lax.optimization_barrier((left_high, bias_blocks[-1]))
     high_far = swap(left_high_sent, "dap", count // 2)
     attend_outs = call(
         partial(attend_kernel, count),
@@ -1077,10 +1181,10 @@
         name="attention",
     )
     pair_out, d_projected3, d_output, d_table = attend_outs[:4]
-    d_table, high_far = lax.optimization_barrier((d_table, high_far))
     d_bias_parts = [attend_outs[4]] + [
         swap(attend_outs[4 + offset], "dap", offset) for offset in range(1, count)
     ]
+    d_bias_parts[1], high_far = lax.optimization_barrier((d_bias_parts[1], high_far))
     d_normed3, packed_a = call(
         projection_kernel,
         [(turned, F32), ((4 * channels + channels + 2 * HEAD_ROWS, channels), BF16)],
@@ -1093,7 +1197,7 @@
             fixed(5 * channels + 2 * HEAD_ROWS, channels),
         ],
         scratch=[pltpu.VMEM((4 * channels, channels), F32)],
-        us=6.0,
+        us=0.5,
         name="projection_back",
     )
     groups = channels * rows // length
@@ -1107,7 +1211,7 @@
         ]
         + [((groups, rows, length), BF16)] * count,
         [*d_bias_parts, d_normed3, normed3, middle, cot, gain3_col, attend_bias]
-        + [normed2, scale2, update, gate, gain2_col, triangle_output],
+        + [normed2, scale2_near, scale2_other, update, gate, gain2_col, triangle_output],
         out_specs=[anywhere] * 3 + [vmem] + [anywhere] * count,
         scratch=[
             pltpu.VMEM((rows * HEAD_ROWS, length), F32),
@@ -1133,23 +1237,24 @@
     ]
     d_left, packed_b = call(
         left_back_kernel,
-        [((rows, 3 * channels, length), BF16), ((4 * channels + HEAD_ROWS, channels), BF16)],
-        [right_all, d_product, normed1, left_factors, d_gate, grad_middle],
+        [(turned, F32), ((4 * channels + HEAD_ROWS, channels), BF16)],
+        [*right_sides, d_product, normed1, left_factors, d_gate, grad_middle]
+        + [triangle_input, triangle_gating],
         scratch=[
             pltpu.VMEM((rows * channels, length), F32),
             pltpu.VMEM((3 * channels, channels), F32),
-            pltpu.VMEM((rows, 3 * channels, length), BF16),
+            pltpu.VMEM(turned, F32),
             pltpu.SemaphoreType.DMA((4,)),
             pltpu.VMEM((channels, length, length), BF16),
             pltpu.VMEM((channels * rows, length), BF16),
             cell_buffer,
             pltpu.VMEM((rows, 2 * channels, length), BF16),
             cell_buffer,
-            pltpu.SemaphoreType.DMA((4,)),
+            pltpu.SemaphoreType.DMA((2, 4)),
             pltpu.SemaphoreType.DMA((4,)),
             pltpu.SemaphoreType.DMA((3,)),
         ],
-        in_specs=[anywhere] * 5 + [vmem],
+        in_specs=[anywhere] * 6 + [vmem] * 3,
         out_specs=[anywhere, vmem],
         us=10.0,
         name="left_back",
@@ -1185,11 +1290,11 @@
         (pair_grad,) = call(
             partial(input_back_kernel, part, parts),
             [(cells, BF16)],
-            [d_left, d_right, slab, d_middle, gain1_col, triangle_input, triangle_gating, *given],
-            in_specs=[anywhere] * 4 + [vmem] * 3 + [anywhere] * len(given),
+            [d_left, d_right, slab, d_middle, gain1_col, triangle_input, *given],
+            in_specs=[anywhere] * 4 + [vmem] * 2 + [anywhere] * len(given),
             out_specs=[anywhere],
             scratch=[
-                pltpu.VMEM((rows // parts, 3 * channels, length), BF16),
+                pltpu.VMEM((rows // parts, channels, length), F32),
                 pltpu.VMEM((rows // parts, 2 * channels, length), BF16),
                 pltpu.VMEM(some, BF16),
                 pltpu.VMEM(some, BF16),
@@ -1197,32 +1302,38 @@
                 pltpu.SemaphoreType.DMA((4,)),
                 pltpu.SemaphoreType.DMA,
             ],
-            aliases={7: 0} if given else None,
+            aliases={6: 0} if given else None,
             us=3.0,
             name="input_back",
         )
         return pair_grad
 
-    grad_share = right_outs[1].astype(F32)
-    for offset in range(1, count):
-        grad_share = grad_share + swap(right_outs[1 + offset], "dap", offset).astype(F32)
-    grad_share = grad_share.astype(BF16)
+    shares = dict(enumerate(right_outs[1:]))
+    step = 1
     done = 0
+    while step < count:
+        if 2 * step == count:
+            pair_grad = input_back(done, pair_grad)
+            done += 1
+        for offset in [one for one in shares if one & step]:
+            arrived = swap(shares.pop(offset), "dap", step)
+            shares[offset ^ step] = shares[offset ^ step] + arrived
+        step *= 2
+    grad_share, pair_grad = lax.optimization_barrier((shares[0], pair_grad))
     step = 1
     while step < lax.axis_size("dp"):
-        if done < parts - 1:
+        if step > 1 and done < parts - 1:
             pair_grad = input_back(done, pair_grad)
             grad_share, pair_grad = lax.optimization_barrier((grad_share, pair_grad))
             done += 1
         grad_share = grad_share + swap(grad_share, "dp", step)
         step *= 2
-    grad_blocks = [grad_share] + [
-        swap(grad_share, "dap", offset) for offset in range(1, count)
-    ]
+    grad_far = swap(grad_share, "dap", count // 2)
     while done < parts:
         pair_grad = input_back(done, pair_grad)
         done += 1
-    pair_grad, *grad_blocks = lax.optimization_barrier((pair_grad, *grad_blocks))
+    pair_grad, grad_far = lax.optimization_barrier((pair_grad, grad_far))
+    grad_blocks = gather_near(grad_share, grad_far, "dap")
     weights = (triangle_input, triangle_gating, triangle_output, attend_bias, attend_input)
     gains = (gain1_row, product_gain[None, :], gain3_row)
     grads = call(
@@ -1234,7 +1345,7 @@
             ((1, channels), F32),
             (triangle_output.shape, F32),
             ((1, channels), F32),
-            (attend_bias.shape, F32),
+            (attend_bias.shape[::-1], F32),
             (attend_input.shape, F32),
             (attend_output.shape, F32),
             (type_table.shape, F32),
@@ -1245,6 +1356,7 @@
         name="scale_gradients",
     )
     grads = [grad[0] if grad.shape[0] == 1 else grad for grad in grads]
+    grads[6] = grads[6].T
     return (pair_out[None], pair_grad[None], *grads)
 
 

time: 134 us -> 126 us (0.940)
  waiting for transfers between devices: 23.5 us -> 15.7 us
    ppermute x30, waiting for transfers between devices: 23.5 us -> 15.7 us  [swap(): lax.ppermute(value, axis, [(index, index ^ step) for index in range(count)])]
    pallas_call x16 -> x17, Pallas kernels: 84.7 us -> 83.8 us  [call(): pl.pallas_call(kernel, out_shape=[pltpu.HBM(shape, dtype) if spec.memory_...]
  transfers between devices with their start and end apart: 30 -> 30, of which waited for: 11 -> 13; matrix products, arithmetic and copies ran while one was open for 0% -> 0% of each run, Pallas kernels for 56% -> 59%
where the time goes in v2:
time: 126 us
  Pallas kernels  83.8 us (67%)
  starting transfers between devices  23.5 us (19%)
  waiting for transfers between devices  15.7 us (12%)
  local copies, waits for them, and re-layouts  1.69 us (1%)
    pallas_call x17, Pallas kernels, call(): pl.pallas_call(kernel, out_shape=[pltpu.HBM(shape, dtype) if spec.memory_...  83.8 us
    ppermute x30, starting transfers between devices, swap(): lax.ppermute(value, axis, [(index, index ^ step) for index in range(count)])  23.5 us
    ppermute x30, waiting for transfers between devices, swap(): lax.ppermute(value, axis, [(index, index ^ step) for index in range(count)])  15.7 us
  transfers between devices with their start and end apart: 30, of which 13 were waited for; matrix products, arithmetic and copies ran while one was open for 0% of the time, Pallas kernels for 59%

profile of v2, /device:TPU:0, one launch (start us, length us, event | category | flops | bytes accessed | tf_op | source)
XLA Modules:
  0.0 126.0 jit_solution(8639633048115954356)
XLA Ops:
  0.6 3.3 %right_projection.2 = (bf16[32,128,128]{2,1,0:T(8,128)(2,1)}, bf16[128,16,128]{2,1,0:T(8,128)(2,1)S(1)}, f32[16,128]{1,0:T(8,128)S(1)}) custom-call(bf16[32,128,128]{2,1,0:T(8,128)(2,1)} %bitcast.32, s32[32,128]{1,0:T(8,128)} %bitcast.40, s32[1,128]{1,0:T(1,128)} %tokens_any.3, f32[1,128]{1,0:T(1,128)} %bitcast.18, bf16[128,512]{1,0:T(8,128)(2,1)} %refs_4_.3), custom_call_target="tpu_custom_call" | custom-call | flops 3000000000 | bytes 9000000 | tf_op jit(solution)/shard_map/right_projection/pallas_call | solution.py:109
  4.5 2.6 %collective-permute-start = (bf16[128,16,128]{2,1,0:T(8,128)(2,1)S(1)}, bf16[128,16,128]{2,1,0:T(8,128)(2,1)S(1)}, u32[]{:S(2)}, u32[]{:S(2)}) collective-permute-start(bf16[128,16,128]{2,1,0:T(8,128)(2,1)S(1)} %get-tuple-element.109.refs_0_), channel_id=1, source_target_pairs={{0,16},{8,24},{16,0},{24,8},{1,17},{9,25},{17,1},{25,9},{2,18},{10... | collective-permute-start | bytes 1572872 | tf_op jit(solution)/shard_map/ppermute | solution.py:924
  7.1 3.4 %right_projection.3 = (bf16[32,128,128]{2,1,0:T(8,128)(2,1)}, bf16[128,16,128]{2,1,0:T(8,128)(2,1)S(1)}, f32[16,128]{1,0:T(8,128)S(1)}) custom-call(bf16[32,128,128]{2,1,0:T(8,128)(2,1)} %bitcast.33, s32[32,128]{1,0:T(8,128)} %bitcast.41, s32[1,128]{1,0:T(1,128)} %tokens_any.3, f32[1,128]{1,0:T(1,128)} %bitcast.19, ...), custom_call_target="tpu_custom_call", output_to_operand_aliasing={{0}: (5, {})} | custom-call | flops 3000000000 | bytes 9000000 | tf_op jit(solution)/shard_map/right_projection/pallas_call | solution.py:109
  11.3 5.9 %left_projection.1 = (bf16[40,32,128]{2,1,0:T(8,128)(2,1)S(1)}, bf16[88,32,128]{2,1,0:T(8,128)(2,1)S(1)}, f32[32,128,128]{2,1,0:T(8,128)}, f32[32,128]{1,0:T(8,128)S(1)}, bf16[32,256,128]{2,1,0:T(8,128)(2,1)}) custom-call(bf16[32,128,128]{2,1,0:T(8,128)(2,1)} %get-tuple-element.105.normed_any.refs_3_.normed1_any.refs_12_, ...), custom_call_target="tpu_custom_call" | custom-call | flops 6000000000 | bytes 18000000 | tf_op jit(solution)/shard_map/left_projection/pallas_call | solution.py:109
  17.2 6.6 %product_near.1 = (bf16[2,16,128,128]{3,2,1,0:T(8,128)(2,1)}, bf16[32,128,128]{2,1,0:T(8,128)(2,1)}, bf16[32,128,128]{2,1,0:T(8,128)(2,1)}, bf16[32,128,128]{2,1...) custom-call(bf16[128,16,128]{2,1,0:T(8,128)(2,1)S(1)} %get-tuple-element.109.refs_0_, ...), custom_call_target="tpu_custom_call" | custom-call | flops 7000000000 | bytes 21000000 | tf_op jit(solution)/shard_map/product_near/pallas_call | solution.py:109
  23.9 4.5 %right_factors.1 = (bf16[32,256,128]{2,1,0:T(8,128)(2,1)}, bf16[32,128,128]{2,1,0:T(8,128)(2,1)}) custom-call(f32[32,128]{1,0:T(8,128)S(1)} %get-tuple-element.116.refs_0_.refs_6_, bf16[128,512]{1,0:T(8,128)(2,1)S(1)} %copy-done.10, bf16[128,128]{1,0:T(8,128)(2,1)S(1)} %copy-done.11, ...), custom_call_target="tpu_custom_call" | custom-call | flops 5000000000 | bytes 15000000 | tf_op jit(solution)/shard_map/right_factors/pallas_call | solution.py:109
  28.4 2.4 %collective-permute-done.3.refs_1_ = bf16[128,16,128]{2,1,0:T(8,128)(2,1)S(1)} collective-permute-done((bf16[128,16,128]{2,1,0:T(8,128)(2,1)S(1)}, bf16[128,16,128]{2,1,0:T(8,128)(2,1)S(1)}, u32[]{:S(2)}, u32[]{:S(2)}) %collective-permute-start.3) | collective-permute-done | bytes 524320 | tf_op jit(solution)/shard_map/ppermute | solution.py:924
  31.5 1.8 %collective-permute-start.6 = (bf16[40,32,128]{2,1,0:T(8,128)(2,1)}, bf16[40,32,128]{2,1,0:T(8,128)(2,1)S(1)}, u32[]{:S(2)}, u32[]{:S(2)}) collective-permute-start(bf16[40,32,128]{2,1,0:T(8,128)(2,1)} %copy-done.7), channel_id=1, source_target_pairs={{0,16},{8,24},{16,0},{24,8},{1,17},{9,25},{17,1},{25,9},{2,18},{10... | collective-permute-start | bytes 983048 | tf_op jit(solution)/shard_map/ppermute | solution.py:924
  35.0 6.5 %product_other.1 = (bf16[2,16,128,128]{3,2,1,0:T(8,128)(2,1)}, bf16[32,128,128]{2,1,0:T(8,128)(2,1)}, bf16[32,128,128]{2,1,0:T(8,128)(2,1)}, bf16[32,128,128]{2,...) custom-call(bf16[128,16,128]{2,1,0:T(8,128)(2,1)S(1)} %collective-pe, ...), custom_call_target="tpu_custom_call", output_to_operand_aliasing={{0}: (13, {}), {1}: (14, {}), {2}: (15, {}), {3}: (16, {})} | custom-call | flops 7000000000 | bytes 21000000 | tf_op jit(solution)/shard_map/product_other/pallas_call | solution.py:109
  41.9 1.7 %collective-permute-start.8 = (bf16[32,512]{1,0:T(8,128)(2,1)S(1)}, bf16[32,512]{1,0:T(8,128)(2,1)S(1)}, u32[]{:S(2)}, u32[]{:S(2)}) collective-permute-start(bf16[32,512]{1,0:T(8,128)(2,1)S(1)} %get-tuple-element.129.refs_0_), channel_id=1, source_target_pairs={{0,16},{8,24},{16,0},{24,8},{1,17},{9,25},{17,1},{25,9},{2,18},{10... | collective-permute-start | bytes 98312 | tf_op jit(solution)/shard_map/ppermute | solution.py:924
  43.7 4.6 %attention_projections.1 = (bf16[32,384,128]{2,1,0:T(8,128)(2,1)}, bf16[32,128,128]{2,1,0:T(8,128)(2,1)}, f32[32,128,128]{2,1,0:T(8,128)}) custom-call(bf16[32,128,128]{2,1,0:T(8,128)(2,1)} %get-tuple-element.126.normed3_any.normed3.refs_5_, bf16[128,512]{1,0:T(8,128)(2,1)} %refs_8_.1), custom_call_target="tpu_custom_call" | custom-call | flops 5000000000 | bytes 15000000 | tf_op jit(solution)/shard_map/attention_projections/pallas_call | solution.py:109
  49.9 13.9 %attention.1 = (bf16[32,128,128]{2,1,0:T(8,128)(2,1)}, bf16[32,512,128]{2,1,0:T(8,128)(2,1)S(1)}, f32[128,128]{1,0:T(8,128)S(1)}, f32[16,128]{1,0:T(8,128)S(1)},...) custom-call(f32[16,4]{1,0:T(8,128)S(1)} %bitcast.31, ...), custom_call_target="tpu_custom_call" | custom-call | flops 20000000000 | bytes 60000000 | tf_op jit(solution)/shard_map/attention/pallas_call | solution.py:109
  65.8 2.4 %projection_back.1 = (f32[32,128,128]{2,1,0:T(8,128)S(1)}, bf16[672,128]{1,0:T(8,128)(2,1)S(1)}) custom-call(bf16[32,512,128]{2,1,0:T(8,128)(2,1)S(1)} %get-tuple-element.147.d_projected, bf16[32,128,128]{2,1,0:T(8,128)(2,1)S(1)} %copy-done, bf16[128,512]{1,0:T(8,128)(2,1)S(1)} %copy-done.1, f32[128,128]{1,0:T(8,128)S(1)} %get-tuple-element.148.d_output, ...), custom_call_target="tpu_custom_call" | custom-call | flops 500000000 | bytes 1500000 | tf_op jit(solution)/shard_map/projection_back/pallas_call | solution.py:109
  69.0 8.5 %middle_back.1 = (bf16[32,128,128]{2,1,0:T(8,128)(2,1)}, bf16[32,128,128]{2,1,0:T(8,128)(2,1)}, bf16[4096,128]{1,0:T(8,128)(2,1)}, f32[144,128]{1,0:T(8,128)S(1)...) custom-call(f32[32,512]{1,0:T(8,128)S(1)} %get-tuple-element.141.ref, ...), custom_call_target="tpu_custom_call" | custom-call | flops 12000000000 | bytes 36000000 | tf_op jit(solution)/shard_map/middle_back/pallas_call | solution.py:109
  80.0 7.2 %left_back.1 = (f32[32,128,128]{2,1,0:T(8,128)}, bf16[528,128]{1,0:T(8,128)(2,1)S(1)}) custom-call(bf16[128,64,128]{2,1,0:T(8,128)(2,1)} %get-tuple-element.139.near_any, bf16[128,64,128]{2,1,0:T(8,128)(2,1)} %get-tuple-element.140.other_any, bf16[4096,128]{1,0:T(8,128)(2,1)} %get-tuple-element.155.d_product_any, ...), custom_call_target="tpu_custom_call" | custom-call | flops 10000000000 | bytes 30000000 | tf_op jit(solution)/shard_map/left_back/pallas_call | solution.py:109
  87.5 4.7 %collective-permute-done.16.refs_3_ = bf16[32,32,128]{2,1,0:T(8,128)(2,1)S(1)} collective-permute-done((bf16[32,32,128]{2,1,0:T(8,128)(2,1)}, bf16[32,32,128]{2,1,0:T(8,128)(2,1)S(1)}, u32[]{:S(2)}, u32[]{:S(2)}) %collective-permute-start.16) | collective-permute-done | bytes 262176 | tf_op jit(solution)/shard_map/ppermute | solution.py:924
  92.2 5.4 %right_back.1 = (bf16[32,256,128]{2,1,0:T(8,128)(2,1)}, bf16[368,128]{1,0:T(8,128)(2,1)S(1)}, bf16[368,128]{1,0:T(8,128)(2,1)S(1)}, bf16[368,128]{1,0:T(8,128)(2,1)S(1)}, bf16[368,128]{1,0:T(8,128)(2,1)S(1)}) custom-call(bf16[32,32,128]{2,1,0:T(8,128)(2,1)S(1)} %copy-done.22, bf16[32,32,128]{2,1,0:T(8,128)(2,1)S(1)} %collective-permute-done.14.refs_1_, ...), custom_call_target="tpu_custom_call" | custom-call | flops 7000000000 | bytes 21000000 | tf_op jit(solution)/shard_map/right_back/pallas_call | solution.py:109
  100.1 2.6 %input_back.4.refs_6_ = bf16[32,128,128]{2,1,0:T(8,128)(2,1)} custom-call(f32[32,128,128]{2,1,0:T(8,128)} %get-tuple-element.159.refs_0_, bf16[32,256,128]{2,1,0:T(8,128)(2,1)} %get-tuple-element.172.refs_1_, bf16[32,128,128]{2,1,0:T(8,128)(2,1)} %bitcast.36, bf16[32,128,128]{2,1,0:T(8,128)(2,1)} %get-tuple-element.173.refs_3_, f32[128,1]{1,0:T(8,128)S(1)} %copy.48.refs_4_, ...), custom_call_target="tpu_custom_call" | custom-call | flops 3000000000 | bytes 9000000 | tf_op jit(solution)/shard_map/input_back/pallas_call | solution.py:109
  105.6 2.6 %input_back.5.refs_6_ = bf16[32,128,128]{2,1,0:T(8,128)(2,1)} custom-call(f32[32,128,128]{2,1,0:T(8,128)} %get-tuple-element.159.refs_0_, bf16[32,256,128]{2,1,0:T(8,128)(2,1)} %get-tuple-element.172.refs_1_, bf16[32,128,128]{2,1,0:T(8,128)(2,1)} %bitcast.37, bf16[32,128,128]{2,1,0:T(8,128)(2,1)} %get-tuple-element.173.refs_3_, ...), custom_call_target="tpu_custom_call", output_to_operand_aliasing={{}: (6, {})} | custom-call | flops 3000000000 | bytes 9000000 | tf_op jit(solution)/shard_map/input_back/pallas_call | solution.py:109
  108.6 1.6 %collective-permute-start.25 = (bf16[368,128]{1,0:T(8,128)(2,1)S(1)}, bf16[368,128]{1,0:T(8,128)(2,1)S(1)}, u32[]{:S(2)}, u32[]{:S(2)}) collective-permute-start(bf16[368,128]{1,0:T(8,128)(2,1)S(1)} %add.21), channel_id=1, source_target_pairs={{0,2},{1,3},{2,0},{3,1},{4,6},{5,7},{6,4},{7,5},{8,10},{9,11},{10,... | collective-permute-start | bytes 282632 | tf_op jit(solution)/shard_map/ppermute | solution.py:924
  110.3 2.6 %input_back.6.refs_6_ = bf16[32,128,128]{2,1,0:T(8,128)(2,1)} custom-call(f32[32,128,128]{2,1,0:T(8,128)} %get-tuple-element.159.refs_0_, bf16[32,256,128]{2,1,0:T(8,128)(2,1)} %get-tuple-element.172.refs_1_, bf16[32,128,128]{2,1,0:T(8,128)(2,1)} %bitcast.38, bf16[32,128,128]{2,1,0:T(8,128)(2,1)} %get-tuple-element.173.refs_3_, ...), custom_call_target="tpu_custom_call", output_to_operand_aliasing={{}: (6, {})} | custom-call | flops 3000000000 | bytes 9000000 | tf_op jit(solution)/shard_map/input_back/pallas_call | solution.py:109
  113.3 2.7 %collective-permute-start.26 = (bf16[368,128]{1,0:T(8,128)(2,1)S(1)}, bf16[368,128]{1,0:T(8,128)(2,1)S(1)}, u32[]{:S(2)}, u32[]{:S(2)}) collective-permute-start(bf16[368,128]{1,0:T(8,128)(2,1)S(1)} %add.22), channel_id=1, source_target_pairs={{0,4},{1,5},{2,6},{3,7},{4,0},{5,1},{6,2},{7,3},{8,12},{9,13},{10,... | collective-permute-start | bytes 282632 | tf_op jit(solution)/shard_map/ppermute | solution.py:924
  116.0 2.9 %collective-permute-done.26 = bf16[368,128]{1,0:T(8,128)(2,1)S(1)} collective-permute-done((bf16[368,128]{1,0:T(8,128)(2,1)S(1)}, bf16[368,128]{1,0:T(8,128)(2,1)S(1)}, u32[]{:S(2)}, u32[]{:S(2)}) %collective-permute-start.26) | collective-permute-done | bytes 94240 | tf_op jit(solution)/shard_map/ppermute | solution.py:924
  120.0 2.6 %input_back.7 = bf16[32,128,128]{2,1,0:T(8,128)(2,1)} custom-call(f32[32,128,128]{2,1,0:T(8,128)} %get-tuple-element.159.refs_0_, bf16[32,256,128]{2,1,0:T(8,128)(2,1)} %get-tuple-element.172.refs_1_, bf16[32,128,128]{2,1,0:T(8,128)(2,1)} %bitcast.39, bf16[32,128,128]{2,1,0:T(8,128)(2,1)} %get-tuple-element.173.refs_3_, ...), custom_call_target="tpu_custom_call", output_to_operand_aliasing={{}: (6, {})} | custom-call | flops 3000000000 | bytes 9000000 | tf_op jit(solution)/shard_map/input_back/pallas_call | solution.py:109
  (119 shorter events, 21.7 us)
Async XLA Ops:
  4.0 13.2 %collective-permute-start.1 = (bf16[128,16,128]{2,1,0:T(8,128)(2,1)S(1)}, bf16[128,16,128]{2,1,0:T(8,128)(2,1)}, u32[]{:S(2)}, u32[]{:S(2)}) collective-permute-start(bf16[128,16,128]{2,1,0:T(8,128)(2,1)S(1)} %get-tuple-element.109.refs_0_), channel_id=1, source_target_pairs={{0,8},{8,0},{16,24},{24,16},{1,9},{9,1},{17,25},{25,17},{2,10},{10... | collective-permute-start | bytes 1572872 | tf_op jit(solution)/shard_map/ppermute | solution.py:924
  4.5 19.3 %collective-permute-start = (bf16[128,16,128]{2,1,0:T(8,128)(2,1)S(1)}, bf16[128,16,128]{2,1,0:T(8,128)(2,1)S(1)}, u32[]{:S(2)}, u32[]{:S(2)}) collective-permute-start(bf16[128,16,128]{2,1,0:T(8,128)(2,1)S(1)} %get-tuple-element.109.refs_0_), channel_id=1, source_target_pairs={{0,16},{8,24},{16,0},{24,8},{1,17},{9,25},{17,1},{25,9},{2,18},{10... | collective-permute-start | bytes 1572872 | tf_op jit(solution)/shard_map/ppermute | solution.py:924
  10.5 6.7 %collective-permute-start.2 = (bf16[128,16,128]{2,1,0:T(8,128)(2,1)S(1)}, bf16[128,16,128]{2,1,0:T(8,128)(2,1)}, u32[]{:S(2)}, u32[]{:S(2)}) collective-permute-start(bf16[128,16,128]{2,1,0:T(8,128)(2,1)S(1)} %get-tuple-element.111.refs_1_), channel_id=1, source_target_pairs={{0,8},{8,0},{16,24},{24,16},{1,9},{9,1},{17,25},{25,17},{2,10},{10... | collective-permute-start | bytes 1572872 | tf_op jit(solution)/shard_map/ppermute | solution.py:924
  10.7 20.1 %collective-permute-start.3 = (bf16[128,16,128]{2,1,0:T(8,128)(2,1)S(1)}, bf16[128,16,128]{2,1,0:T(8,128)(2,1)S(1)}, u32[]{:S(2)}, u32[]{:S(2)}) collective-permute-start(bf16[128,16,128]{2,1,0:T(8,128)(2,1)S(1)} %get-tuple-element.111.refs_1_), channel_id=1, source_target_pairs={{0,16},{8,24},{16,0},{24,8},{1,17},{9,25},{17,1},{25,9},{2,18},{10... | collective-permute-start | bytes 1572872 | tf_op jit(solution)/shard_map/ppermute | solution.py:924
  31.3 47.9 %collective-permute-start.19 = (bf16[88,32,128]{2,1,0:T(8,128)(2,1)S(1)}, bf16[88,32,128]{2,1,0:T(8,128)(2,1)S(1)}, u32[]{:S(2)}, u32[]{:S(2)}) collective-permute-start(bf16[88,32,128]{2,1,0:T(8,128)(2,1)S(1)} %get-tuple-element.143.refs_5_.refs_8_), channel_id=1, source_target_pairs={{0,8},{8,0},{16,24},{24,16},{1,9},{9,1},{17,25},{25,17},{2,10},{10... | collective-permute-start | bytes 2162696 | tf_op jit(solution)/shard_map/ppermute | solution.py:924
  31.5 12.1 %collective-permute-start.6 = (bf16[40,32,128]{2,1,0:T(8,128)(2,1)}, bf16[40,32,128]{2,1,0:T(8,128)(2,1)S(1)}, u32[]{:S(2)}, u32[]{:S(2)}) collective-permute-start(bf16[40,32,128]{2,1,0:T(8,128)(2,1)} %copy-done.7), channel_id=1, source_target_pairs={{0,16},{8,24},{16,0},{24,8},{1,17},{9,25},{17,1},{25,9},{2,18},{10... | collective-permute-start | bytes 983048 | tf_op jit(solution)/shard_map/ppermute | solution.py:924
  41.5 6.8 %collective-permute-start.7 = (bf16[32,512]{1,0:T(8,128)(2,1)S(1)}, bf16[32,512]{1,0:T(8,128)(2,1)S(1)}, u32[]{:S(2)}, u32[]{:S(2)}) collective-permute-start(bf16[32,512]{1,0:T(8,128)(2,1)S(1)} %get-tuple-element.129.refs_0_), channel_id=1, source_target_pairs={{0,8},{8,0},{16,24},{24,16},{1,9},{9,1},{17,25},{25,17},{2,10},{10... | collective-permute-start | bytes 98312 | tf_op jit(solution)/shard_map/ppermute | solution.py:924
  41.9 6.4 %collective-permute-start.8 = (bf16[32,512]{1,0:T(8,128)(2,1)S(1)}, bf16[32,512]{1,0:T(8,128)(2,1)S(1)}, u32[]{:S(2)}, u32[]{:S(2)}) collective-permute-start(bf16[32,512]{1,0:T(8,128)(2,1)S(1)} %get-tuple-element.129.refs_0_), channel_id=1, source_target_pairs={{0,16},{8,24},{16,0},{24,8},{1,17},{9,25},{17,1},{25,9},{2,18},{10... | collective-permute-start | bytes 98312 | tf_op jit(solution)/shard_map/ppermute | solution.py:924
  43.6 4.7 %collective-permute-start.9 = (bf16[32,512]{1,0:T(8,128)(2,1)S(1)}, bf16[32,512]{1,0:T(8,128)(2,1)S(1)}, u32[]{:S(2)}, u32[]{:S(2)}) collective-permute-start(bf16[32,512]{1,0:T(8,128)(2,1)S(1)} %get-tuple-element.129.refs_0_), channel_id=1, source_target_pairs={{0,24},{8,16},{16,8},{24,0},{1,25},{9,17},{17,9},{25,1},{2,26},{10... | collective-permute-start | bytes 98312 | tf_op jit(solution)/shard_map/ppermute | solution.py:924
  48.3 20.6 %collective-permute-start.11 = (bf16[88,32,128]{2,1,0:T(8,128)(2,1)S(1)}, bf16[88,32,128]{2,1,0:T(8,128)(2,1)S(1)}, u32[]{:S(2)}, u32[]{:S(2)}) collective-permute-start(bf16[88,32,128]{2,1,0:T(8,128)(2,1)S(1)} %get-tuple-element.143.refs_5_.refs_8_), channel_id=1, source_target_pairs={{0,16},{8,24},{16,0},{24,8},{1,17},{9,25},{17,1},{25,9},{2,18},{10... | collective-permute-start | bytes 2162696 | tf_op jit(solution)/shard_map/ppermute | solution.py:924
  63.8 4.4 %collective-permute-start.10 = (bf16[32,512]{1,0:T(8,128)(2,1)S(1)}, bf16[32,512]{1,0:T(8,128)(2,1)S(1)}, u32[]{:S(2)}, u32[]{:S(2)}) collective-permute-start(bf16[32,512]{1,0:T(8,128)(2,1)S(1)} %get-tuple-element.142), channel_id=1, source_target_pairs={{0,8},{8,0},{16,24},{24,16},{1,9},{9,1},{17,25},{25,17},{2,10},{10... | collective-permute-start | bytes 98312 | tf_op jit(solution)/shard_map/ppermute | solution.py:924
  64.2 4.7 %collective-permute-start.12 = (bf16[32,512]{1,0:T(8,128)(2,1)S(1)}, bf16[32,512]{1,0:T(8,128)(2,1)S(1)}, u32[]{:S(2)}, u32[]{:S(2)}) collective-permute-start(bf16[32,512]{1,0:T(8,128)(2,1)S(1)} %get-tuple-element.145), channel_id=1, source_target_pairs={{0,16},{8,24},{16,0},{24,8},{1,17},{9,25},{17,1},{25,9},{2,18},{10... | collective-permute-start | bytes 98312 | tf_op jit(solution)/shard_map/ppermute | solution.py:924
  68.2 10.0 %collective-permute-start.17 = (bf16[40,32,128]{2,1,0:T(8,128)(2,1)S(1)}, bf16[40,32,128]{2,1,0:T(8,128)(2,1)S(1)}, u32[]{:S(2)}, u32[]{:S(2)}) collective-permute-start(bf16[40,32,128]{2,1,0:T(8,128)(2,1)S(1)} %copy-done.9), channel_id=1, source_target_pairs={{0,8},{8,0},{16,24},{24,16},{1,9},{9,1},{17,25},{25,17},{2,10},{10... | collective-permute-start | bytes 983048 | tf_op jit(solution)/shard_map/ppermute | solution.py:924
  77.5 14.7 %collective-permute-start.20 = (bf16[88,32,128]{2,1,0:T(8,128)(2,1)S(1)}, bf16[88,32,128]{2,1,0:T(8,128)(2,1)S(1)}, u32[]{:S(2)}, u32[]{:S(2)}) collective-permute-start(bf16[88,32,128]{2,1,0:T(8,128)(2,1)S(1)} %collective-permute-done.11.refs_10_), channel_id=1, source_target_pairs={{0,8},{8,0},{16,24},{24,16},{1,9},{9,1},{17,25},{25,17},{2,10},{10... | collective-permute-start | bytes 2162696 | tf_op jit(solution)/shard_map/ppermute | solution.py:924
  77.6 14.6 %collective-permute-start.18 = (bf16[40,32,128]{2,1,0:T(8,128)(2,1)S(1)}, bf16[40,32,128]{2,1,0:T(8,128)(2,1)S(1)}, u32[]{:S(2)}, u32[]{:S(2)}) collective-permute-start(bf16[40,32,128]{2,1,0:T(8,128)(2,1)S(1)} %collective-permute-done.6.refs_6_), channel_id=1, source_target_pairs={{0,8},{8,0},{16,24},{24,16},{1,9},{9,1},{17,25},{25,17},{2,10},{10... | collective-permute-start | bytes 983048 | tf_op jit(solution)/shard_map/ppermute | solution.py:924
  78.1 9.1 %collective-permute-start.14 = (bf16[32,32,128]{2,1,0:T(8,128)(2,1)}, bf16[32,32,128]{2,1,0:T(8,128)(2,1)S(1)}, u32[]{:S(2)}, u32[]{:S(2)}) collective-permute-start(bf16[32,32,128]{2,1,0:T(8,128)(2,1)} %get-tuple-element.161), channel_id=1, source_target_pairs={{0,8},{8,0},{16,24},{24,16},{1,9},{9,1},{17,25},{25,17},{2,10},{10... | collective-permute-start | bytes 786440 | tf_op jit(solution)/shard_map/ppermute | solution.py:924
  78.2 9.3 %collective-permute-start.15 = (bf16[32,32,128]{2,1,0:T(8,128)(2,1)}, bf16[32,32,128]{2,1,0:T(8,128)(2,1)S(1)}, u32[]{:S(2)}, u32[]{:S(2)}) collective-permute-start(bf16[32,32,128]{2,1,0:T(8,128)(2,1)} %get-tuple-element.162), channel_id=1, source_target_pairs={{0,16},{8,24},{16,0},{24,8},{1,17},{9,25},{17,1},{25,9},{2,18},{10... | collective-permute-start | bytes 786440 | tf_op jit(solution)/shard_map/ppermute | solution.py:924
  79.2 13.0 %collective-permute-start.16 = (bf16[32,32,128]{2,1,0:T(8,128)(2,1)}, bf16[32,32,128]{2,1,0:T(8,128)(2,1)S(1)}, u32[]{:S(2)}, u32[]{:S(2)}) collective-permute-start(bf16[32,32,128]{2,1,0:T(8,128)(2,1)} %get-tuple-element.163), channel_id=1, source_target_pairs={{0,24},{8,16},{16,8},{24,0},{1,25},{9,17},{17,9},{25,1},{2,26},{10... | collective-permute-start | bytes 786440 | tf_op jit(solution)/shard_map/ppermute | solution.py:924
  98.1 4.6 %collective-permute-start.21 = (bf16[368,128]{1,0:T(8,128)(2,1)S(1)}, bf16[368,128]{1,0:T(8,128)(2,1)S(1)}, u32[]{:S(2)}, u32[]{:S(2)}) collective-permute-start(bf16[368,128]{1,0:T(8,128)(2,1)S(1)} %get-tuple-element.175), channel_id=1, source_target_pairs={{0,8},{8,0},{16,24},{24,16},{1,9},{9,1},{17,25},{25,17},{2,10},{10... | collective-permute-start | bytes 282632 | tf_op jit(solution)/shard_map/ppermute | solution.py:924
  99.0 5.0 %collective-permute-start.23 = (bf16[368,128]{1,0:T(8,128)(2,1)S(1)}, bf16[368,128]{1,0:T(8,128)(2,1)S(1)}, u32[]{:S(2)}, u32[]{:S(2)}) collective-permute-start(bf16[368,128]{1,0:T(8,128)(2,1)S(1)} %add.19), channel_id=1, source_target_pairs={{0,16},{8,24},{16,0},{24,8},{1,17},{9,25},{17,1},{25,9},{2,18},{10... | collective-permute-start | bytes 282632 | tf_op jit(solution)/shard_map/ppermute | solution.py:924
  104.0 4.6 %collective-permute-start.24 = (bf16[368,128]{1,0:T(8,128)(2,1)S(1)}, bf16[368,128]{1,0:T(8,128)(2,1)S(1)}, u32[]{:S(2)}, u32[]{:S(2)}) collective-permute-start(bf16[368,128]{1,0:T(8,128)(2,1)S(1)} %add_add_fusion), channel_id=1, source_target_pairs={{0,1},{1,0},{2,3},{3,2},{4,5},{5,4},{6,7},{7,6},{8,9},{9,8},{10,11... | collective-permute-start | bytes 282632 | tf_op jit(solution)/shard_map/ppermute | solution.py:924
  108.6 4.6 %collective-permute-start.25 = (bf16[368,128]{1,0:T(8,128)(2,1)S(1)}, bf16[368,128]{1,0:T(8,128)(2,1)S(1)}, u32[]{:S(2)}, u32[]{:S(2)}) collective-permute-start(bf16[368,128]{1,0:T(8,128)(2,1)S(1)} %add.21), channel_id=1, source_target_pairs={{0,2},{1,3},{2,0},{3,1},{4,6},{5,7},{6,4},{7,5},{8,10},{9,11},{10,... | collective-permute-start | bytes 282632 | tf_op jit(solution)/shard_map/ppermute | solution.py:924
  113.3 5.5 %collective-permute-start.26 = (bf16[368,128]{1,0:T(8,128)(2,1)S(1)}, bf16[368,128]{1,0:T(8,128)(2,1)S(1)}, u32[]{:S(2)}, u32[]{:S(2)}) collective-permute-start(bf16[368,128]{1,0:T(8,128)(2,1)S(1)} %add.22), channel_id=1, source_target_pairs={{0,4},{1,5},{2,6},{3,7},{4,0},{5,1},{6,2},{7,3},{8,12},{9,13},{10,... | collective-permute-start | bytes 282632 | tf_op jit(solution)/shard_map/ppermute | solution.py:924
  118.9 4.6 %collective-permute-start.27 = (bf16[368,128]{1,0:T(8,128)(2,1)S(1)}, bf16[368,128]{1,0:T(8,128)(2,1)S(1)}, u32[]{:S(2)}, u32[]{:S(2)}) collective-permute-start(bf16[368,128]{1,0:T(8,128)(2,1)S(1)} %add.23.refs_0_), channel_id=1, source_target_pairs={{0,16},{8,24},{16,0},{24,8},{1,17},{9,25},{17,1},{25,9},{2,18},{10... | collective-permute-start | bytes 282632 | tf_op jit(solution)/shard_map/ppermute | solution.py:924
  (34 other events, 215.3 us)

commit v3 on v2

--- a/solution.py
+++ b/solution.py
@@ -177,8 +177,8 @@
 def left_kernel(parts, normed_any, *refs):
     live_parts = refs[:parts]
     weight, gating = refs[parts : parts + 2]
-    low_out, high_out, gate_any, live, factor_any = refs[parts + 2 : parts + 7]
-    weight_t, lay, gates, factors, normed1, in_sems, sems = refs[parts + 7 :]
+    high_out, gate_any, live, factor_any, low_any = refs[parts + 2 : parts + 7]
+    weight_t, lay, gates, factors, normed1, in_sems, sems, low_sem, low_out = refs[parts + 7 :]
     arrivals = split_copies(normed_any, normed1, in_sems, parts)
     start(arrivals)
     rows, length, channels = gates.shape
@@ -210,6 +210,9 @@
     left = lay[...].reshape(channels, rows, length).astype(BF16)
     low = low_out.shape[0]
     low_out[...] = left[:low]
+    copy = pltpu.make_async_copy(low_out, low_any, low_sem)
+    copy.start()
+    outs.append(copy)
     high_out[...] = left[low:]
     wait(outs)
 
@@ -250,7 +253,7 @@
 def product_kernel(count, side, *refs):
     near = count // 2
     blocks = refs[: 2 * near]
-    lefts = refs[2 * near : 2 * near + 2]
+    low_any, high = refs[2 * near : 2 * near + 2]
     (pair_any, gate_any, gain2_col, gain3, output_w, bias_w) = refs[2 * near + 2 : 2 * near + 8]
     rest = refs[2 * near + 8 :]
     if side:
@@ -259,7 +262,7 @@
     right_any, scale2_out, bias_out, product, bias_scr, right_side, pair, gate = rest[4:12]
     kept = rest[12:16]
     normed2_out, update_out, middle_out, normed3_out = kept
-    in_sems, out_sems, right_sem, bias_sem, bias_near = rest[16:]
+    in_sems, out_sems, right_sem, bias_sem, bias_near, low = rest[16:]
     rows, wide, channels = pair.shape
     length = 2 * wide
     lines = rows // 2
@@ -267,6 +270,8 @@
     place = lax.axis_index("dap")
     chip = place // near
     span = pl.ds(pl.multiple_of((chip ^ side) * wide, wide), wide)
+    low_copy = pltpu.make_async_copy(low_any, low, in_sems.at[2])
+    low_copy.start()
     arrivals = [
         pltpu.make_async_copy(pair_any.at[:, span, :], pair, in_sems.at[0]),
         pltpu.make_async_copy(gate_any.at[:, span, :], gate, in_sems.at[1]),
@@ -288,7 +293,9 @@
     side_by_side(0, channels, channel)
     right_copy = pltpu.make_async_copy(right_side, right_any, right_sem)
     right_copy.start()
-    for left, first in zip(lefts, (0, lefts[0].shape[0])):
+    for left, first in ((high, low.shape[0]), (low, 0)):
+        if first == 0:
+            low_copy.wait()
 
         def multiply(pair_of, left=left, first=first):
             c = 2 * pair_of
@@ -416,15 +423,15 @@
 
 def attend_kernel(count, table, *refs):
     bias_refs = refs[:count]
-    types_row, types_col, live, output_w = refs[count : count + 4]
-    row_arrays = refs[count + 4 : count + 10]
-    (pair_out_any, d_projected, d_output, d_table) = refs[count + 10 : count + 14]
-    d_bias_outs = refs[count + 14 : 2 * count + 14]
-    bias, d_bias, head_mask = refs[2 * count + 14 : 2 * count + 17]
-    fetched = refs[2 * count + 17 : 2 * count + 23]
-    projected, queries, gates, d_gateds, cotangent, middle = fetched
-    pair_out, in_sems, out_sems = refs[2 * count + 23 :]
-    rows, length, channels = middle.shape
+    types_row, types_col, live = refs[count : count + 3]
+    row_arrays = refs[count + 3 : count + 7]
+    gated_any, d_projected, d_table = refs[count + 7 : count + 10]
+    d_bias_outs = refs[count + 10 : 2 * count + 10]
+    bias, d_bias, head_mask = refs[2 * count + 10 : 2 * count + 13]
+    fetched = refs[2 * count + 13 : 2 * count + 17]
+    projected, queries, gates, d_gateds = fetched
+    gated_all, in_sems, out_sems = refs[2 * count + 17 :]
+    rows, length, channels = queries.shape
     types = table.shape[1]
     heads = table.shape[0] // types
     size = channels // heads
@@ -456,7 +463,6 @@
             total = jnp.where(col_types == a, values, total)
         bias[:, spans(h)] = (bias[:, spans(h)] + total) * LOG2_E
     d_bias[...] = jnp.zeros_like(d_bias)
-    d_output[...] = jnp.zeros_like(d_output)
     lines = lax.broadcasted_iota(jnp.int32, head_mask.shape, 0) // size
     columns = lax.broadcasted_iota(jnp.int32, head_mask.shape, 1) // length
     head_mask[...] = (lines == columns).astype(F32).astype(BF16)
@@ -485,7 +491,7 @@
         total = sums[:, channels:]
         inverse = 1.0 / jnp.maximum(total, 1.0)
         attended = sums[:, :channels] * inverse
-        gated = (gate * attended).astype(BF16)
+        gated_all[i] = (gate * attended).astype(BF16)
         d_attended = d_gated * gate * inverse
         d_gate = d_gated * attended * gate * (1.0 - gate)
         slope = jnp.where(total > 1.0, 1.0, jnp.where(total == 1.0, 0.5, 0.0))
@@ -494,16 +500,14 @@
             [d_attended_b, (-d_attended * attended * slope).astype(BF16)], axis=1
         )
         d_expo = mm(both, values)
-        turned = jnp.concatenate([d_attended_b.T, d_gate.astype(BF16).T, gated.T], axis=1)
-        yield
-        update = mm(gated, output_w[...])
+        turned = jnp.concatenate([d_attended_b.T, d_gate.astype(BF16).T], axis=1)
+        yield
         d_score = expo * d_expo
         d_score_b = d_score.astype(BF16)
         d_query_t = mmt(keys, d_score_b) * factor
         d_key_t = mm(query_t, d_score_b)
         d_value_t = mm(turned[:, :length], expo_b)
         yield
-        pair_out[i] = (middle[i].astype(F32) + update).astype(BF16)
 
         def diagonal(full):
             return jnp.concatenate(
@@ -513,15 +517,13 @@
         d_projected[i, :channels] = d_query_t.astype(BF16)
         d_projected[i, channels : 2 * channels] = diagonal(d_key_t).astype(BF16)
         d_projected[i, 2 * channels : 3 * channels] = (diagonal(d_value_t) * live_row).astype(BF16)
-        d_projected[i, 3 * channels :] = turned[:, length : 2 * length]
-        return turned[:, 2 * length :], cotangent[i], d_score
+        d_projected[i, 3 * channels :] = turned[:, length:]
+        return d_score
 
     def finish(results):
-        gated_t, cots, d_scores = zip(*results)
-        d_output[...] += mm(jnp.concatenate(gated_t, axis=1), jnp.concatenate(cots, axis=0))
-        d_bias[...] += sum(d_scores)
-
-    departures = split_copies(pair_out, pair_out_any, out_sems, parts)
+        d_bias[...] += sum(results)
+
+    departures = split_copies(gated_all, gated_any, out_sems, parts)
     for part in range(parts):
         wait([copies[part] for copies in arrivals])
         over_rows(rows // parts, W_ATTEND, row, finish, first=part * (rows // parts))
@@ -547,7 +549,33 @@
     wait(departures)
 
 
-def projection_kernel(d_projected, normed3, input_w, d_output, d_table, d_normed, packed, total):
+def output_kernel(gated_any, middle_any, cotangent_any, output_w, pair_out_any, d_output, *scratch):
+    gated, middle, cotangent, pair_out, in_sems, out_sems = scratch
+    rows, length, channels = gated.shape
+    parts = 4
+    arrivals = [
+        split_copies(source, target, in_sems.at[at], parts)
+        for at, (source, target) in enumerate(
+            ((gated_any, gated), (cotangent_any, cotangent), (middle_any, middle))
+        )
+    ]
+    for part in range(parts):
+        start([copies[part] for copies in arrivals])
+    departures = split_copies(pair_out, pair_out_any, out_sems, parts)
+    d_output[...] = jnp.zeros_like(d_output)
+    size = rows // parts
+    for part in range(parts):
+        wait([copies[part] for copies in arrivals])
+        some = pl.ds(part * size, size)
+        flat = gated[some].reshape(size * length, channels)
+        update = mm(flat, output_w[...]).reshape(size, length, channels)
+        pair_out[some] = (middle[some].astype(F32) + update).astype(BF16)
+        departures[part].start()
+        d_output[...] += mm(flat.T, cotangent[some].reshape(size * length, channels))
+    wait(departures)
+
+
+def projection_kernel(d_projected, normed3, input_w, d_table, d_normed, packed, total):
     block = normed3.shape[0]
     wide, length = d_projected.shape[1:]
     channels = normed3.shape[2]
@@ -571,7 +599,7 @@
     @pl.when(step == pl.num_programs(0) - 1)
     def _():
         packed[:wide] = total[...].astype(BF16)
-        packed[wide : wide + channels] = d_output[...].astype(BF16)
+        packed[wide : wide + channels] = jnp.zeros((channels, channels), BF16)
         high = d_table[...].astype(BF16)
         packed[wide + channels : wide + channels + HEAD_ROWS] = high
         packed[wide + channels + HEAD_ROWS :] = (d_table[...] - high.astype(F32)).astype(BF16)
@@ -774,10 +802,10 @@
     arrived = refs[:count]
     left_halves = refs[count : 2 * count], refs[2 * count : 3 * count]
     refs = refs[count:]
-    normed1_any, factors_any, packed_a, packed_b = refs[2 * count : 2 * count + 4]
-    d_projected_any = refs[2 * count + 4]
-    sends = refs[2 * count + 5 : 3 * count + 5]
-    lay, grad, packed, d_projected_out, sems, normed1, factors, in_sems = refs[3 * count + 5 :]
+    normed1_any, factors_any, packed_a, packed_b, d_output = refs[2 * count : 2 * count + 5]
+    d_projected_any = refs[2 * count + 5]
+    sends = refs[2 * count + 6 : 3 * count + 6]
+    lay, grad, packed, d_projected_out, sems, normed1, factors, in_sems = refs[3 * count + 6 :]
     rows, length, channels = normed1.shape
     arrivals = [
         pltpu.make_async_copy(normed1_any, normed1, in_sems.at[0]),
@@ -825,6 +853,7 @@
         departures[part].start()
     first, second = packed_a.shape[0], packed_b.shape[0]
     packed[:first] = packed_a[...]
+    packed[4 * channels : 5 * channels] = d_output[...].astype(BF16)
     packed[first : first + second] = packed_b[...]
     packed[first + second : first + second + 2 * channels] = grad[...].astype(BF16)
     packed[first + second + 2 * channels :] = jnp.zeros_like(
@@ -1017,18 +1046,18 @@
         right_halves.append(right_part)
         live_halves.append(live_part)
     low_count = 5 * channels // 16
-    left_low, left_high, gate, live, left_factors = call(
+    left_high, gate, live, left_factors, left_low = call(
         partial(left_kernel, 2),
         [
-            ((low_count, rows, length), BF16),
             ((channels - low_count, rows, length), BF16),
             (cells, F32),
             ((rows, length), F32),
             ((rows, 2 * channels, length), BF16),
+            ((low_count, rows, length), BF16),
         ],
         [normed1, *live_halves, triangle_input, triangle_gating],
         in_specs=[anywhere] + [vmem] * 4,
-        out_specs=[vmem, vmem, anywhere, vmem, anywhere],
+        out_specs=[vmem, anywhere, vmem, anywhere, anywhere],
         scratch=[
             pltpu.VMEM((2 * channels, channels), BF16),
             pltpu.VMEM((channels * rows, length), F32),
@@ -1037,6 +1066,8 @@
             cell_buffer,
             pltpu.SemaphoreType.DMA((2,)),
             pltpu.SemaphoreType.DMA((2, 2)),
+            pltpu.SemaphoreType.DMA,
+            pltpu.VMEM((low_count, rows, length), BF16),
         ],
         us=6.0,
         name="left_projection",
@@ -1077,7 +1108,8 @@
             ],
             [*blocks, left_low, left_high, slab, gate, gain2_col, gain3_row]
             + [triangle_output, attend_bias, *given],
-            in_specs=[vmem] * (count + 2)
+            in_specs=[vmem] * count
+            + [anywhere, vmem]
             + [anywhere] * 2
             + [vmem] * 4
             + [anywhere] * (5 if side else 0),
@@ -1092,11 +1124,12 @@
             ]
             + [pltpu.VMEM((rows, wide, channels), BF16)] * 3
             + [
-                pltpu.SemaphoreType.DMA((2,)),
+                pltpu.SemaphoreType.DMA((3,)),
                 pltpu.SemaphoreType.DMA((4, 4)),
                 pltpu.SemaphoreType.DMA,
                 pltpu.SemaphoreType.DMA,
                 pltpu.VMEM((lines * HEAD_ROWS, length), F32),
+                pltpu.VMEM(left_low.shape, BF16),
             ],
             aliases={count + 9 + at: at for at in range(4)} if side else None,
             us=7.0,
@@ -1156,42 +1189,41 @@
         [
             (cells, BF16),
             ((rows, 4 * channels, length), BF16),
-            ((channels, channels), F32),
             ((HEAD_ROWS, channels), F32),
             ((rows, heads * length), F32),
         ]
         + [((rows, heads * length), BF16)] * (count - 1),
         [type_table.reshape(heads * types, types), *bias_blocks]
-        + [tok_types, tok_types.reshape(length, 1), live, attend_output]
-        + [projected3, query, gate3, d_gated, cot, middle],
-        in_specs=[smem] + [vmem] * (count + 4) + [anywhere] * 6,
-        out_specs=[anywhere] + [vmem] * (count + 3),
+        + [tok_types, tok_types.reshape(length, 1), live]
+        + [projected3, query, gate3, d_gated],
+        in_specs=[smem] + [vmem] * (count + 3) + [anywhere] * 4,
+        out_specs=[anywhere] + [vmem] * (count + 2),
         scratch=[
             pltpu.VMEM((length, heads * length), F32),
             pltpu.VMEM((length, heads * length), F32),
             pltpu.VMEM((channels, heads * length), BF16),
         ]
         + [pltpu.VMEM((rows, 3 * channels, length), BF16), cell_buffer, pltpu.VMEM(cells, F32)]
-        + [cell_buffer] * 4
+        + [cell_buffer] * 2
         + [
-            pltpu.SemaphoreType.DMA((6, rows // W_ATTEND)),
+            pltpu.SemaphoreType.DMA((4, rows // W_ATTEND)),
             pltpu.SemaphoreType.DMA((rows // W_ATTEND,)),
         ],
         us=20.0,
         name="attention",
     )
-    pair_out, d_projected3, d_output, d_table = attend_outs[:4]
-    d_bias_parts = [attend_outs[4]] + [
-        swap(attend_outs[4 + offset], "dap", offset) for offset in range(1, count)
+    gated, d_projected3, d_table = attend_outs[:3]
+    d_bias_parts = [attend_outs[3]] + [
+        swap(attend_outs[3 + offset], "dap", offset) for offset in range(1, count)
     ]
     d_bias_parts[1], high_far = lax.optimization_barrier((d_bias_parts[1], high_far))
     d_normed3, packed_a = call(
         projection_kernel,
         [(turned, F32), ((4 * channels + channels + 2 * HEAD_ROWS, channels), BF16)],
-        [d_projected3, normed3, attend_input, d_output, d_table],
+        [d_projected3, normed3, attend_input, d_table],
         grid=(steps,),
         in_specs=[by_row_wide, by_row, fixed(channels, 4 * channels)]
-        + [fixed(channels, channels), fixed(HEAD_ROWS, channels)],
+        + [fixed(HEAD_ROWS, channels)],
         out_specs=[
             pl.BlockSpec((block, channels, length), lambda step: (step, 0, 0)),
             fixed(5 * channels + 2 * HEAD_ROWS, channels),
@@ -1259,13 +1291,26 @@
         us=10.0,
         name="left_back",
     )
+    gated, d_left = lax.optimization_barrier((gated, d_left))
+    pair_out, d_output = call(
+        output_kernel,
+        [(cells, BF16), ((channels, channels), F32)],
+        [gated, middle, cot, attend_output],
+        in_specs=[anywhere] * 3 + [vmem],
+        out_specs=[anywhere, vmem],
+        scratch=[cell_buffer] * 4
+        + [pltpu.SemaphoreType.DMA((3, 4)), pltpu.SemaphoreType.DMA((4,))],
+        us=0.1,
+        name="attention_output",
+    )
     used = packed_a.shape[0] + packed_b.shape[0] + 2 * channels
     share = -(-used // (count * HEAD_ROWS)) * HEAD_ROWS
     right_outs = call(
         partial(right_back_kernel, count),
         [((rows, 2 * channels, length), BF16)] + [((share, channels), BF16)] * count,
-        [*product_parts, *left_blocks, normed1, right_factors, packed_a, packed_b],
-        in_specs=[vmem] * (3 * count) + [anywhere] * 2 + [vmem] * 2,
+        [*product_parts, *left_blocks, normed1, right_factors, packed_a, packed_b]
+        + [d_output],
+        in_specs=[vmem] * (3 * count) + [anywhere] * 2 + [vmem] * 3,
         out_specs=[anywhere] + [vmem] * count,
         scratch=[
             pltpu.VMEM((channels * rows, length), F32),

time: 126 us -> 124 us (0.984)
  waiting for transfers between devices: 15.7 us -> 10 us
  starting transfers between devices: 23.5 us -> 26.1 us
  Pallas kernels: 83.8 us -> 85.7 us
    ppermute x30, waiting for transfers between devices: 15.7 us -> 10 us  [swap(): lax.ppermute(value, axis, [(index, index ^ step) for index in range(count)])]
    ppermute x30, starting transfers between devices: 23.5 us -> 26.1 us  [swap(): lax.ppermute(value, axis, [(index, index ^ step) for index in range(count)])]
    pallas_call x17 -> x18, Pallas kernels: 83.8 us -> 85.7 us  [call(): pl.pallas_call(kernel, out_shape=[pltpu.HBM(shape, dtype) if spec.memory_...]
  transfers between devices with their start and end apart: 30 -> 30, of which waited for: 13 -> 13; matrix products, arithmetic and copies ran while one was open for 0% -> 0% of each run, Pallas kernels for 59% -> 61%
where the time goes in v3:
time: 124 us
  Pallas kernels  85.7 us (69%)
  starting transfers between devices  26.1 us (21%)
  waiting for transfers between devices  10 us (8%)
    pallas_call x18, Pallas kernels, call(): pl.pallas_call(kernel, out_shape=[pltpu.HBM(shape, dtype) if spec.memory_...  85.7 us
    ppermute x30, starting transfers between devices, swap(): lax.ppermute(value, axis, [(index, index ^ step) for index in range(count)])  26.1 us
    ppermute x30, waiting for transfers between devices, swap(): lax.ppermute(value, axis, [(index, index ^ step) for index in range(count)])  10 us
  transfers between devices with their start and end apart: 30, of which 13 were waited for; matrix products, arithmetic and copies ran while one was open for 0% of the time, Pallas kernels for 61%

profile of v3, /device:TPU:0, one launch (start us, length us, event | category | flops | bytes accessed | tf_op | source)
XLA Modules:
  0.0 123.9 jit_solution(9258413705646402961)
XLA Ops:
  0.6 3.3 %right_projection.2 = (bf16[32,128,128]{2,1,0:T(8,128)(2,1)}, bf16[128,16,128]{2,1,0:T(8,128)(2,1)S(1)}, f32[16,128]{1,0:T(8,128)S(1)}) custom-call(bf16[32,128,128]{2,1,0:T(8,128)(2,1)} %bitcast.32, s32[32,128]{1,0:T(8,128)} %bitcast.41, s32[1,128]{1,0:T(1,128)} %tokens_any.3, f32[1,128]{1,0:T(1,128)} %bitcast.21, bf16[128,512]{1,0:T(8,128)(2,1)} %refs_4_.3), custom_call_target="tpu_custom_call" | custom-call | flops 3000000000 | bytes 9000000 | tf_op jit(solution)/shard_map/right_projection/pallas_call | solution.py:109
  4.5 2.6 %collective-permute-start = (bf16[128,16,128]{2,1,0:T(8,128)(2,1)S(1)}, bf16[128,16,128]{2,1,0:T(8,128)(2,1)S(1)}, u32[]{:S(2)}, u32[]{:S(2)}) collective-permute-start(bf16[128,16,128]{2,1,0:T(8,128)(2,1)S(1)} %get-tuple-element.112.refs_0_), channel_id=1, source_target_pairs={{0,16},{8,24},{16,0},{24,8},{1,17},{9,25},{17,1},{25,9},{2,18},{10... | collective-permute-start | bytes 1572872 | tf_op jit(solution)/shard_map/ppermute | solution.py:953
  7.1 3.4 %right_projection.3 = (bf16[32,128,128]{2,1,0:T(8,128)(2,1)}, bf16[128,16,128]{2,1,0:T(8,128)(2,1)S(1)}, f32[16,128]{1,0:T(8,128)S(1)}) custom-call(bf16[32,128,128]{2,1,0:T(8,128)(2,1)} %bitcast.33, s32[32,128]{1,0:T(8,128)} %bitcast.42, s32[1,128]{1,0:T(1,128)} %tokens_any.3, f32[1,128]{1,0:T(1,128)} %bitcast.22, ...), custom_call_target="tpu_custom_call", output_to_operand_aliasing={{0}: (5, {})} | custom-call | flops 3000000000 | bytes 9000000 | tf_op jit(solution)/shard_map/right_projection/pallas_call | solution.py:109
  11.3 5.9 %left_projection.1 = (bf16[88,32,128]{2,1,0:T(8,128)(2,1)S(1)}, f32[32,128,128]{2,1,0:T(8,128)}, f32[32,128]{1,0:T(8,128)S(1)}, bf16[32,256,128]{2,1,0:T(8,128)(2,1)}, bf16[40,32,128]{2,1,0:T(8,128)(2,1)}) custom-call(bf16[32,128,128]{2,1,0:T(8,128)(2,1)} %get-tuple-element.108.normed_any.refs_3_.normed1_any.refs_12_, ...), custom_call_target="tpu_custom_call" | custom-call | flops 6000000000 | bytes 18000000 | tf_op jit(solution)/shard_map/left_projection/pallas_call | solution.py:109
  17.3 6.5 %product_near.1 = (bf16[2,16,128,128]{3,2,1,0:T(8,128)(2,1)}, bf16[32,128,128]{2,1,0:T(8,128)(2,1)}, bf16[32,128,128]{2,1,0:T(8,128)(2,1)}, bf16[32,128,128]{2,1...) custom-call(bf16[128,16,128]{2,1,0:T(8,128)(2,1)S(1)} %get-tuple-element.112.refs_0_, ...), custom_call_target="tpu_custom_call" | custom-call | flops 7000000000 | bytes 21000000 | tf_op jit(solution)/shard_map/product_near/pallas_call | solution.py:109
  23.9 4.5 %right_factors.1 = (bf16[32,256,128]{2,1,0:T(8,128)(2,1)}, bf16[32,128,128]{2,1,0:T(8,128)(2,1)}) custom-call(f32[32,128]{1,0:T(8,128)S(1)} %get-tuple-element.119.refs_0_.refs_6_, bf16[128,512]{1,0:T(8,128)(2,1)S(1)} %copy-done.10, bf16[128,128]{1,0:T(8,128)(2,1)S(1)} %copy-done.4, ...), custom_call_target="tpu_custom_call" | custom-call | flops 5000000000 | bytes 15000000 | tf_op jit(solution)/shard_map/right_factors/pallas_call | solution.py:109
  28.4 2.4 %collective-permute-done.3.refs_1_ = bf16[128,16,128]{2,1,0:T(8,128)(2,1)S(1)} collective-permute-done((bf16[128,16,128]{2,1,0:T(8,128)(2,1)S(1)}, bf16[128,16,128]{2,1,0:T(8,128)(2,1)S(1)}, u32[]{:S(2)}, u32[]{:S(2)}) %collective-permute-start.3) | collective-permute-done | bytes 524320 | tf_op jit(solution)/shard_map/ppermute | solution.py:953
  31.5 1.8 %collective-permute-start.6 = (bf16[40,32,128]{2,1,0:T(8,128)(2,1)}, bf16[40,32,128]{2,1,0:T(8,128)(2,1)S(1)}, u32[]{:S(2)}, u32[]{:S(2)}) collective-permute-start(bf16[40,32,128]{2,1,0:T(8,128)(2,1)} %get-tuple-element.128.refs_4_), channel_id=1, source_target_pairs={{0,16},{8,24},{16,0},{24,8},{1,17},{9,25},{17,1},{25,9},{2,18},{10... | collective-permute-start | bytes 983048 | tf_op jit(solution)/shard_map/ppermute | solution.py:953
  34.0 6.5 %product_other.1 = (bf16[2,16,128,128]{3,2,1,0:T(8,128)(2,1)}, bf16[32,128,128]{2,1,0:T(8,128)(2,1)}, bf16[32,128,128]{2,1,0:T(8,128)(2,1)}, bf16[32,128,128]{2,...) custom-call(bf16[128,16,128]{2,1,0:T(8,128)(2,1)S(1)} %collective-pe, ...), custom_call_target="tpu_custom_call", output_to_operand_aliasing={{0}: (13, {}), {1}: (14, {}), {2}: (15, {}), {3}: (16, {})} | custom-call | flops 7000000000 | bytes 21000000 | tf_op jit(solution)/shard_map/product_other/pallas_call | solution.py:109
  42.7 4.6 %attention_projections.1 = (bf16[32,384,128]{2,1,0:T(8,128)(2,1)}, bf16[32,128,128]{2,1,0:T(8,128)(2,1)}, f32[32,128,128]{2,1,0:T(8,128)}) custom-call(bf16[32,128,128]{2,1,0:T(8,128)(2,1)} %get-tuple-element.129.normed3_any.normed3.refs_5_, bf16[128,512]{1,0:T(8,128)(2,1)} %refs_8_.1), custom_call_target="tpu_custom_call" | custom-call | flops 5000000000 | bytes 15000000 | tf_op jit(solution)/shard_map/attention_projections/pallas_call | solution.py:109
  48.9 12.7 %attention.1 = (bf16[32,128,128]{2,1,0:T(8,128)(2,1)}, bf16[32,512,128]{2,1,0:T(8,128)(2,1)S(1)}, f32[16,128]{1,0:T(8,128)S(1)}, f32[32,512]{1,0:T(8,128)S(1)}, ...) custom-call(f32[16,4]{1,0:T(8,128)S(1)} %bitcast.31, ...), custom_call_target="tpu_custom_call" | custom-call | flops 20000000000 | bytes 60000000 | tf_op jit(solution)/shard_map/attention/pallas_call | solution.py:109
  63.6 2.4 %projection_back.1 = (f32[32,128,128]{2,1,0:T(8,128)S(1)}, bf16[672,128]{1,0:T(8,128)(2,1)S(1)}) custom-call(bf16[32,512,128]{2,1,0:T(8,128)(2,1)S(1)} %get-tuple-element.149.d_projected, bf16[32,128,128]{2,1,0:T(8,128)(2,1)S(1)} %copy-done.2, bf16[128,512]{1,0:T(8,128)(2,1)S(1)} %copy-done.3, f32[16,128]{1,0:T(8,128)S(1)} %get-tuple-element.150.d_table), custom_call_target="tpu_custom_call" | custom-call | flops 500000000 | bytes 1500000 | tf_op jit(solution)/shard_map/projection_back/pallas_call | solution.py:109
  66.9 8.4 %middle_back.1 = (bf16[32,128,128]{2,1,0:T(8,128)(2,1)}, bf16[32,128,128]{2,1,0:T(8,128)(2,1)}, bf16[4096,128]{1,0:T(8,128)(2,1)}, f32[144,128]{1,0:T(8,128)S(1)...) custom-call(f32[32,512]{1,0:T(8,128)S(1)} %get-tuple-element.143.ref, ...), custom_call_target="tpu_custom_call" | custom-call | flops 12000000000 | bytes 36000000 | tf_op jit(solution)/shard_map/middle_back/pallas_call | solution.py:109
  77.9 7.1 %left_back.1 = (f32[32,128,128]{2,1,0:T(8,128)}, bf16[528,128]{1,0:T(8,128)(2,1)S(1)}) custom-call(bf16[128,64,128]{2,1,0:T(8,128)(2,1)} %get-tuple-element.141.near_any, bf16[128,64,128]{2,1,0:T(8,128)(2,1)} %get-tuple-element.142.other_any, bf16[4096,128]{1,0:T(8,128)(2,1)} %get-tuple-element.157.d_product_any, ...), custom_call_target="tpu_custom_call" | custom-call | flops 10000000000 | bytes 30000000 | tf_op jit(solution)/shard_map/left_back/pallas_call | solution.py:109
  85.0 3.2 %attention_output.1 = (bf16[32,128,128]{2,1,0:T(8,128)(2,1)}, f32[128,128]{1,0:T(8,128)S(1)}) custom-call(bf16[32,128,128]{2,1,0:T(8,128)(2,1)} %get-tuple-element.162.gated_any, bf16[32,128,128]{2,1,0:T(8,128)(2,1)} %get-tuple-element.152.refs_6_.middle_any, bf16[32,128,128]{2,1,0:T(8,128)(2,1)} %bitcast.18, bf16[128,128]{1,0:T(8,128)(2,1)S(1)} %copy-done.4), custom_call_target="tpu_custom_call" | custom-call | flops 100000000 | bytes 300000 | tf_op jit(solution)/shard_map/attention_output/pallas_call | solution.py:109
  90.0 5.4 %right_back.1 = (bf16[32,256,128]{2,1,0:T(8,128)(2,1)}, bf16[368,128]{1,0:T(8,128)(2,1)S(1)}, bf16[368,128]{1,0:T(8,128)(2,1)S(1)}, bf16[368,128]{1,0:T(8,128)(2,1)S(1)}, bf16[368,128]{1,0:T(8,128)(2,1)S(1)}) custom-call(bf16[32,32,128]{2,1,0:T(8,128)(2,1)S(1)} %copy-done.20, bf16[32,32,128]{2,1,0:T(8,128)(2,1)S(1)} %collective-permute-done.14.refs_1_, ...), custom_call_target="tpu_custom_call" | custom-call | flops 7000000000 | bytes 21000000 | tf_op jit(solution)/shard_map/right_back/pallas_call | solution.py:109
  96.8 1.8 %collective-permute-start.23 = (bf16[368,128]{1,0:T(8,128)(2,1)S(1)}, bf16[368,128]{1,0:T(8,128)(2,1)S(1)}, u32[]{:S(2)}, u32[]{:S(2)}) collective-permute-start(bf16[368,128]{1,0:T(8,128)(2,1)S(1)} %add.19), channel_id=1, source_target_pairs={{0,16},{8,24},{16,0},{24,8},{1,17},{9,25},{17,1},{25,9},{2,18},{10... | collective-permute-start | bytes 282632 | tf_op jit(solution)/shard_map/ppermute | solution.py:953
  98.6 2.6 %input_back.4.refs_6_ = bf16[32,128,128]{2,1,0:T(8,128)(2,1)} custom-call(f32[32,128,128]{2,1,0:T(8,128)} %get-tuple-element.164.refs_0_, bf16[32,256,128]{2,1,0:T(8,128)(2,1)} %get-tuple-element.178.refs_1_, bf16[32,128,128]{2,1,0:T(8,128)(2,1)} %bitcast.36, bf16[32,128,128]{2,1,0:T(8,128)(2,1)} %get-tuple-element.179.refs_3_, f32[128,1]{1,0:T(8,128)S(1)} %copy.48.refs_4_, ...), custom_call_target="tpu_custom_call" | custom-call | flops 3000000000 | bytes 9000000 | tf_op jit(solution)/shard_map/input_back/pallas_call | solution.py:109
  103.6 2.6 %input_back.5.refs_6_ = bf16[32,128,128]{2,1,0:T(8,128)(2,1)} custom-call(f32[32,128,128]{2,1,0:T(8,128)} %get-tuple-element.164.refs_0_, bf16[32,256,128]{2,1,0:T(8,128)(2,1)} %get-tuple-element.178.refs_1_, bf16[32,128,128]{2,1,0:T(8,128)(2,1)} %bitcast.37, bf16[32,128,128]{2,1,0:T(8,128)(2,1)} %get-tuple-element.179.refs_3_, ...), custom_call_target="tpu_custom_call", output_to_operand_aliasing={{}: (6, {})} | custom-call | flops 3000000000 | bytes 9000000 | tf_op jit(solution)/shard_map/input_back/pallas_call | solution.py:109
  106.5 1.9 %collective-permute-start.25 = (bf16[368,128]{1,0:T(8,128)(2,1)S(1)}, bf16[368,128]{1,0:T(8,128)(2,1)S(1)}, u32[]{:S(2)}, u32[]{:S(2)}) collective-permute-start(bf16[368,128]{1,0:T(8,128)(2,1)S(1)} %add.21), channel_id=1, source_target_pairs={{0,2},{1,3},{2,0},{3,1},{4,6},{5,7},{6,4},{7,5},{8,10},{9,11},{10,... | collective-permute-start | bytes 282632 | tf_op jit(solution)/shard_map/ppermute | solution.py:953
  108.4 2.6 %input_back.6.refs_6_ = bf16[32,128,128]{2,1,0:T(8,128)(2,1)} custom-call(f32[32,128,128]{2,1,0:T(8,128)} %get-tuple-element.164.refs_0_, bf16[32,256,128]{2,1,0:T(8,128)(2,1)} %get-tuple-element.178.refs_1_, bf16[32,128,128]{2,1,0:T(8,128)(2,1)} %bitcast.38, bf16[32,128,128]{2,1,0:T(8,128)(2,1)} %get-tuple-element.179.refs_3_, ...), custom_call_target="tpu_custom_call", output_to_operand_aliasing={{}: (6, {})} | custom-call | flops 3000000000 | bytes 9000000 | tf_op jit(solution)/shard_map/input_back/pallas_call | solution.py:109
  111.2 2.9 %collective-permute-start.26 = (bf16[368,128]{1,0:T(8,128)(2,1)S(1)}, bf16[368,128]{1,0:T(8,128)(2,1)S(1)}, u32[]{:S(2)}, u32[]{:S(2)}) collective-permute-start(bf16[368,128]{1,0:T(8,128)(2,1)S(1)} %add.22), channel_id=1, source_target_pairs={{0,4},{1,5},{2,6},{3,7},{4,0},{5,1},{6,2},{7,3},{8,12},{9,13},{10,... | collective-permute-start | bytes 282632 | tf_op jit(solution)/shard_map/ppermute | solution.py:953
  114.1 2.7 %collective-permute-done.26 = bf16[368,128]{1,0:T(8,128)(2,1)S(1)} collective-permute-done((bf16[368,128]{1,0:T(8,128)(2,1)S(1)}, bf16[368,128]{1,0:T(8,128)(2,1)S(1)}, u32[]{:S(2)}, u32[]{:S(2)}) %collective-permute-start.26) | collective-permute-done | bytes 94240 | tf_op jit(solution)/shard_map/ppermute | solution.py:953
  118.5 2.6 %input_back.7 = bf16[32,128,128]{2,1,0:T(8,128)(2,1)} custom-call(f32[32,128,128]{2,1,0:T(8,128)} %get-tuple-element.164.refs_0_, bf16[32,256,128]{2,1,0:T(8,128)(2,1)} %get-tuple-element.178.refs_1_, bf16[32,128,128]{2,1,0:T(8,128)(2,1)} %bitcast.39, bf16[32,128,128]{2,1,0:T(8,128)(2,1)} %get-tuple-element.179.refs_3_, ...), custom_call_target="tpu_custom_call", output_to_operand_aliasing={{}: (6, {})} | custom-call | flops 3000000000 | bytes 9000000 | tf_op jit(solution)/shard_map/input_back/pallas_call | solution.py:109
  (116 shorter events, 22.1 us)
Async XLA Ops:
  4.0 13.3 %collective-permute-start.1 = (bf16[128,16,128]{2,1,0:T(8,128)(2,1)S(1)}, bf16[128,16,128]{2,1,0:T(8,128)(2,1)}, u32[]{:S(2)}, u32[]{:S(2)}) collective-permute-start(bf16[128,16,128]{2,1,0:T(8,128)(2,1)S(1)} %get-tuple-element.112.refs_0_), channel_id=1, source_target_pairs={{0,8},{8,0},{16,24},{24,16},{1,9},{9,1},{17,25},{25,17},{2,10},{10... | collective-permute-start | bytes 1572872 | tf_op jit(solution)/shard_map/ppermute | solution.py:953
  4.5 19.3 %collective-permute-start = (bf16[128,16,128]{2,1,0:T(8,128)(2,1)S(1)}, bf16[128,16,128]{2,1,0:T(8,128)(2,1)S(1)}, u32[]{:S(2)}, u32[]{:S(2)}) collective-permute-start(bf16[128,16,128]{2,1,0:T(8,128)(2,1)S(1)} %get-tuple-element.112.refs_0_), channel_id=1, source_target_pairs={{0,16},{8,24},{16,0},{24,8},{1,17},{9,25},{17,1},{25,9},{2,18},{10... | collective-permute-start | bytes 1572872 | tf_op jit(solution)/shard_map/ppermute | solution.py:953
  10.4 6.8 %collective-permute-start.2 = (bf16[128,16,128]{2,1,0:T(8,128)(2,1)S(1)}, bf16[128,16,128]{2,1,0:T(8,128)(2,1)}, u32[]{:S(2)}, u32[]{:S(2)}) collective-permute-start(bf16[128,16,128]{2,1,0:T(8,128)(2,1)S(1)} %get-tuple-element.114.refs_1_), channel_id=1, source_target_pairs={{0,8},{8,0},{16,24},{24,16},{1,9},{9,1},{17,25},{25,17},{2,10},{10... | collective-permute-start | bytes 1572872 | tf_op jit(solution)/shard_map/ppermute | solution.py:953
  10.7 20.1 %collective-permute-start.3 = (bf16[128,16,128]{2,1,0:T(8,128)(2,1)S(1)}, bf16[128,16,128]{2,1,0:T(8,128)(2,1)S(1)}, u32[]{:S(2)}, u32[]{:S(2)}) collective-permute-start(bf16[128,16,128]{2,1,0:T(8,128)(2,1)S(1)} %get-tuple-element.114.refs_1_), channel_id=1, source_target_pairs={{0,16},{8,24},{16,0},{24,8},{1,17},{9,25},{17,1},{25,9},{2,18},{10... | collective-permute-start | bytes 1572872 | tf_op jit(solution)/shard_map/ppermute | solution.py:953
  31.3 46.6 %collective-permute-start.19 = (bf16[88,32,128]{2,1,0:T(8,128)(2,1)S(1)}, bf16[88,32,128]{2,1,0:T(8,128)(2,1)S(1)}, u32[]{:S(2)}, u32[]{:S(2)}) collective-permute-start(bf16[88,32,128]{2,1,0:T(8,128)(2,1)S(1)} %get-tuple-element.145.refs_5_.refs_8_), channel_id=1, source_target_pairs={{0,8},{8,0},{16,24},{24,16},{1,9},{9,1},{17,25},{25,17},{2,10},{10... | collective-permute-start | bytes 2162696 | tf_op jit(solution)/shard_map/ppermute | solution.py:953
  31.5 11.1 %collective-permute-start.6 = (bf16[40,32,128]{2,1,0:T(8,128)(2,1)}, bf16[40,32,128]{2,1,0:T(8,128)(2,1)S(1)}, u32[]{:S(2)}, u32[]{:S(2)}) collective-permute-start(bf16[40,32,128]{2,1,0:T(8,128)(2,1)} %get-tuple-element.128.refs_4_), channel_id=1, source_target_pairs={{0,16},{8,24},{16,0},{24,8},{1,17},{9,25},{17,1},{25,9},{2,18},{10... | collective-permute-start | bytes 983048 | tf_op jit(solution)/shard_map/ppermute | solution.py:953
  40.5 6.8 %collective-permute-start.7 = (bf16[32,512]{1,0:T(8,128)(2,1)S(1)}, bf16[32,512]{1,0:T(8,128)(2,1)S(1)}, u32[]{:S(2)}, u32[]{:S(2)}) collective-permute-start(bf16[32,512]{1,0:T(8,128)(2,1)S(1)} %get-tuple-element.132.refs_0_), channel_id=1, source_target_pairs={{0,8},{8,0},{16,24},{24,16},{1,9},{9,1},{17,25},{25,17},{2,10},{10... | collective-permute-start | bytes 98312 | tf_op jit(solution)/shard_map/ppermute | solution.py:953
  40.9 6.4 %collective-permute-start.8 = (bf16[32,512]{1,0:T(8,128)(2,1)S(1)}, bf16[32,512]{1,0:T(8,128)(2,1)S(1)}, u32[]{:S(2)}, u32[]{:S(2)}) collective-permute-start(bf16[32,512]{1,0:T(8,128)(2,1)S(1)} %get-tuple-element.132.refs_0_), channel_id=1, source_target_pairs={{0,16},{8,24},{16,0},{24,8},{1,17},{9,25},{17,1},{25,9},{2,18},{10... | collective-permute-start | bytes 98312 | tf_op jit(solution)/shard_map/ppermute | solution.py:953
  42.7 4.6 %collective-permute-start.9 = (bf16[32,512]{1,0:T(8,128)(2,1)S(1)}, bf16[32,512]{1,0:T(8,128)(2,1)S(1)}, u32[]{:S(2)}, u32[]{:S(2)}) collective-permute-start(bf16[32,512]{1,0:T(8,128)(2,1)S(1)} %get-tuple-element.132.refs_0_), channel_id=1, source_target_pairs={{0,24},{8,16},{16,8},{24,0},{1,25},{9,17},{17,9},{25,1},{2,26},{10... | collective-permute-start | bytes 98312 | tf_op jit(solution)/shard_map/ppermute | solution.py:953
  47.3 19.4 %collective-permute-start.11 = (bf16[88,32,128]{2,1,0:T(8,128)(2,1)S(1)}, bf16[88,32,128]{2,1,0:T(8,128)(2,1)S(1)}, u32[]{:S(2)}, u32[]{:S(2)}) collective-permute-start(bf16[88,32,128]{2,1,0:T(8,128)(2,1)S(1)} %get-tuple-element.145.refs_5_.refs_8_), channel_id=1, source_target_pairs={{0,16},{8,24},{16,0},{24,8},{1,17},{9,25},{17,1},{25,9},{2,18},{10... | collective-permute-start | bytes 2162696 | tf_op jit(solution)/shard_map/ppermute | solution.py:953
  62.0 4.8 %collective-permute-start.12 = (bf16[32,512]{1,0:T(8,128)(2,1)S(1)}, bf16[32,512]{1,0:T(8,128)(2,1)S(1)}, u32[]{:S(2)}, u32[]{:S(2)}) collective-permute-start(bf16[32,512]{1,0:T(8,128)(2,1)S(1)} %get-tuple-element.147), channel_id=1, source_target_pairs={{0,16},{8,24},{16,0},{24,8},{1,17},{9,25},{17,1},{25,9},{2,18},{10... | collective-permute-start | bytes 98312 | tf_op jit(solution)/shard_map/ppermute | solution.py:953
  62.4 4.5 %collective-permute-start.13 = (bf16[32,512]{1,0:T(8,128)(2,1)S(1)}, bf16[32,512]{1,0:T(8,128)(2,1)S(1)}, u32[]{:S(2)}, u32[]{:S(2)}) collective-permute-start(bf16[32,512]{1,0:T(8,128)(2,1)S(1)} %get-tuple-element.148), channel_id=1, source_target_pairs={{0,24},{8,16},{16,8},{24,0},{1,25},{9,17},{17,9},{25,1},{2,26},{10... | collective-permute-start | bytes 98312 | tf_op jit(solution)/shard_map/ppermute | solution.py:953
  66.0 10.1 %collective-permute-start.17 = (bf16[40,32,128]{2,1,0:T(8,128)(2,1)S(1)}, bf16[40,32,128]{2,1,0:T(8,128)(2,1)S(1)}, u32[]{:S(2)}, u32[]{:S(2)}) collective-permute-start(bf16[40,32,128]{2,1,0:T(8,128)(2,1)S(1)} %copy-done.9), channel_id=1, source_target_pairs={{0,8},{8,0},{16,24},{24,16},{1,9},{9,1},{17,25},{25,17},{2,10},{10... | collective-permute-start | bytes 983048 | tf_op jit(solution)/shard_map/ppermute | solution.py:953
  75.4 14.6 %collective-permute-start.20 = (bf16[88,32,128]{2,1,0:T(8,128)(2,1)S(1)}, bf16[88,32,128]{2,1,0:T(8,128)(2,1)S(1)}, u32[]{:S(2)}, u32[]{:S(2)}) collective-permute-start(bf16[88,32,128]{2,1,0:T(8,128)(2,1)S(1)} %collective-permute-done.11.refs_10_), channel_id=1, source_target_pairs={{0,8},{8,0},{16,24},{24,16},{1,9},{9,1},{17,25},{25,17},{2,10},{10... | collective-permute-start | bytes 2162696 | tf_op jit(solution)/shard_map/ppermute | solution.py:953
  75.6 14.4 %collective-permute-start.18 = (bf16[40,32,128]{2,1,0:T(8,128)(2,1)S(1)}, bf16[40,32,128]{2,1,0:T(8,128)(2,1)S(1)}, u32[]{:S(2)}, u32[]{:S(2)}) collective-permute-start(bf16[40,32,128]{2,1,0:T(8,128)(2,1)S(1)} %collective-permute-done.6.refs_6_), channel_id=1, source_target_pairs={{0,8},{8,0},{16,24},{24,16},{1,9},{9,1},{17,25},{25,17},{2,10},{10... | collective-permute-start | bytes 983048 | tf_op jit(solution)/shard_map/ppermute | solution.py:953
  75.9 12.4 %collective-permute-start.14 = (bf16[32,32,128]{2,1,0:T(8,128)(2,1)}, bf16[32,32,128]{2,1,0:T(8,128)(2,1)S(1)}, u32[]{:S(2)}, u32[]{:S(2)}) collective-permute-start(bf16[32,32,128]{2,1,0:T(8,128)(2,1)} %get-tuple-element.166), channel_id=1, source_target_pairs={{0,8},{8,0},{16,24},{24,16},{1,9},{9,1},{17,25},{25,17},{2,10},{10... | collective-permute-start | bytes 786440 | tf_op jit(solution)/shard_map/ppermute | solution.py:953
  76.1 12.2 %collective-permute-start.15 = (bf16[32,32,128]{2,1,0:T(8,128)(2,1)}, bf16[32,32,128]{2,1,0:T(8,128)(2,1)S(1)}, u32[]{:S(2)}, u32[]{:S(2)}) collective-permute-start(bf16[32,32,128]{2,1,0:T(8,128)(2,1)} %get-tuple-element.167), channel_id=1, source_target_pairs={{0,16},{8,24},{16,0},{24,8},{1,17},{9,25},{17,1},{25,9},{2,18},{10... | collective-permute-start | bytes 786440 | tf_op jit(solution)/shard_map/ppermute | solution.py:953
  77.9 12.1 %collective-permute-start.16 = (bf16[32,32,128]{2,1,0:T(8,128)(2,1)}, bf16[32,32,128]{2,1,0:T(8,128)(2,1)S(1)}, u32[]{:S(2)}, u32[]{:S(2)}) collective-permute-start(bf16[32,32,128]{2,1,0:T(8,128)(2,1)} %get-tuple-element.168), channel_id=1, source_target_pairs={{0,24},{8,16},{16,8},{24,0},{1,25},{9,17},{17,9},{25,1},{2,26},{10... | collective-permute-start | bytes 786440 | tf_op jit(solution)/shard_map/ppermute | solution.py:953
  95.9 5.3 %collective-permute-start.21 = (bf16[368,128]{1,0:T(8,128)(2,1)S(1)}, bf16[368,128]{1,0:T(8,128)(2,1)S(1)}, u32[]{:S(2)}, u32[]{:S(2)}) collective-permute-start(bf16[368,128]{1,0:T(8,128)(2,1)S(1)} %get-tuple-element.181), channel_id=1, source_target_pairs={{0,8},{8,0},{16,24},{24,16},{1,9},{9,1},{17,25},{25,17},{2,10},{10... | collective-permute-start | bytes 282632 | tf_op jit(solution)/shard_map/ppermute | solution.py:953
  96.8 5.0 %collective-permute-start.23 = (bf16[368,128]{1,0:T(8,128)(2,1)S(1)}, bf16[368,128]{1,0:T(8,128)(2,1)S(1)}, u32[]{:S(2)}, u32[]{:S(2)}) collective-permute-start(bf16[368,128]{1,0:T(8,128)(2,1)S(1)} %add.19), channel_id=1, source_target_pairs={{0,16},{8,24},{16,0},{24,8},{1,17},{9,25},{17,1},{25,9},{2,18},{10... | collective-permute-start | bytes 282632 | tf_op jit(solution)/shard_map/ppermute | solution.py:953
  101.8 4.6 %collective-permute-start.24 = (bf16[368,128]{1,0:T(8,128)(2,1)S(1)}, bf16[368,128]{1,0:T(8,128)(2,1)S(1)}, u32[]{:S(2)}, u32[]{:S(2)}) collective-permute-start(bf16[368,128]{1,0:T(8,128)(2,1)S(1)} %add_add_fusion), channel_id=1, source_target_pairs={{0,1},{1,0},{2,3},{3,2},{4,5},{5,4},{6,7},{7,6},{8,9},{9,8},{10,11... | collective-permute-start | bytes 282632 | tf_op jit(solution)/shard_map/ppermute | solution.py:953
  106.5 4.6 %collective-permute-start.25 = (bf16[368,128]{1,0:T(8,128)(2,1)S(1)}, bf16[368,128]{1,0:T(8,128)(2,1)S(1)}, u32[]{:S(2)}, u32[]{:S(2)}) collective-permute-start(bf16[368,128]{1,0:T(8,128)(2,1)S(1)} %add.21), channel_id=1, source_target_pairs={{0,2},{1,3},{2,0},{3,1},{4,6},{5,7},{6,4},{7,5},{8,10},{9,11},{10,... | collective-permute-start | bytes 282632 | tf_op jit(solution)/shard_map/ppermute | solution.py:953
  111.2 5.5 %collective-permute-start.26 = (bf16[368,128]{1,0:T(8,128)(2,1)S(1)}, bf16[368,128]{1,0:T(8,128)(2,1)S(1)}, u32[]{:S(2)}, u32[]{:S(2)}) collective-permute-start(bf16[368,128]{1,0:T(8,128)(2,1)S(1)} %add.22), channel_id=1, source_target_pairs={{0,4},{1,5},{2,6},{3,7},{4,0},{5,1},{6,2},{7,3},{8,12},{9,13},{10,... | collective-permute-start | bytes 282632 | tf_op jit(solution)/shard_map/ppermute | solution.py:953
  116.7 4.6 %collective-permute-start.27 = (bf16[368,128]{1,0:T(8,128)(2,1)S(1)}, bf16[368,128]{1,0:T(8,128)(2,1)S(1)}, u32[]{:S(2)}, u32[]{:S(2)}) collective-permute-start(bf16[368,128]{1,0:T(8,128)(2,1)S(1)} %add.23.refs_0_), channel_id=1, source_target_pairs={{0,16},{8,24},{16,0},{24,8},{1,17},{9,25},{17,1},{25,9},{2,18},{10... | collective-permute-start | bytes 282632 | tf_op jit(solution)/shard_map/ppermute | solution.py:953
  (32 other events, 196.6 us)
